TPU v7x, 256 devices: a whole 4x4x8 slice. The times are simulated.
256 devices in a mesh: band: 32 (over z, x_hi, core), head: 8 (over y, x_lo).
Axes of the slice: x: 4 (x_hi: 2, x_lo: 2; x = x_hi * 2 + x_lo), y: 4, z: 8, core: 2. Of those that a mesh axis runs over, the one named last changes fastest.
Arguments:
- grid_in: bfloat16 [110, 524288], P(None, ('band', 'head')), may hold values from -6 to 6
- enc_node: int32 [524288], P(('band', 'head')), may hold values from 0 to 40959, as said below
- dec_node: int32 [524288], P(('band', 'head')), may hold values from 0 to 40959, as said below
- win_offsets: int32 [2, 40960], P(None, 'band'), may hold values from 1 to 640, as said below
- w_in: bfloat16 [110, 1024], replicated, may hold values from -0.5 to 0.5
- b_in: float32 [1024], replicated, may hold values from -4 to 4
- w_qkv: bfloat16 [1024, 3072], replicated, may hold values from -8 to 8
- w_out: bfloat16 [1024, 1024], replicated, may hold values from -0.75 to 0.75
- norm_gain: float32 [1024], replicated, may hold values from 0.1 to 1.9
- w_dec: bfloat16 [1024, 110], replicated, may hold values from -0.1875 to 0.1875
- cotangent: bfloat16 [110, 524288], P(None, ('band', 'head')), may hold values from -6 to 6
Outputs:
- prediction: bfloat16 [110, 524288], P(None, ('band', 'head'))
- grad_dec: float32 [1024, 110], replicated
Inputs may be any that keep to these rules, and one draw needn't show every extreme that they name: `enc_node`: grid points and nodes are numbered by latitude; the node of the encoder edge of a grid point held by index j of band+head is held by index j - 1, j or j + 1 of band+head. `dec_node`: the node of the decoder edge of a grid point held by index j of band+head is held by index j - 1, j or j + 1 of band+head. `win_offsets`: row 0 is the reach towards lower node numbers, row 1 towards higher ones.
All inputs are finite; a program needn't handle non-finite values.
Results may differ from a plain program's by a relative error of at most 0.012.
Values may be sent and summed in bfloat16 or wider, within the bound.
No kernel may reach another device: no remote copies, remote signals or barrier semaphores. Data moves between devices by JAX's collectives and lax.ppermute only.
A program may use at most 128 MiB of HBM per device.

v0:
```python
import jax
import jax.numpy as jnp
from jax import lax
from jax.sharding import PartitionSpec as P

HDIM = 64
NODE_DEV = 160


def extended(block, sides, width):
    for axis, dim in sides:
        count = lax.axis_size(axis)
        forward = [(i, i + 1) for i in range(count - 1)]
        backward = [(target, source) for source, target in forward]
        low = lax.ppermute(
            lax.slice_in_dim(block, block.shape[dim] - width, None, axis=dim), axis, forward
        )
        high = lax.ppermute(lax.slice_in_dim(block, 0, width, axis=dim), axis, backward)
        block = jnp.concatenate([low, block, high], axis=dim)
    return block


def select_sum(local_index, row_count, message):
    model_width = message.shape[1]
    high_part = message.astype(jnp.bfloat16)
    low_part = (message - high_part.astype(jnp.float32)).astype(jnp.bfloat16)
    split_parts = jnp.concatenate([high_part, low_part], axis=1)
    selector = (local_index[None, :] == jnp.arange(row_count, dtype=jnp.int32)[:, None]).astype(
        jnp.bfloat16
    )
    summed = jnp.dot(selector, split_parts, preferred_element_type=jnp.float32)
    return summed[:, :model_width] + summed[:, model_width:]


def shards(
    grid_in, enc_node, dec_node, win_offsets, w_in, b_in, w_qkv, w_out, norm_gain, w_dec, cotangent
):
    model_width = w_in.shape[1]
    per_device = NODE_DEV
    device_index = lax.axis_index(("band", "head"))
    base_node = (device_index - 1) * per_device
    preact = (
        lax.dot_general(grid_in, w_in, (((0,), (0,)), ((), ())), preferred_element_type=jnp.float32)
        + b_in
    )
    local_index = enc_node - base_node
    spread = select_sum(local_index, 3 * per_device, jax.nn.silu(preact))
    outer_rows = jnp.concatenate([spread[:per_device], spread[2 * per_device :]], axis=0)
    padded = extended(outer_rows, ((("band", "head"), 0),), per_device)
    encoded = spread[per_device : 2 * per_device] + padded[:per_device] + padded[3 * per_device :]
    centred = encoded - jnp.mean(encoded, axis=1, keepdims=True)
    spread_sq = jnp.mean(centred * centred, axis=1, keepdims=True)
    normed = (centred * lax.rsqrt(spread_sq + 1e-05) * norm_gain).astype(jnp.bfloat16)
    packed = jnp.dot(normed, w_qkv, preferred_element_type=jnp.float32).astype(jnp.bfloat16)
    head_rows = lax.all_to_all(
        packed.reshape(per_device, 3, model_width), "head", split_axis=2, concat_axis=0, tiled=True
    )
    band_rows = head_rows.shape[0]
    local_width = head_rows.shape[2]
    head_count = local_width // HDIM
    reach_rows = band_rows // 2
    stacked = extended(head_rows[:, 1:], (("band", 0),), reach_rows)
    key_count = band_rows + 2 * reach_rows
    queries = head_rows[:, 0].reshape(band_rows, head_count, HDIM)
    key_block = stacked[:, 0].reshape(key_count, head_count, HDIM)
    values = stacked[:, 1].reshape(key_count, head_count, HDIM)
    band_index = lax.axis_index("band")
    first_node = band_index * band_rows
    node_total = lax.axis_size("band") * band_rows
    offset_grid = (
        jnp.arange(key_count, dtype=jnp.int32)[None, :]
        - reach_rows
        - jnp.arange(band_rows, dtype=jnp.int32)[:, None]
    )
    global_key = first_node - reach_rows + jnp.arange(key_count, dtype=jnp.int32)
    allowed = (offset_grid >= -win_offsets[0][:, None]) & (offset_grid <= win_offsets[1][:, None])
    allowed = allowed & (global_key >= 0)[None, :] & (global_key < node_total)[None, :]
    scores = jnp.einsum(
        "qhd,khd->hqk", queries, key_block, preferred_element_type=jnp.float32
    ) * HDIM ** (-0.5)
    scores = jnp.where(allowed[None], scores, -jnp.inf)
    largest = jnp.max(scores, axis=2, keepdims=True)
    weights = jnp.exp(scores - largest)
    weights = (weights / jnp.sum(weights, axis=2, keepdims=True)).astype(jnp.bfloat16)
    attended = jnp.einsum("hqk,khd->qhd", weights, values, preferred_element_type=jnp.float32)
    attended = attended.reshape(band_rows, local_width).astype(jnp.bfloat16)
    node_mixed = lax.all_to_all(attended, "head", split_axis=0, concat_axis=1, tiled=True)
    state = (encoded + jnp.dot(node_mixed, w_out, preferred_element_type=jnp.float32)).astype(
        jnp.bfloat16
    )
    beside_all = extended(state, ((("band", "head"), 0),), per_device)
    node_rows = beside_all[dec_node - base_node]
    decoded = lax.dot_general(
        w_dec, node_rows, (((0,), (1,)), ((), ())), preferred_element_type=jnp.float32
    )
    prediction = (grid_in.astype(jnp.float32) + decoded).astype(jnp.bfloat16)
    grad_term = lax.dot_general(
        node_rows, cotangent, (((0,), (1,)), ((), ())), preferred_element_type=jnp.float32
    )
    grad_dec = lax.psum(grad_term, ("band", "head"))
    return (prediction, grad_dec)


def solution(mesh):
    placed = (
        P(None, ("band", "head")),
        P(("band", "head")),
        P(("band", "head")),
        P(None, "band"),
        P(),
        P(),
        P(),
        P(),
        P(),
        P(),
        P(None, ("band", "head")),
    )
    return jax.shard_map(
        shards,
        mesh=mesh,
        in_specs=placed,
        out_specs=(P(None, ("band", "head")), P()),
        check_vma=False,
    )
```

profile of v0, /device:TPU:32, one launch (start us, length us, event | category | flops | bytes accessed | tf_op | source)
XLA Modules:
  0.0 454.2 jit_solution(3013782198563968816)
XLA Ops:
  8.0 3.7 subtract_convert_fusion
  11.8 4.3 fusion.11
  16.7 6.4 %collective-permute-start.1 = (f32[160,1024]{1,0:T(8,128)S(1)}, f32[160,1024]{1,0:T(8,128)S(1)}, u32[]{:S(2)}, u32[]{:S(2)}) collective-permute-start(f32[160,1024]{1,0:T(8,128)S(1)} %get-tuple-element.9), channel_id=1, source_target_pairs={{1,0},{2,1},{3,2},{4,3},{5,4},{6,5},{7,6},{8,7},{9,8},{10,9},{11,1... | collective-permute-start | bytes 1966088 | tf_op jit(solution)/shard_map/ppermute | solution.py:18
  23.1 1.9 collective-permute-start
  25.0 11.5 %collective-permute-done.1 = f32[160,1024]{1,0:T(8,128)S(1)} collective-permute-done((f32[160,1024]{1,0:T(8,128)S(1)}, f32[160,1024]{1,0:T(8,128)S(1)}, u32[]{:S(2)}, u32[]{:S(2)}) %collective-permute-start.1) | collective-permute-done | bytes 655392 | tf_op jit(solution)/shard_map/ppermute | solution.py:18
  36.5 3.9 collective-permute-done
  40.8 2.2 convolution_convert_fusion
  43.1 4.0 reshape.129
  47.1 5.5 %copy.28 = bf16[160,3,1024]{0,1,2:T(4,128)(2,1)} copy(bf16[160,3,1024]{2,1,0:T(4,128)(2,1)} %reshape.129) | data formatting | bytes 1966080 | tf_op jit(solution)/shard_map/reshape | solution.py:56
  52.6 4.8 %reshape.141 = bf16[8,2,30720]{2,1,0:T(2,128)(2,1)} reshape(bf16[1024,3,160]{2,1,0:T(4,128)(2,1)} %bitcast.40) | data formatting | bytes 1966080
  57.4 14.4 %all-to-all-start = ((bf16[8,2,30720]{2,1,0:T(2,128)(2,1)}), bf16[8,2,30720]{2,1,0:T(2,128)(2,1)}, u32[]{:S(2)}, u32[]{:S(2)}) async-start(bf16[8,2,30720]{2,1,0:T(2,128)(2,1)} %reshape.141), calls=%async_computation | async-start | bytes 1966080 | tf_op jit(solution)/shard_map/all_to_all | solution.py:55
  71.9 14.1 %all-to-all-done = bf16[8,2,30720]{2,1,0:T(2,128)(2,1)} async-done(((bf16[8,2,30720]{2,1,0:T(2,128)(2,1)}), bf16[8,2,30720]{2,1,0:T(2,128)(2,1)}, u32[]{:S(2)}, u32[]{:S(2)}) %all-to-all-start) | async-done | bytes 983072 | tf_op jit(solution)/shard_map/all_to_all | solution.py:55
  86.1 4.8 %reshape.142 = bf16[1024,3,160]{2,1,0:T(4,128)(2,1)} reshape(bf16[8,2,30720]{2,1,0:T(2,128)(2,1)} %all-to-all-done) | data formatting | bytes 1966080
  90.8 4.0 copy.37
  94.8 2.0 fusion.39
  96.9 1.9 collective-permute-start.3
  98.8 2.6 collective-permute-start.2
  101.4 11.9 %fusion.8 = pred[1280,2560]{1,0:T(8,128)(4,1)} fusion(s32[1280]{0:T(1024)S(1)} %get-tuple-element.3, s32[1280]{0:T(1024)S(1)} %get-tuple-element.2, s32[2560]{0:T(1024)S(1)} %iota_add_fusion.1, pred[2560]{0:T(1024)(128)(4,1)S(1)} %get-tuple-element.16, pred[2560]{0:T(1024)(128)(4,1)S(1)} %get-tuple-element.17), kind=kLoop, calls=%fused_computation.13 | loop fusion | flops 19660800 | bytes 3302400 | tf_op jit(solution)/shard_map/and | solution.py:77
  114.1 1.9 copy.32
  118.1 2.2 copy.31
  121.4 15.2 %fusion.40 = (f32[2,1280]{1,0:T(2,128)S(1)}, f32[2,1280,2560]{2,1,0:T(8,128)}) fusion(pred[1280,2560]{1,0:T(8,128)(4,1)} %fusion.8, bf16[1280,2,64]{0,2,1:T(8,128)(2,1)} %bitcast.46, bf16[2560,2,64]{0,2,1:T(8,128)(2,1)} %bitcast.45), kind=kOutput, calls=%fused_computation.63 | convolution fusion | flops 865077760 | bytes 30484480 | tf_op jit(solution)/shard_map/sub | solution.py:83
  136.7 11.4 %fusion.20 = bf16[1280,2,64]{0,2,1:T(8,128)(2,1)} fusion(bf16[2560,2,64]{0,2,1:T(8,128)(2,1)S(1)} %bitcast.44, f32[2,1280,2560]{2,1,0:T(8,128)} %get-tuple-element.15, f32[2,1280]{1,0:T(2,128)S(1)} %get-tuple-element.14), kind=kOutput, calls=%fused_computation.29 | convolution fusion | flops 852131840 | bytes 27207680 | tf_op jit(solution)/shard_map/hqk,khd->qhd/dot_general | solution.py:85
  150.8 11.4 %all_to_all.34 = bf16[8,160,128]{2,1,0:T(8,128)(2,1)S(1)} all-to-all(bf16[8,160,128]{2,1,0:T(8,128)(2,1)} %copy.34), channel_id=1, replica_groups=mesh['band'=32,'head'=8] {'head'}, dimensions={0} | all-to-all | bytes 655360 | tf_op jit(solution)/shard_map/all_to_all | solution.py:87
  162.7 4.9 %collective-permute-start.5 = (bf16[160,1024]{1,0:T(8,128)(2,1)S(1)}, bf16[160,1024]{1,0:T(8,128)(2,1)S(1)}, u32[]{:S(2)}, u32[]{:S(2)}) collective-permute-start(bf16[160,1024]{1,0:T(8,128)(2,1)S(1)} %fusion.22), channel_id=1, source_target_pairs={{1,0},{2,1},{3,2},{4,3},{5,4},{6,5},{7,6},{8,7},{9,8},{10,9},{11,1... | collective-permute-start | bytes 983048 | tf_op jit(solution)/shard_map/ppermute | solution.py:18
  167.7 1.9 collective-permute-start.4
  169.6 5.3 %collective-permute-done.5 = bf16[160,1024]{1,0:T(8,128)(2,1)S(1)} collective-permute-done((bf16[160,1024]{1,0:T(8,128)(2,1)S(1)}, bf16[160,1024]{1,0:T(8,128)(2,1)S(1)}, u32[]{:S(2)}, u32[]{:S(2)}) %collective-permute-start.5) | collective-permute-done | bytes 327712 | tf_op jit(solution)/shard_map/ppermute | solution.py:18
  174.9 7.8 %collective-permute-done.4 = bf16[160,1024]{1,0:T(8,128)(2,1)S(1)} collective-permute-done((bf16[160,1024]{1,0:T(8,128)(2,1)S(1)}, bf16[160,1024]{1,0:T(8,128)(2,1)S(1)}, u32[]{:S(2)}, u32[]{:S(2)}) %collective-permute-start.4) | collective-permute-done | bytes 327712 | tf_op jit(solution)/shard_map/ppermute | solution.py:15
  182.8 9.6 %gather_fusion = bf16[2048,1024]{1,0:T(8,128)(2,1)} fusion(bf16[480,1024]{1,0:T(8,128)(2,1)S(1)} %pad_maximum_fusion.1, s32[2048]{0:T(1024)S(1)} %fusion.31), kind=kCustom, calls=%fused_computation | custom fusion | bytes 8396800 | tf_op jit(solution)/shard_map/gather | solution.py:92
  192.4 3.7 fusion.41
  196.2 4.4 fusion.19
  200.6 244.9 %all-reduce.2.cloned.1.call-done = f32[1024,110]{0,1:T(8,128)} async-done(((f32[1024,110]{0,1:T(8,128)}), f32[1024,110]{0,1:T(8,128)}) %all-reduce.2.cloned.1.call-update) | async-done | bytes 450576 | tf_op jit(solution)/shard_map/psum | solution.py:100
  445.5 1.8 copy.44
  (44 shorter events, 9.3 us)
Async XLA Ops:
  7.2 155.1 %copy-start = (bf16[1024,1024]{1,0:T(8,128)(2,1)S(1)}, bf16[1024,1024]{1,0:T(8,128)(2,1)}, u32[]{:S(2)}) copy-start(bf16[1024,1024]{1,0:T(8,128)(2,1)} %param.18) | copy-start | bytes 6291460
  16.0 24.8 %copy-start.2 = (bf16[1024,3072]{1,0:T(8,128)(2,1)S(1)}, bf16[1024,3072]{1,0:T(8,128)(2,1)}, u32[]{:S(2)}) copy-start(bf16[1024,3072]{1,0:T(8,128)(2,1)} %param.17) | copy-start | bytes 18874372
  16.6 24.3 %copy-start.9 = (f32[1024]{0:T(1024)S(1)}, f32[1024]{0:T(1024)}, u32[]{:S(2)}) copy-start(f32[1024]{0:T(1024)} %param.19) | copy-start | bytes 12292
  16.7 19.8 %collective-permute-start.1 = (f32[160,1024]{1,0:T(8,128)S(1)}, f32[160,1024]{1,0:T(8,128)S(1)}, u32[]{:S(2)}, u32[]{:S(2)}) collective-permute-start(f32[160,1024]{1,0:T(8,128)S(1)} %get-tuple-element.9), channel_id=1, source_target_pairs={{1,0},{2,1},{3,2},{4,3},{5,4},{6,5},{7,6},{8,7},{9,8},{10,9},{11,1... | collective-permute-start | bytes 1966088 | tf_op jit(solution)/shard_map/ppermute | solution.py:18
  23.1 17.3 %collective-permute-start = (f32[160,1024]{1,0:T(8,128)S(1)}, f32[160,1024]{1,0:T(8,128)S(1)}, u32[]{:S(2)}, u32[]{:S(2)}) collective-permute-start(f32[160,1024]{1,0:T(8,128)S(1)} %get-tuple-element.8), channel_id=1, source_target_pairs={{0,1},{1,2},{2,3},{3,4},{4,5},{5,6},{6,7},{7,8},{8,9},{9,10},{10,1... | collective-permute-start | bytes 1966088 | tf_op jit(solution)/shard_map/ppermute | solution.py:15
  47.0 24.8 %copy-start.7 = (s32[2,1280]{1,0:T(2,128)S(1)}, s32[2,1280]{1,0:T(2,128)}, u32[]{:S(2)}) copy-start(s32[2,1280]{1,0:T(2,128)} %param.14) | copy-start | bytes 30724
  57.4 28.6 %all-to-all-start = ((bf16[8,2,30720]{2,1,0:T(2,128)(2,1)}), bf16[8,2,30720]{2,1,0:T(2,128)(2,1)}, u32[]{:S(2)}, u32[]{:S(2)}) async-start(bf16[8,2,30720]{2,1,0:T(2,128)(2,1)} %reshape.141), calls=%async_computation | async-start | bytes 1966080 | tf_op jit(solution)/shard_map/all_to_all | solution.py:55
  71.8 373.8 %all-reduce.2.cloned.1.call-start = ((), (), s32[]{:S(2)}) async-start(), calls=%async_computation.2 | async-start | bytes 917504 | tf_op jit(solution)/shard_map/psum | solution.py:100
  94.8 18.5 %copy-start.1 = (bf16[160,3,8,128]{3,0,2,1:T(8,128)(2,1)S(1)}, bf16[160,3,8,128]{3,0,2,1:T(8,128)(2,1)}, u32[]{:S(2)}) copy-start(bf16[160,3,8,128]{3,0,2,1:T(8,128)(2,1)} %copy.37) | copy-start | bytes 2949124
  96.9 19.1 %collective-permute-start.3 = (bf16[640,2,128]{2,0,1:T(8,128)(2,1)}, bf16[640,2,128]{2,0,1:T(8,128)(2,1)}, u32[]{:S(2)}, u32[]{:S(2)}) collective-permute-start(bf16[640,2,128]{2,0,1:T(8,128)(2,1)} %get-tuple-element.13), channel_id=1, source_target_pairs={{8,0},{16,8},{24,16},{32,24},{40,32},{48,40},{56,48},{64,56},{72,6... | collective-permute-start | bytes 983048 | tf_op jit(solution)/shard_map/ppermute | solution.py:18
  98.8 17.2 %collective-permute-start.2 = (bf16[640,2,128]{2,0,1:T(8,128)(2,1)}, bf16[640,2,128]{2,0,1:T(8,128)(2,1)}, u32[]{:S(2)}, u32[]{:S(2)}) collective-permute-start(bf16[640,2,128]{2,0,1:T(8,128)(2,1)} %get-tuple-element.12), channel_id=1, source_target_pairs={{0,8},{8,16},{16,24},{24,32},{32,40},{40,48},{48,56},{56,64},{64,7... | collective-permute-start | bytes 983048 | tf_op jit(solution)/shard_map/ppermute | solution.py:15
  121.4 15.3 %copy-start.4 = (bf16[2560,1,128]{0,2,1:T(8,128)(2,1)S(1)}, bf16[2560,1,128]{0,2,1:T(8,128)(2,1)}, u32[]{:S(2)}) copy-start(bf16[2560,1,128]{0,2,1:T(8,128)(2,1)} %copy.31) | copy-start | bytes 1966084
  148.1 21.5 %copy-start.8 = (s32[2048]{0:T(1024)S(1)}, s32[2048]{0:T(1024)}, u32[]{:S(2)}) copy-start(s32[2048]{0:T(1024)} %param.13) | copy-start | bytes 24580
  162.7 12.2 %collective-permute-start.5 = (bf16[160,1024]{1,0:T(8,128)(2,1)S(1)}, bf16[160,1024]{1,0:T(8,128)(2,1)S(1)}, u32[]{:S(2)}, u32[]{:S(2)}) collective-permute-start(bf16[160,1024]{1,0:T(8,128)(2,1)S(1)} %fusion.22), channel_id=1, source_target_pairs={{1,0},{2,1},{3,2},{4,3},{5,4},{6,5},{7,6},{8,7},{9,8},{10,9},{11,1... | collective-permute-start | bytes 983048 | tf_op jit(solution)/shard_map/ppermute | solution.py:18
  167.7 15.0 %collective-permute-start.4 = (bf16[160,1024]{1,0:T(8,128)(2,1)S(1)}, bf16[160,1024]{1,0:T(8,128)(2,1)S(1)}, u32[]{:S(2)}, u32[]{:S(2)}) collective-permute-start(bf16[160,1024]{1,0:T(8,128)(2,1)S(1)} %fusion.22), channel_id=1, source_target_pairs={{0,1},{1,2},{2,3},{3,4},{4,5},{5,6},{6,7},{7,8},{8,9},{9,10},{10,1... | collective-permute-start | bytes 983048 | tf_op jit(solution)/shard_map/ppermute | solution.py:15
  182.8 9.6 %copy-start.5 = (bf16[110,2048]{1,0:T(8,128)(2,1)S(1)}, bf16[110,2048]{1,0:T(8,128)(2,1)}, u32[]{:S(2)}) copy-start(bf16[110,2048]{1,0:T(8,128)(2,1)} %param.21) | copy-start | bytes 1351684
  192.4 3.8 copy-start.3
  192.4 3.8 copy-start.6
Sparse Core Ops, SparseCore 0:
  196.3 249.2 all-reduce.1
where the time goes:
time: 458 us; the launch traced here: 454 us
  waiting for transfers between devices  288 us (63%)
  local copies, waits for them, and re-layouts  46.4 us (10%)
  matrix products  45.6 us (10%)
  starting transfers between devices  34 us (7%)
  other arithmetic  15 us (3%)
  between operations  14.3 us (3%)
  blocking collectives  11.4 us (2%)
    psum x1, waiting for transfers between devices, shards(): grad_dec = lax.psum(grad_term, ('band', 'head'))  245 us
    ppermute x3, waiting for transfers between devices, extended(): lax.ppermute(lax.slice_in_dim(block, 0, width, axis=dim), axis, backward)  16.8 us
    sub x1, matrix products, shards(): weights = jnp.exp(scores - largest)  15.2 us
    all_to_all x1, starting transfers between devices, shards(): lax.all_to_all(packed.reshape(per_device, 3, model_width), 'head', split_...  14.4 us
    all_to_all x1, waiting for transfers between devices, shards(): lax.all_to_all(packed.reshape(per_device, 3, model_width), 'head', split_...  14.1 us
    ppermute x3, starting transfers between devices, extended(): lax.ppermute(lax.slice_in_dim(block, 0, width, axis=dim), axis, backward)  13.2 us
    and x1, other arithmetic, shards(): allowed & (global_key >= 0)[None, :] & (global_key < node_total)[None, :]  11.9 us
    ppermute x3, waiting for transfers between devices, extended(): lax.ppermute(lax.slice_in_dim(block, block.shape[dim] - width, None, axis...  11.7 us
  transfers between devices with their start and end apart: 8, of which 6 were waited for; matrix products, arithmetic and copies ran while one was open for 4% of the time, Pallas kernels for 0%

commit v1 on v0

v1 whole, which is shorter than its diff:
```python
import functools

import jax
import jax.numpy as jnp
from jax import lax
from jax.experimental import pallas as pl
from jax.experimental.pallas import tpu as pltpu
from jax.sharding import PartitionSpec as P

HDIM = 64
NODE_DEV = 160
BOTH = ("band", "head")
LANES = 128
BF = jnp.bfloat16
F32 = jnp.float32
LOG2E = 1.4426950408889634
NEG = -1e30


def params(mib=40):
    return pltpu.CompilerParams(vmem_limit_bytes=mib * 1024 * 1024)


def dot(a, b, ca, cb):
    return lax.dot_general(a, b, (((ca,), (cb,)), ((), ())), preferred_element_type=F32)


def my_index():
    return lax.axis_index("band") * lax.axis_size("head") + lax.axis_index("head")


def encode_kernel(grid_ref, enc_ref, w_ref, b_ref, cot_ref, dec_ref, own_ref, low_ref, high_ref,
                  rows_ref, w_pad, cot_pad, pick_ref):
    channels, points = grid_ref.shape
    model = w_ref.shape[1]
    nodes = NODE_DEV
    base = (my_index() - 1) * nodes
    padded = jnp.concatenate(
        [grid_ref[...].astype(F32), jnp.zeros((LANES - channels, points), F32)], axis=0
    )
    rows_ref[...] = padded.T.astype(BF)
    w_pad[...] = jnp.zeros_like(w_pad)
    w_pad[:channels, :] = (w_ref[...].astype(F32) * 0.5).astype(BF)
    node_id = lax.broadcasted_iota(jnp.int32, (3 * nodes, points), 0)
    pick_ref[...] = jnp.where(node_id == enc_ref[...] - base, 1.0, 0.0).astype(BF)
    width = 256
    for at in range(0, model, width):
        half = dot(rows_ref[...], w_pad[:, at : at + width], 1, 0) + b_ref[:, at : at + width] * 0.5
        message = (half + half * jnp.tanh(half)).astype(BF)
        spread = dot(pick_ref[...], message, 1, 0)
        low_ref[:, at : at + width] = spread[:nodes].astype(BF)
        own_ref[:, at : at + width] = spread[nodes : 2 * nodes]
        high_ref[:, at : at + width] = spread[2 * nodes :].astype(BF)
    cot_pad[...] = jnp.zeros_like(cot_pad)
    cot_pad[:channels, :] = cot_ref[...]
    pick_ref[...] = jnp.where(node_id == dec_ref[...] - base, 1.0, 0.0).astype(BF)
    spread = dot(pick_ref[...], cot_pad[...], 1, 1)
    low_ref[:, model:] = spread[:nodes].astype(BF)
    own_ref[:, model:] = spread[nodes : 2 * nodes]
    high_ref[:, model:] = spread[2 * nodes :].astype(BF)


def encode(grid_in, enc_row, w_in, b_row, cotangent, dec_row):
    channels, points = grid_in.shape
    model = w_in.shape[1]
    wide = model + LANES
    return pl.pallas_call(
        encode_kernel,
        out_shape=(
            jax.ShapeDtypeStruct((NODE_DEV, wide), F32),
            jax.ShapeDtypeStruct((NODE_DEV, wide), BF),
            jax.ShapeDtypeStruct((NODE_DEV, wide), BF),
        ),
        scratch_shapes=[
            pltpu.VMEM((points, LANES), BF),
            pltpu.VMEM((LANES, model), BF),
            pltpu.VMEM((LANES, points), BF),
            pltpu.VMEM((3 * NODE_DEV, points), BF),
        ],
        compiler_params=params(),
        name="encode",
    )(grid_in, enc_row, w_in, b_row, cotangent, dec_row)


def project_kernel(own_ref, from_low, from_high, gain_ref, wq_ref, wk_ref, wv_ref,
                   packed_ref, enc_ref, s_ref, normed_ref):
    model = gain_ref.shape[1]

    @pl.when(pl.program_id(0) == 0)
    def _():
        total = own_ref[...] + from_low[...].astype(F32) + from_high[...].astype(F32)
        enc = total[:, :model]
        s_ref[...] = total[:, model:].astype(BF)
        enc_ref[...] = enc.astype(BF)
        centred = enc - jnp.mean(enc, axis=1, keepdims=True)
        spread_sq = jnp.mean(centred * centred, axis=1, keepdims=True)
        normed_ref[...] = (centred * lax.rsqrt(spread_sq + 1e-05) * gain_ref[...]).astype(BF)

    normed = normed_ref[...]
    scale = HDIM ** (-0.5) * LOG2E
    packed_ref[0, :, :LANES] = (dot(normed, wq_ref[...], 1, 0) * scale).astype(BF)
    packed_ref[0, :, LANES : 2 * LANES] = dot(normed, wk_ref[...], 1, 0).astype(BF)
    packed_ref[0, :, 2 * LANES :] = dot(normed, wv_ref[...], 1, 0).astype(BF)


def project(own, from_low, from_high, gain_row, w_qkv):
    model = w_qkv.shape[0]
    groups = model // LANES
    whole = lambda shape: pl.BlockSpec(shape, lambda h: (0, 0))
    return pl.pallas_call(
        project_kernel,
        grid=(groups,),
        in_specs=[
            whole(own.shape),
            whole(own.shape),
            whole(own.shape),
            whole(gain_row.shape),
            pl.BlockSpec((model, LANES), lambda h: (0, h)),
            pl.BlockSpec((model, LANES), lambda h: (0, h + groups)),
            pl.BlockSpec((model, LANES), lambda h: (0, h + 2 * groups)),
        ],
        out_specs=(
            pl.BlockSpec((1, NODE_DEV, 3 * LANES), lambda h: (h, 0, 0)),
            whole((NODE_DEV, model)),
            whole((NODE_DEV, LANES)),
        ),
        out_shape=(
            jax.ShapeDtypeStruct((groups, NODE_DEV, 3 * LANES), BF),
            jax.ShapeDtypeStruct((NODE_DEV, model), BF),
            jax.ShapeDtypeStruct((NODE_DEV, LANES), BF),
        ),
        scratch_shapes=[pltpu.VMEM((NODE_DEV, model), BF)],
        compiler_params=params(),
        name="project",
    )(own, from_low, from_high, gain_row, w_qkv, w_qkv, w_qkv)


def side_kernel(head_ref, enc_ref, s_ref, w_dec_ref, w_out_ref, send_ref, node_ref, mix_ref, dec_pad):
    channels = w_dec_ref.shape[1]
    groups = send_ref.shape[0]
    dec_pad[...] = jnp.zeros_like(dec_pad)
    dec_pad[:, :channels] = w_dec_ref[...]
    enc = enc_ref[...]
    summed = s_ref[...]
    node_ref[...] = dot(enc, dec_pad[...], 1, 0)
    mix_ref[...] = dot(w_out_ref[...], dec_pad[...], 1, 0).astype(BF)
    grad = dot(summed, enc, 0, 0).T.astype(BF)
    for group in range(groups):
        send_ref[group, :NODE_DEV, :] = summed
        send_ref[group, NODE_DEV:, :] = grad[group * LANES : (group + 1) * LANES]


def side(enc, summed, w_dec, w_out):
    model = enc.shape[1]
    groups = model // LANES
    head = lax.axis_index("head").astype(jnp.int32)[None]
    whole = lambda shape: pl.BlockSpec(shape, lambda i, h: (0,) * len(shape))
    send_shape = (groups, NODE_DEV + LANES, LANES)
    return pl.pallas_call(
        side_kernel,
        grid_spec=pltpu.PrefetchScalarGridSpec(
            num_scalar_prefetch=1,
            grid=(1,),
            in_specs=[
                whole(enc.shape),
                whole(summed.shape),
                whole(w_dec.shape),
                pl.BlockSpec((LANES, model), lambda i, h: (h[0], 0)),
            ],
            out_specs=(whole(send_shape), whole((NODE_DEV, LANES)), whole((LANES, LANES))),
            scratch_shapes=[pltpu.VMEM((model, LANES), BF)],
        ),
        out_shape=(
            jax.ShapeDtypeStruct(send_shape, BF),
            jax.ShapeDtypeStruct((NODE_DEV, LANES), F32),
            jax.ShapeDtypeStruct((LANES, LANES), BF),
        ),
        compiler_params=params(),
        name="side",
    )(head, enc, summed, w_dec, w_out)


QB = 256
KC = 128


def attend_kernel(reach, qkv_ref, low_ref, high_ref, win_ref, extra_ref, mix_ref,
                  node_ref, grad_ref, k_ref, vt_ref, score_ref, prob_ref, out_ref):
    groups = extra_ref.shape[0]
    band_rows = qkv_ref.shape[0]
    first_node = lax.axis_index("band") * band_rows
    node_total = lax.axis_size("band") * band_rows
    keys = QB + 2 * reach
    chunks = keys // KC
    k_ref[:reach, :] = low_ref[:, :LANES]
    k_ref[reach : reach + band_rows, :] = qkv_ref[:, LANES : 2 * LANES]
    k_ref[reach + band_rows :, :] = high_ref[:, :LANES]
    ones = jnp.ones((16, band_rows + 2 * reach), BF)
    vt = jnp.concatenate(
        [low_ref[:, LANES:].astype(F32), qkv_ref[:, 2 * LANES :].astype(F32), high_ref[:, LANES:].astype(F32)],
        axis=0,
    ).T.astype(BF)
    for head in range(2):
        vt_ref[head, :HDIM, :] = vt[head * HDIM : (head + 1) * HDIM]
        vt_ref[head, HDIM:, :] = ones
    lane = lax.broadcasted_iota(jnp.int32, (QB, LANES), 1)
    zero = jnp.zeros((QB, LANES), BF)
    for block in range(band_rows // QB):
        start = block * QB
        queries = qkv_ref[start : start + QB, :LANES]
        both = jnp.concatenate(
            [jnp.where(lane < HDIM, queries, zero), jnp.where(lane >= HDIM, queries, zero)], axis=0
        )
        offsets = win_ref[:, start : start + QB]
        column = lax.broadcasted_iota(jnp.int32, (1, QB), 1) + reach
        bottom = jnp.maximum(column - offsets[0:1], reach - start - first_node)
        top = jnp.minimum(column + offsets[1:2], reach - start - first_node + node_total - 1)
        bottom = jnp.concatenate([bottom, bottom], axis=1)
        top = jnp.concatenate([top, top], axis=1)
        largest = jnp.full((8, 2 * QB), NEG, F32)
        for chunk in range(chunks):
            at = chunk * KC
            scores = dot(k_ref[start + at : start + at + KC, :], both, 1, 1)
            key = lax.broadcasted_iota(jnp.int32, (KC, 2 * QB), 0) + at
            if at + KC - 1 <= reach:
                scores = jnp.where(key >= bottom, scores, NEG)
            elif at >= reach + QB - 1:
                scores = jnp.where(key <= top, scores, NEG)
            else:
                scores = jnp.where((key >= bottom) & (key <= top), scores, NEG)
            score_ref[at : at + KC, :] = scores
            largest = jnp.maximum(largest, jnp.max(scores.reshape(KC // 8, 8, 2 * QB), axis=0))
        largest = jnp.max(largest, axis=0, keepdims=True)
        for chunk in range(chunks):
            at = chunk * KC
            prob_ref[at : at + KC, :] = jnp.exp2(score_ref[at : at + KC, :] - largest).astype(BF)
        for head in range(2):
            mixed = dot(vt_ref[head, :, start : start + keys], prob_ref[:, head * QB : (head + 1) * QB], 1, 0)
            out_ref[head * HDIM : (head + 1) * HDIM, start : start + QB] = (
                mixed[:HDIM] / mixed[HDIM : HDIM + 1]
            ).astype(BF)
    attended = out_ref[...]
    grad = jnp.zeros((LANES, LANES), F32)
    total = jnp.zeros((LANES, LANES), F32)
    for group in range(groups):
        summed = extra_ref[group, :NODE_DEV, :]
        grad += dot(attended[:, group * NODE_DEV : (group + 1) * NODE_DEV], summed, 1, 0)
        total += extra_ref[group, NODE_DEV:, :].astype(F32)
    grad_ref[:LANES, :] = grad.astype(BF)
    grad_ref[LANES:, :] = total.astype(BF)
    node = dot(mix_ref[...], attended, 0, 0).T.astype(BF)
    for group in range(groups):
        node_ref[group] = node[group * NODE_DEV : (group + 1) * NODE_DEV]


def attend(qkv, low, high, win, extra, mix):
    band_rows = qkv.shape[0]
    reach = low.shape[0]
    keys = QB + 2 * reach
    total = band_rows + 2 * reach
    return pl.pallas_call(
        functools.partial(attend_kernel, reach),
        out_shape=(
            jax.ShapeDtypeStruct((extra.shape[0], NODE_DEV, LANES), BF),
            jax.ShapeDtypeStruct((2 * LANES, LANES), BF),
        ),
        scratch_shapes=[
            pltpu.VMEM((total, LANES), BF),
            pltpu.VMEM((2, HDIM + 16, total), BF),
            pltpu.VMEM((keys, 2 * QB), F32),
            pltpu.VMEM((keys, 2 * QB), BF),
            pltpu.VMEM((LANES, band_rows), BF),
        ],
        compiler_params=params(),
        name="attend",
    )(qkv, low, high, win, extra, mix)


def nodes_kernel(parts_ref, node_ref, out_ref):
    total = node_ref[...]
    for group in range(parts_ref.shape[0]):
        total += parts_ref[group].astype(F32)
    out_ref[...] = total.astype(BF)


def sum_nodes(parts, node):
    return pl.pallas_call(
        nodes_kernel,
        out_shape=jax.ShapeDtypeStruct(node.shape, BF),
        compiler_params=params(),
        name="sum_nodes",
    )(parts, node)


def decode_kernel(low_ref, own_ref, high_ref, dec_ref, grid_ref, pred_ref):
    channels, points = grid_ref.shape
    nodes = NODE_DEV
    rows = 4 * LANES
    base = (my_index() - 1) * nodes
    table = jnp.concatenate(
        [
            low_ref[...].astype(F32),
            own_ref[...].astype(F32),
            high_ref[...].astype(F32),
            jnp.zeros((rows - 3 * nodes, LANES), F32),
        ],
        axis=0,
    ).T.astype(BF)
    width = 512
    for at in range(0, points, width):
        node_id = lax.broadcasted_iota(jnp.int32, (rows, width), 0)
        pick = jnp.where(node_id == dec_ref[:, at : at + width] - base, 1.0, 0.0).astype(BF)
        decoded = dot(table, pick, 1, 0)
        pred_ref[:, at : at + width] = (
            grid_ref[:, at : at + width].astype(F32) + decoded[:channels]
        ).astype(BF)


def decode(low, own, high, dec_row, grid_in):
    return pl.pallas_call(
        decode_kernel,
        out_shape=jax.ShapeDtypeStruct(grid_in.shape, BF),
        compiler_params=params(),
        name="decode",
    )(low, own, high, dec_row, grid_in)


def gradient_kernel(parts_ref, w_out_ref, grad_ref):
    model, channels = grad_ref.shape
    groups = parts_ref.shape[0]
    mixed = jnp.zeros((LANES, model), F32)
    for group in range(groups):
        part = parts_ref[group, :LANES, :].astype(F32).T.astype(BF)
        mixed += dot(part, w_out_ref[group * LANES : (group + 1) * LANES, :], 1, 0)
    mixed = mixed.T
    for group in range(groups):
        at = group * LANES
        whole = mixed[at : at + LANES] + parts_ref[group, LANES:, :].astype(F32)
        grad_ref[at : at + LANES, :] = whole[:, :channels]


def gradient(parts, w_out, channels):
    return pl.pallas_call(
        gradient_kernel,
        out_shape=jax.ShapeDtypeStruct((w_out.shape[0], channels), F32),
        compiler_params=params(),
        name="gradient",
    )(parts, w_out)


def steps(axis, shift):
    count = lax.axis_size(axis)
    return [(i, i + shift) for i in range(count) if 0 <= i + shift < count]


def exchange(to_low, to_high, axis):
    from_high = lax.ppermute(to_low, axis, steps(axis, -1))
    from_low = lax.ppermute(to_high, axis, steps(axis, 1))
    return from_low, from_high


def shards(
    grid_in, enc_node, dec_node, win_offsets, w_in, b_in, w_qkv, w_out, norm_gain, w_dec, cotangent
):
    channels = grid_in.shape[0]
    enc_row = enc_node[None]
    dec_row = dec_node[None]
    own, low, high = encode(grid_in, enc_row, w_in, b_in[None], cotangent, dec_row)
    from_low, from_high = exchange(low, high, BOTH)
    packed, enc, summed = project(own, from_low, from_high, norm_gain[None], w_qkv)
    head_rows = lax.all_to_all(packed, "head", split_axis=0, concat_axis=0, tiled=True)
    send, node, mix = side(enc, summed, w_dec, w_out)
    qkv = head_rows.reshape(-1, head_rows.shape[2])
    reach = qkv.shape[0] // 2
    kv_low, kv_high = exchange(qkv[:reach, LANES:], qkv[reach:, LANES:], "band")
    extra = lax.all_to_all(send, "head", split_axis=0, concat_axis=0, tiled=True)
    node_parts, grad_part = attend(qkv, kv_low, kv_high, win_offsets, extra, mix)
    node_parts = lax.all_to_all(node_parts, "head", split_axis=0, concat_axis=0, tiled=True)
    table = sum_nodes(node_parts, node)
    table_low, table_high = exchange(table, table, BOTH)
    prediction = decode(table_low, table, table_high, dec_row, grid_in)
    shift = 1
    count = lax.axis_size("band")
    while shift < count:
        other = lax.ppermute(grad_part, "band", [(i, i ^ shift) for i in range(count)])
        grad_part = (grad_part.astype(F32) + other.astype(F32)).astype(BF)
        shift *= 2
    groups = lax.axis_size("head")
    spread = jnp.broadcast_to(grad_part[None], (groups,) + grad_part.shape)
    parts = lax.all_to_all(spread, "head", split_axis=0, concat_axis=0, tiled=True)
    grad_dec = gradient(parts, w_out, channels)
    return (prediction, grad_dec)


def solution(mesh):
    placed = (
        P(None, BOTH),
        P(BOTH),
        P(BOTH),
        P(None, "band"),
        P(),
        P(),
        P(),
        P(),
        P(),
        P(),
        P(None, BOTH),
    )
    return jax.shard_map(
        shards,
        mesh=mesh,
        in_specs=placed,
        out_specs=(P(None, BOTH), P()),
        check_vma=False,
    )
```

time: 458 us -> 150 us (0.33)
  waiting for transfers between devices: 288 us -> 42.4 us
  matrix products: 45.6 us -> 0 us
  starting transfers between devices: 34 us -> 60.6 us
  local copies, waits for them, and re-layouts: 46.4 us -> 22.5 us
  Pallas kernels: 0 us -> 20.3 us
  other arithmetic: 15 us -> 0.11 us
  between operations: 14.3 us -> 0.85 us
  blocking collectives: 11.4 us -> 0 us
    psum x1 -> x0, waiting for transfers between devices: 245 us -> none  [shards(): grad_dec = lax.psum(grad_term, ('band', 'head'))]
    dot_general x7 -> x0, matrix products: 30.3 us -> none  [the longest x1 11.4 us: shards(): jnp.einsum('hqk,khd->qhd', weights, values, preferred_element_type=jnp.fl...]
    ppermute x6 -> x11, starting transfers between devices: 19.6 us -> 42.6 us  [the longest x3 18.6 us: exchange(): from_high = lax.ppermute(to_low, axis, steps(axis, -1))]
    pallas_call x0 -> x7, Pallas kernels: none -> 20.3 us  [the longest x1 7.75 us: attend(): pl.pallas_call(functools.partial(attend_kernel, reach), out_shape=(jax.Sh...]
    sub x1 -> x0, matrix products: 15.2 us -> none  [shards(): weights = jnp.exp(scores - largest)]
    and x1 -> x0, other arithmetic: 11.9 us -> none  [shards(): allowed & (global_key >= 0)[None, :] & (global_key < node_total)[None, :]]
    all_to_all x1 -> x0, blocking collectives: 11.4 us -> none  [shards(): lax.all_to_all(attended, 'head', split_axis=0, concat_axis=1, tiled=True)]
    gather x1 -> x0, local copies, waits for them, and re-layouts: 9.63 us -> none  [shards(): node_rows = beside_all[dec_node - base_node]]
  transfers between devices with their start and end apart: 8 -> 15, of which waited for: 6 -> 12; matrix products, arithmetic and copies ran while one was open for 4% -> 2% of each run, Pallas kernels for 0% -> 1%
where the time goes in v1:
time: 150 us; the launch traced here: 147 us
  starting transfers between devices  60.6 us (40%)
  waiting for transfers between devices  42.4 us (28%)
  local copies, waits for them, and re-layouts  22.5 us (15%)
  Pallas kernels  20.3 us (14%)
    unnamed x50, local copies, waits for them, and re-layouts  20.8 us
    ppermute x3, starting transfers between devices, exchange(): from_high = lax.ppermute(to_low, axis, steps(axis, -1))  18.6 us
    ppermute x5, starting transfers between devices, shards(): lax.ppermute(grad_part, 'band', [(i, i ^ shift) for i in range(count)])  14.9 us
    ppermute x5, waiting for transfers between devices, shards(): lax.ppermute(grad_part, 'band', [(i, i ^ shift) for i in range(count)])  10.1 us
    ppermute x3, waiting for transfers between devices, exchange(): from_high = lax.ppermute(to_low, axis, steps(axis, -1))  9.25 us
    ppermute x3, starting transfers between devices, exchange(): from_low = lax.ppermute(to_high, axis, steps(axis, 1))  9.14 us
    ppermute x3, waiting for transfers between devices, exchange(): from_low = lax.ppermute(to_high, axis, steps(axis, 1))  8.25 us
    pallas_call x1, Pallas kernels, attend(): pl.pallas_call(functools.partial(attend_kernel, reach), out_shape=(jax.Sh...  7.75 us
  transfers between devices with their start and end apart: 15, of which 12 were waited for; matrix products, arithmetic and copies ran while one was open for 2% of the time, Pallas kernels for 1%

profile of v1, /device:TPU:32, one launch (start us, length us, event | category | flops | bytes accessed | tf_op | source)
XLA Modules:
  0.0 146.8 jit_solution(7054599288282953301)
XLA Ops:
  0.6 1.0 copy-done.2
  1.7 1.0 copy-done.7
  5.7 4.1 %encode.1 = (f32[160,1152]{1,0:T(8,128)S(1)}, bf16[160,1152]{1,0:T(8,128)(2,1)S(1)}, bf16[160,1152]{1,0:T(8,128)(2,1)S(1)}) custom-call(bf16[110,2048]{1,0:T(8,128)(2,1)S(1)} %copy-done.2, s32[1,2048]{1,0:T(1,128)S(1)} %bitcast.10, bf16[110,1024]{1,0:T(8,128)(2,1)S(1)} %copy-done.11, f32[1,1024]{1,0:T(1,128)S(1)} %bitcast.11, ...), custom_call_target="tpu_custom_call" | custom-call | tf_op jit(solution)/shard_map/encode/pallas_call | solution.py:67
  9.8 3.4 %collective-permute-start = (bf16[160,1152]{1,0:T(8,128)(2,1)S(1)}, bf16[160,1152]{1,0:T(8,128)(2,1)S(1)}, u32[]{:S(2)}, u32[]{:S(2)}) collective-permute-start(bf16[160,1152]{1,0:T(8,128)(2,1)S(1)} %get-tuple-element.14), channel_id=1, source_target_pairs={{0,1},{1,2},{2,3},{3,4},{4,5},{5,6},{6,7},{7,8},{8,9},{9,10},{10,1... | collective-permute-start | bytes 1105928 | tf_op jit(solution)/shard_map/ppermute | solution.py:358
  13.2 6.4 %collective-permute-start.1 = (bf16[160,1152]{1,0:T(8,128)(2,1)S(1)}, bf16[160,1152]{1,0:T(8,128)(2,1)S(1)}, u32[]{:S(2)}, u32[]{:S(2)}) collective-permute-start(bf16[160,1152]{1,0:T(8,128)(2,1)S(1)} %get-tuple-element.15), channel_id=1, source_target_pairs={{1,0},{2,1},{3,2},{4,3},{5,4},{6,5},{7,6},{8,7},{9,8},{10,9},{11,1... | collective-permute-start | bytes 1105928 | tf_op jit(solution)/shard_map/ppermute | solution.py:357
  19.6 5.5 %collective-permute-done.from_low = bf16[160,1152]{1,0:T(8,128)(2,1)S(1)} collective-permute-done((bf16[160,1152]{1,0:T(8,128)(2,1)S(1)}, bf16[160,1152]{1,0:T(8,128)(2,1)S(1)}, u32[]{:S(2)}, u32[]{:S(2)}) %collective-permute-start) | collective-permute-done | bytes 368672 | tf_op jit(solution)/shard_map/ppermute | solution.py:358
  25.1 5.8 %collective-permute-done.1.from_high = bf16[160,1152]{1,0:T(8,128)(2,1)S(1)} collective-permute-done((bf16[160,1152]{1,0:T(8,128)(2,1)S(1)}, bf16[160,1152]{1,0:T(8,128)(2,1)S(1)}, u32[]{:S(2)}, u32[]{:S(2)}) %collective-permute-start.1) | collective-permute-done | bytes 368672 | tf_op jit(solution)/shard_map/ppermute | solution.py:357
  30.9 2.8 %copy-done = bf16[1024,3072]{1,0:T(8,128)(2,1)S(1)} copy-done((bf16[1024,3072]{1,0:T(8,128)(2,1)S(1)}, bf16[1024,3072]{1,0:T(8,128)(2,1)}, u32[]{:S(2)}) %copy-start) | copy-done | bytes 6291480
  34.4 5.5 %project.1 = (bf16[8,160,384]{2,1,0:T(8,128)(2,1)S(1)}, bf16[160,1024]{1,0:T(8,128)(2,1)S(1)}, bf16[160,128]{1,0:T(8,128)(2,1)S(1)}) custom-call(f32[160,1152]{1,0:T(8,128)S(1)} %get-tuple-element.13.own_ref, bf16[160,1152]{1,0:T(8,128)(2,1)S(1)} %collective-permute-done.from_low, bf16[160,1152]{1,0:T(8,128)(2,1)S(1)} %collective-permute-done.1.from_high, ...), custom_call_target="tpu_custom_call" | custom-call | tf_op jit(solution)/shard_map/project/pallas_call | solution.py:110
  42.2 5.1 %all-to-all-start = ((bf16[8,160,384]{2,1,0:T(8,128)(2,1)}), bf16[8,160,384]{2,1,0:T(8,128)(2,1)S(1)}, u32[]{:S(2)}, u32[]{:S(2)}) async-start(bf16[8,160,384]{2,1,0:T(8,128)(2,1)} %copy-done.5), calls=%async_computation | async-start | bytes 1966080 | tf_op jit(solution)/shard_map/all_to_all | solution.py:371
  47.3 1.8 %copy.13.w_dec_ref = bf16[1024,110]{1,0:T(8,128)(2,1)} copy(bf16[1024,110]{0,1:T(8,128)(2,1)} %param.20) | data formatting | bytes 450560 | tf_op args[9]
  54.5 7.0 %all-to-all-done = bf16[8,160,384]{2,1,0:T(8,128)(2,1)S(1)} async-done(((bf16[8,160,384]{2,1,0:T(8,128)(2,1)}), bf16[8,160,384]{2,1,0:T(8,128)(2,1)S(1)}, u32[]{:S(2)}, u32[]{:S(2)}) %all-to-all-start) | async-done | bytes 983072 | tf_op jit(solution)/shard_map/all_to_all | solution.py:371
  61.5 4.2 %all-to-all-start.1 = ((bf16[8,288,128]{2,1,0:T(8,128)(2,1)}), bf16[8,288,128]{2,1,0:T(8,128)(2,1)}, u32[]{:S(2)}, u32[]{:S(2)}) async-start(bf16[8,288,128]{2,1,0:T(8,128)(2,1)} %copy-done.6), calls=%async_computation.1 | async-start | bytes 1179648 | tf_op jit(solution)/shard_map/all_to_all | solution.py:376
  66.6 1.9 %collective-permute-start.2 = (bf16[640,256]{1,0:T(8,128)(2,1)}, bf16[640,256]{1,0:T(8,128)(2,1)}, u32[]{:S(2)}, u32[]{:S(2)}) collective-permute-start(bf16[640,256]{1,0:T(8,128)(2,1)} %get-tuple-element.27), channel_id=1, source_target_pairs={{0,8},{8,16},{16,24},{24,32},{32,40},{40,48},{48,56},{56,64},{64,7... | collective-permute-start | bytes 983048 | tf_op jit(solution)/shard_map/ppermute | solution.py:358
  68.5 6.2 %collective-permute-start.3 = (bf16[640,256]{1,0:T(8,128)(2,1)}, bf16[640,256]{1,0:T(8,128)(2,1)}, u32[]{:S(2)}, u32[]{:S(2)}) collective-permute-start(bf16[640,256]{1,0:T(8,128)(2,1)} %get-tuple-element.26), channel_id=1, source_target_pairs={{8,0},{16,8},{24,16},{32,24},{40,32},{48,40},{56,48},{64,56},{72,6... | collective-permute-start | bytes 983048 | tf_op jit(solution)/shard_map/ppermute | solution.py:357
  74.9 2.8 %collective-permute-done.2.low_ref = bf16[640,256]{1,0:T(8,128)(2,1)} collective-permute-done((bf16[640,256]{1,0:T(8,128)(2,1)}, bf16[640,256]{1,0:T(8,128)(2,1)}, u32[]{:S(2)}, u32[]{:S(2)}) %collective-permute-start.2) | collective-permute-done | bytes 327712 | tf_op jit(solution)/shard_map/ppermute | solution.py:358
  77.7 1.8 %collective-permute-done.3.high_ref = bf16[640,256]{1,0:T(8,128)(2,1)} collective-permute-done((bf16[640,256]{1,0:T(8,128)(2,1)}, bf16[640,256]{1,0:T(8,128)(2,1)}, u32[]{:S(2)}, u32[]{:S(2)}) %collective-permute-start.3) | collective-permute-done | bytes 327712 | tf_op jit(solution)/shard_map/ppermute | solution.py:357
  80.9 7.8 %attend.1 = (bf16[8,160,128]{2,1,0:T(8,128)(2,1)S(1)}, bf16[256,128]{1,0:T(8,128)(2,1)S(1)}) custom-call(bf16[1280,384]{1,0:T(8,128)(2,1)S(1)} %bitcast.7, bf16[640,256]{1,0:T(8,128)(2,1)} %collective-permute-done.2.low_ref, bf16[640,256]{1,0:T(8,128)(2,1)} %collective-permute-done.3.high_ref, s32[2,1280]{1,0:T(2,128)S(1)} %copy-done.20, ...), custom_call_target="tpu_custom_call" | custom-call | tf_op jit(solution)/shard_map/attend/pallas_call | solution.py:261
  88.6 2.2 %collective-permute-start.6 = (bf16[256,128]{1,0:T(8,128)(2,1)S(1)}, bf16[256,128]{1,0:T(8,128)(2,1)S(1)}, u32[]{:S(2)}, u32[]{:S(2)}) collective-permute-start(bf16[256,128]{1,0:T(8,128)(2,1)S(1)} %get-tuple-element.23), channel_id=1, source_target_pairs={{0,8},{8,0},{16,24},{24,16},{32,40},{40,32},{48,56},{56,48},{64,72... | collective-permute-start | bytes 196616 | tf_op jit(solution)/shard_map/ppermute | solution.py:385
  91.8 3.1 %collective-permute-start.7 = (bf16[256,128]{1,0:T(8,128)(2,1)S(1)}, bf16[256,128]{1,0:T(8,128)(2,1)S(1)}, u32[]{:S(2)}, u32[]{:S(2)}) collective-permute-start(bf16[256,128]{1,0:T(8,128)(2,1)S(1)} %add_convert_fusion.4), channel_id=1, source_target_pairs={{0,16},{8,24},{16,0},{24,8},{32,48},{40,56},{48,32},{56,40},{64,80... | collective-permute-start | bytes 196616 | tf_op jit(solution)/shard_map/ppermute | solution.py:385
  94.9 2.8 %collective-permute-done.7 = bf16[256,128]{1,0:T(8,128)(2,1)S(1)} collective-permute-done((bf16[256,128]{1,0:T(8,128)(2,1)S(1)}, bf16[256,128]{1,0:T(8,128)(2,1)S(1)}, u32[]{:S(2)}, u32[]{:S(2)}) %collective-permute-start.7) | collective-permute-done | bytes 65568 | tf_op jit(solution)/shard_map/ppermute | solution.py:385
  97.9 4.2 %collective-permute-done.8 = bf16[256,128]{1,0:T(8,128)(2,1)S(1)} collective-permute-done((bf16[256,128]{1,0:T(8,128)(2,1)S(1)}, bf16[256,128]{1,0:T(8,128)(2,1)S(1)}, u32[]{:S(2)}, u32[]{:S(2)}) %collective-permute-start.8) | collective-permute-done | bytes 65568 | tf_op jit(solution)/shard_map/ppermute | solution.py:385
  102.1 5.6 %collective-permute-start.9 = (bf16[256,128]{1,0:T(8,128)(2,1)S(1)}, bf16[256,128]{1,0:T(8,128)(2,1)S(1)}, u32[]{:S(2)}, u32[]{:S(2)}) collective-permute-start(bf16[256,128]{1,0:T(8,128)(2,1)S(1)} %add_convert_fusion.2), channel_id=1, source_target_pairs={{0,64},{8,72},{16,80},{24,88},{32,96},{40,104},{48,112},{56,120},{... | collective-permute-start | bytes 196616 | tf_op jit(solution)/shard_map/ppermute | solution.py:385
  107.7 2.2 %collective-permute-done.9 = bf16[256,128]{1,0:T(8,128)(2,1)S(1)} collective-permute-done((bf16[256,128]{1,0:T(8,128)(2,1)S(1)}, bf16[256,128]{1,0:T(8,128)(2,1)S(1)}, u32[]{:S(2)}, u32[]{:S(2)}) %collective-permute-start.9) | collective-permute-done | bytes 65568 | tf_op jit(solution)/shard_map/ppermute | solution.py:385
  110.0 3.8 %collective-permute-start.10 = (bf16[256,128]{1,0:T(8,128)(2,1)S(1)}, bf16[256,128]{1,0:T(8,128)(2,1)S(1)}, u32[]{:S(2)}, u32[]{:S(2)}) collective-permute-start(bf16[256,128]{1,0:T(8,128)(2,1)S(1)} %add_convert_fusion.1), channel_id=1, source_target_pairs={{0,128},{8,136},{16,144},{24,152},{32,160},{40,168},{48,176},{56,1... | collective-permute-start | bytes 196616 | tf_op jit(solution)/shard_map/ppermute | solution.py:385
  113.8 5.2 %all-to-all-start.2 = ((bf16[8,160,128]{2,1,0:T(8,128)(2,1)}), bf16[8,160,128]{2,1,0:T(8,128)(2,1)S(1)}, u32[]{:S(2)}, u32[]{:S(2)}) async-start(bf16[8,160,128]{2,1,0:T(8,128)(2,1)} %copy-done.10), calls=%async_computation.2 | async-start | bytes 655360 | tf_op jit(solution)/shard_map/all_to_all | solution.py:378
  119.1 7.6 %all-to-all-done.2.parts_ref = bf16[8,160,128]{2,1,0:T(8,128)(2,1)S(1)} async-done(((bf16[8,160,128]{2,1,0:T(8,128)(2,1)}), bf16[8,160,128]{2,1,0:T(8,128)(2,1)S(1)}, u32[]{:S(2)}, u32[]{:S(2)}) %all-to-all-start.2) | async-done | bytes 327712 | tf_op jit(solution)/shard_map/all_to_all | solution.py:378
  127.5 3.5 %all-to-all-start.3 = ((bf16[8,256,128]{2,1,0:T(8,128)(2,1)}), bf16[8,256,128]{2,1,0:T(8,128)(2,1)S(1)}, u32[]{:S(2)}, u32[]{:S(2)}) async-start(bf16[8,256,128]{2,1,0:T(8,128)(2,1)} %broadcast_in_dim.26), calls=%async_computation.3 | async-start | bytes 1048576 | tf_op jit(solution)/shard_map/all_to_all | solution.py:390
  132.0 3.8 %collective-permute-start.4 = (bf16[160,128]{1,0:T(8,128)(2,1)S(1)}, bf16[160,128]{1,0:T(8,128)(2,1)S(1)}, u32[]{:S(2)}, u32[]{:S(2)}) collective-permute-start(bf16[160,128]{1,0:T(8,128)(2,1)S(1)} %sum_nodes.1.own_ref), channel_id=1, source_target_pairs={{0,1},{1,2},{2,3},{3,4},{4,5},{5,6},{6,7},{7,8},{8,9},{9,10},{10,1... | collective-permute-start | bytes 122888 | tf_op jit(solution)/shard_map/ppermute | solution.py:358
  135.8 6.0 %collective-permute-start.5 = (bf16[160,128]{1,0:T(8,128)(2,1)S(1)}, bf16[160,128]{1,0:T(8,128)(2,1)S(1)}, u32[]{:S(2)}, u32[]{:S(2)}) collective-permute-start(bf16[160,128]{1,0:T(8,128)(2,1)S(1)} %sum_nodes.1.own_ref), channel_id=1, source_target_pairs={{1,0},{2,1},{3,2},{4,3},{5,4},{6,5},{7,6},{8,7},{9,8},{10,9},{11,1... | collective-permute-start | bytes 122888 | tf_op jit(solution)/shard_map/ppermute | solution.py:357
  141.8 1.6 %collective-permute-done.5.high_ref = bf16[160,128]{1,0:T(8,128)(2,1)S(1)} collective-permute-done((bf16[160,128]{1,0:T(8,128)(2,1)S(1)}, bf16[160,128]{1,0:T(8,128)(2,1)S(1)}, u32[]{:S(2)}, u32[]{:S(2)}) %collective-permute-start.5) | collective-permute-done | bytes 40992 | tf_op jit(solution)/shard_map/ppermute | solution.py:357
  143.4 1.5 %decode.1 = bf16[110,2048]{1,0:T(8,128)(2,1)} custom-call(bf16[160,128]{1,0:T(8,128)(2,1)S(1)} %collective-permute-done.4.low_ref, bf16[160,128]{1,0:T(8,128)(2,1)S(1)} %sum_nodes.1.own_ref, bf16[160,128]{1,0:T(8,128)(2,1)S(1)} %collective-permute-done.5.high_ref, s32[1,2048]{1,0:T(1,128)S(1)} %bitcast.9, bf16[110,2048]{1,0:T(8,128)(2,1)S(1)} %copy-done.3), custom_call_target="tpu_custom_call" | custom-call | tf_op jit(solution)/shard_map/decode/pallas_call | solution.py:320
  (62 shorter events, 18.7 us)
Async XLA Ops:
  0.6 1.0 copy-start.2
  1.7 1.0 copy-start.7
  2.7 0.9 copy-start.11
  9.8 15.3 %collective-permute-start = (bf16[160,1152]{1,0:T(8,128)(2,1)S(1)}, bf16[160,1152]{1,0:T(8,128)(2,1)S(1)}, u32[]{:S(2)}, u32[]{:S(2)}) collective-permute-start(bf16[160,1152]{1,0:T(8,128)(2,1)S(1)} %get-tuple-element.14), channel_id=1, source_target_pairs={{0,1},{1,2},{2,3},{3,4},{4,5},{5,6},{6,7},{7,8},{8,9},{9,10},{10,1... | collective-permute-start | bytes 1105928 | tf_op jit(solution)/shard_map/ppermute | solution.py:358
  13.2 17.7 %collective-permute-start.1 = (bf16[160,1152]{1,0:T(8,128)(2,1)S(1)}, bf16[160,1152]{1,0:T(8,128)(2,1)S(1)}, u32[]{:S(2)}, u32[]{:S(2)}) collective-permute-start(bf16[160,1152]{1,0:T(8,128)(2,1)S(1)} %get-tuple-element.15), channel_id=1, source_target_pairs={{1,0},{2,1},{3,2},{4,3},{5,4},{6,5},{7,6},{8,7},{9,8},{10,9},{11,1... | collective-permute-start | bytes 1105928 | tf_op jit(solution)/shard_map/ppermute | solution.py:357
  30.9 2.8 %copy-start = (bf16[1024,3072]{1,0:T(8,128)(2,1)S(1)}, bf16[1024,3072]{1,0:T(8,128)(2,1)}, u32[]{:S(2)}) copy-start(bf16[1024,3072]{1,0:T(8,128)(2,1)} %wv_ref.1) | copy-start | bytes 18874372
  34.4 14.8 %copy-start.1 = (bf16[1024,1024]{1,0:T(8,128)(2,1)S(1)}, bf16[1024,1024]{1,0:T(8,128)(2,1)}, u32[]{:S(2)}) copy-start(bf16[1024,1024]{1,0:T(8,128)(2,1)} %w_out_ref.3) | copy-start | bytes 6291460
  39.9 1.0 copy-start.5
  40.9 0.7 copy-start.8
  42.2 19.2 %all-to-all-start = ((bf16[8,160,384]{2,1,0:T(8,128)(2,1)}), bf16[8,160,384]{2,1,0:T(8,128)(2,1)S(1)}, u32[]{:S(2)}, u32[]{:S(2)}) async-start(bf16[8,160,384]{2,1,0:T(8,128)(2,1)} %copy-done.5), calls=%async_computation | async-start | bytes 1966080 | tf_op jit(solution)/shard_map/all_to_all | solution.py:371
  47.3 96.1 %copy-start.3 = (bf16[110,2048]{1,0:T(8,128)(2,1)S(1)}, bf16[110,2048]{1,0:T(8,128)(2,1)}, u32[]{:S(2)}) copy-start(bf16[110,2048]{1,0:T(8,128)(2,1)} %grid_ref.3) | copy-start | bytes 1351684
  47.3 96.1 %copy-start.17 = (s32[2048]{0:T(1024)S(1)}, s32[2048]{0:T(1024)}, u32[]{:S(2)}) copy-start(s32[2048]{0:T(1024)} %param.13) | copy-start | bytes 24580
  49.2 1.0 copy-start.4
  50.1 1.0 copy-start.9
  51.1 0.8 copy-start.15
  52.4 0.8 copy-start.6
  61.5 13.4 %all-to-all-start.1 = ((bf16[8,288,128]{2,1,0:T(8,128)(2,1)}), bf16[8,288,128]{2,1,0:T(8,128)(2,1)}, u32[]{:S(2)}, u32[]{:S(2)}) async-start(bf16[8,288,128]{2,1,0:T(8,128)(2,1)} %copy-done.6), calls=%async_computation.1 | async-start | bytes 1179648 | tf_op jit(solution)/shard_map/all_to_all | solution.py:376
  66.6 11.1 %collective-permute-start.2 = (bf16[640,256]{1,0:T(8,128)(2,1)}, bf16[640,256]{1,0:T(8,128)(2,1)}, u32[]{:S(2)}, u32[]{:S(2)}) collective-permute-start(bf16[640,256]{1,0:T(8,128)(2,1)} %get-tuple-element.27), channel_id=1, source_target_pairs={{0,8},{8,16},{16,24},{24,32},{32,40},{40,48},{48,56},{56,64},{64,7... | collective-permute-start | bytes 983048 | tf_op jit(solution)/shard_map/ppermute | solution.py:358
  68.5 10.9 %collective-permute-start.3 = (bf16[640,256]{1,0:T(8,128)(2,1)}, bf16[640,256]{1,0:T(8,128)(2,1)}, u32[]{:S(2)}, u32[]{:S(2)}) collective-permute-start(bf16[640,256]{1,0:T(8,128)(2,1)} %get-tuple-element.26), channel_id=1, source_target_pairs={{8,0},{16,8},{24,16},{32,24},{40,32},{48,40},{56,48},{64,56},{72,6... | collective-permute-start | bytes 983048 | tf_op jit(solution)/shard_map/ppermute | solution.py:357
  79.4 0.8 copy-start.19
  80.2 0.7 copy-start.20
  88.6 25.2 %copy-start.10 = (bf16[8,160,128]{2,1,0:T(8,128)(2,1)}, bf16[8,160,128]{2,1,0:T(8,128)(2,1)S(1)}, u32[]{:S(2)}) copy-start(bf16[8,160,128]{2,1,0:T(8,128)(2,1)S(1)} %get-tuple-element.21) | copy-start | bytes 983044
  88.6 3.1 %collective-permute-start.6 = (bf16[256,128]{1,0:T(8,128)(2,1)S(1)}, bf16[256,128]{1,0:T(8,128)(2,1)S(1)}, u32[]{:S(2)}, u32[]{:S(2)}) collective-permute-start(bf16[256,128]{1,0:T(8,128)(2,1)S(1)} %get-tuple-element.23), channel_id=1, source_target_pairs={{0,8},{8,0},{16,24},{24,16},{32,40},{40,32},{48,56},{56,48},{64,72... | collective-permute-start | bytes 196616 | tf_op jit(solution)/shard_map/ppermute | solution.py:385
  91.8 5.9 %collective-permute-start.7 = (bf16[256,128]{1,0:T(8,128)(2,1)S(1)}, bf16[256,128]{1,0:T(8,128)(2,1)S(1)}, u32[]{:S(2)}, u32[]{:S(2)}) collective-permute-start(bf16[256,128]{1,0:T(8,128)(2,1)S(1)} %add_convert_fusion.4), channel_id=1, source_target_pairs={{0,16},{8,24},{16,0},{24,8},{32,48},{40,56},{48,32},{56,40},{64,80... | collective-permute-start | bytes 196616 | tf_op jit(solution)/shard_map/ppermute | solution.py:385
  97.7 4.4 %collective-permute-start.8 = (bf16[256,128]{1,0:T(8,128)(2,1)S(1)}, bf16[256,128]{1,0:T(8,128)(2,1)S(1)}, u32[]{:S(2)}, u32[]{:S(2)}) collective-permute-start(bf16[256,128]{1,0:T(8,128)(2,1)S(1)} %add_convert_fusion.3), channel_id=1, source_target_pairs={{0,32},{8,40},{16,48},{24,56},{32,0},{40,8},{48,16},{56,24},{64,96... | collective-permute-start | bytes 196616 | tf_op jit(solution)/shard_map/ppermute | solution.py:385
  102.1 7.8 %collective-permute-start.9 = (bf16[256,128]{1,0:T(8,128)(2,1)S(1)}, bf16[256,128]{1,0:T(8,128)(2,1)S(1)}, u32[]{:S(2)}, u32[]{:S(2)}) collective-permute-start(bf16[256,128]{1,0:T(8,128)(2,1)S(1)} %add_convert_fusion.2), channel_id=1, source_target_pairs={{0,64},{8,72},{16,80},{24,88},{32,96},{40,104},{48,112},{56,120},{... | collective-permute-start | bytes 196616 | tf_op jit(solution)/shard_map/ppermute | solution.py:385
  110.0 9.1 %collective-permute-start.10 = (bf16[256,128]{1,0:T(8,128)(2,1)S(1)}, bf16[256,128]{1,0:T(8,128)(2,1)S(1)}, u32[]{:S(2)}, u32[]{:S(2)}) collective-permute-start(bf16[256,128]{1,0:T(8,128)(2,1)S(1)} %add_convert_fusion.1), channel_id=1, source_target_pairs={{0,128},{8,136},{16,144},{24,152},{32,160},{40,168},{48,176},{56,1... | collective-permute-start | bytes 196616 | tf_op jit(solution)/shard_map/ppermute | solution.py:385
  113.8 12.9 %all-to-all-start.2 = ((bf16[8,160,128]{2,1,0:T(8,128)(2,1)}), bf16[8,160,128]{2,1,0:T(8,128)(2,1)S(1)}, u32[]{:S(2)}, u32[]{:S(2)}) async-start(bf16[8,160,128]{2,1,0:T(8,128)(2,1)} %copy-done.10), calls=%async_computation.2 | async-start | bytes 655360 | tf_op jit(solution)/shard_map/all_to_all | solution.py:378
  127.5 17.4 %all-to-all-start.3 = ((bf16[8,256,128]{2,1,0:T(8,128)(2,1)}), bf16[8,256,128]{2,1,0:T(8,128)(2,1)S(1)}, u32[]{:S(2)}, u32[]{:S(2)}) async-start(bf16[8,256,128]{2,1,0:T(8,128)(2,1)} %broadcast_in_dim.26), calls=%async_computation.3 | async-start | bytes 1048576 | tf_op jit(solution)/shard_map/all_to_all | solution.py:390
  131.0 0.9 copy-start.13
  132.0 9.8 %collective-permute-start.4 = (bf16[160,128]{1,0:T(8,128)(2,1)S(1)}, bf16[160,128]{1,0:T(8,128)(2,1)S(1)}, u32[]{:S(2)}, u32[]{:S(2)}) collective-permute-start(bf16[160,128]{1,0:T(8,128)(2,1)S(1)} %sum_nodes.1.own_ref), channel_id=1, source_target_pairs={{0,1},{1,2},{2,3},{3,4},{4,5},{5,6},{6,7},{7,8},{8,9},{9,10},{10,1... | collective-permute-start | bytes 122888 | tf_op jit(solution)/shard_map/ppermute | solution.py:358
  135.8 7.6 %collective-permute-start.5 = (bf16[160,128]{1,0:T(8,128)(2,1)S(1)}, bf16[160,128]{1,0:T(8,128)(2,1)S(1)}, u32[]{:S(2)}, u32[]{:S(2)}) collective-permute-start(bf16[160,128]{1,0:T(8,128)(2,1)S(1)} %sum_nodes.1.own_ref), channel_id=1, source_target_pairs={{1,0},{2,1},{3,2},{4,3},{5,4},{6,5},{7,6},{8,7},{9,8},{10,9},{11,1... | collective-permute-start | bytes 122888 | tf_op jit(solution)/shard_map/ppermute | solution.py:357
  (7 other events, 4.6 us)

commit v2 on v1

v2 whole, which is shorter than its diff:
```python
import functools

import jax
import jax.numpy as jnp
from jax import lax
from jax.experimental import pallas as pl
from jax.experimental.pallas import tpu as pltpu
from jax.sharding import PartitionSpec as P

HDIM = 64
NODE_DEV = 160
BOTH = ("band", "head")
LANES = 128
QB = 256
KC = 128
BF = jnp.bfloat16
F32 = jnp.float32
LOG2E = 1.4426950408889634
NEG = -1e30
HBM = pl.BlockSpec(memory_space=pltpu.HBM)
VMEM = pl.BlockSpec(memory_space=pltpu.VMEM)


def params(mib=24):
    return pltpu.CompilerParams(vmem_limit_bytes=mib * 1024 * 1024)


def dot(a, b, ca, cb):
    return lax.dot_general(a, b, (((ca,), (cb,)), ((), ())), preferred_element_type=F32)


def shape(dims, dtype):
    return jax.ShapeDtypeStruct(dims, dtype)


def pinned(*arrays):
    return tuple(pltpu.with_memory_space_constraint(a, pltpu.HBM) for a in arrays)


def started(copies):
    for copy in copies:
        copy.start()
    return copies


def chunk_bases():
    index = lax.axis_index("band") * lax.axis_size("head") + lax.axis_index("head")
    side = 1 - 2 * lax.rem(index, 2)
    return (index - side) * NODE_DEV, index * NODE_DEV, (index + side) * NODE_DEV


def encode_kernel(grid_hbm, enc_hbm, w_hbm, b_hbm, cot_hbm, dec_hbm, far_ref, mid_ref, own_ref,
                  grid_ref, enc_ref, w_ref, b_ref, cot_ref, dec_ref, rows_ref, w_pad, cot_pad, pick_ref, sem):
    channels, points = grid_ref.shape
    model = w_ref.shape[1]
    nodes = NODE_DEV
    copies = started(
        [
            pltpu.make_async_copy(source, target, sem.at[at])
            for at, (source, target) in enumerate(
                [(grid_hbm, grid_ref), (enc_hbm, enc_ref), (w_hbm, w_ref), (b_hbm, b_ref), (cot_hbm, cot_ref), (dec_hbm, dec_ref)]
            )
        ]
    )
    bases = chunk_bases()
    node_id = lax.broadcasted_iota(jnp.int32, (nodes, points), 0)

    def pick(target):
        for at, base in enumerate(bases):
            pick_ref[at * nodes : (at + 1) * nodes, :] = jnp.where(node_id == target - base, 1.0, 0.0).astype(BF)

    copies[1].wait()
    pick(enc_ref[...])
    copies[0].wait()
    padded = jnp.concatenate(
        [grid_ref[...].astype(F32), jnp.zeros((LANES - channels, points), F32)], axis=0
    )
    rows_ref[...] = padded.T.astype(BF)
    copies[2].wait()
    copies[3].wait()
    w_pad[...] = jnp.zeros_like(w_pad)
    w_pad[:channels, :] = (w_ref[...].astype(F32) * 0.5).astype(BF)
    width = 256
    for at in range(0, model, width):
        half = dot(rows_ref[...], w_pad[:, at : at + width], 1, 0) + b_ref[:, at : at + width] * 0.5
        message = (half + half * jnp.tanh(half)).astype(BF)
        spread = dot(pick_ref[...], message, 1, 0)
        far_ref[:, at : at + width] = spread[:nodes].astype(BF)
        mid_ref[:, at : at + width] = spread[nodes : 2 * nodes].astype(BF)
        own_ref[:, at : at + width] = spread[2 * nodes :]
    copies[4].wait()
    copies[5].wait()
    cot_pad[...] = jnp.zeros_like(cot_pad)
    cot_pad[:channels, :] = cot_ref[...]
    pick(dec_ref[...])
    spread = dot(pick_ref[...], cot_pad[...], 1, 1)
    far_ref[:, model:] = spread[:nodes].astype(BF)
    mid_ref[:, model:] = spread[nodes : 2 * nodes].astype(BF)
    own_ref[:, model:] = spread[2 * nodes :]


def encode(grid_in, enc_row, w_in, b_row, cotangent, dec_row):
    channels, points = grid_in.shape
    model = w_in.shape[1]
    wide = model + LANES
    operands = (grid_in, enc_row, w_in, b_row, cotangent, dec_row)
    return pl.pallas_call(
        encode_kernel,
        in_specs=[HBM] * 6,
        out_specs=(VMEM,) * 3,
        out_shape=(shape((NODE_DEV, wide), BF), shape((NODE_DEV, wide), BF), shape((NODE_DEV, wide), F32)),
        scratch_shapes=[pltpu.VMEM(a.shape, a.dtype) for a in operands]
        + [
            pltpu.VMEM((points, LANES), BF),
            pltpu.VMEM((LANES, model), BF),
            pltpu.VMEM((LANES, points), BF),
            pltpu.VMEM((3 * NODE_DEV, points), BF),
            pltpu.SemaphoreType.DMA((6,)),
        ],
        compiler_params=params(),
        name="encode",
    )(*pinned(*operands))


def load_kernel(w_hbm, out_hbm, dec_hbm, after_ref, w_ref, dec_ref, mix_ref, out_rows, dec_rows, sem):
    channels = dec_rows.shape[0]
    at = pl.multiple_of(lax.axis_index("head") * LANES, LANES)
    copies = started(
        [
            pltpu.make_async_copy(out_hbm.at[pl.ds(at, LANES), :], out_rows, sem.at[0]),
            pltpu.make_async_copy(dec_hbm, dec_rows, sem.at[1]),
            pltpu.make_async_copy(w_hbm, w_ref, sem.at[2]),
        ]
    )
    copies[0].wait()
    copies[1].wait()
    dec_ref[...] = jnp.zeros_like(dec_ref)
    dec_ref[:channels, :] = dec_rows[...]
    mix_ref[...] = dot(out_rows[...], dec_ref[...], 1, 1).astype(BF)
    copies[2].wait()


def load(w_qkv, w_out, dec_cols, after):
    model = w_qkv.shape[0]
    return pl.pallas_call(
        load_kernel,
        in_specs=[HBM] * 3 + [pl.BlockSpec(memory_space=pl.ANY)],
        out_specs=(VMEM,) * 3,
        out_shape=(shape(w_qkv.shape, BF), shape((LANES, model), BF), shape((LANES, LANES), BF)),
        scratch_shapes=[
            pltpu.VMEM((LANES, model), BF),
            pltpu.VMEM(dec_cols.shape, BF),
            pltpu.SemaphoreType.DMA((3,)),
        ],
        compiler_params=params(),
        cost_estimate=pl.CostEstimate(flops=2 * model * LANES * LANES, bytes_accessed=2 * w_qkv.size, transcendentals=0),
        name="load",
    )(*pinned(w_qkv, w_out, dec_cols), after)


def project_kernel(own_ref, mid_ref, far_ref, gain_ref, w_ref, packed_hbm, enc_ref, s_ref, packed, sem):
    model = gain_ref.shape[1]
    total = own_ref[...] + mid_ref[...].astype(F32) + far_ref[...].astype(F32)
    enc = total[:, :model]
    s_ref[...] = total[:, model:].astype(BF)
    enc_ref[...] = enc
    centred = enc - jnp.mean(enc, axis=1, keepdims=True)
    spread_sq = jnp.mean(centred * centred, axis=1, keepdims=True)
    normed = (centred * lax.rsqrt(spread_sq + 1e-05) * gain_ref[...]).astype(BF)
    scale = HDIM ** (-0.5) * LOG2E
    copies = []
    for pair in range(model // (2 * LANES)):
        for part in range(3):
            at = part * model + pair * 2 * LANES
            cols = dot(normed, w_ref[:, at : at + 2 * LANES], 1, 0)
            if part == 0:
                cols = cols * scale
            cols = cols.astype(BF)
            for half in range(2):
                packed[2 * pair + half, :, part * LANES : (part + 1) * LANES] = cols[:, half * LANES : (half + 1) * LANES]
        rows = pl.ds(2 * pair, 2)
        copies += started([pltpu.make_async_copy(packed.at[rows], packed_hbm.at[rows], sem.at[pair])])
    for copy in copies:
        copy.wait()


def project(own, mid, far, gain_row, w_qkv):
    model = w_qkv.shape[0]
    groups = model // LANES
    return pl.pallas_call(
        project_kernel,
        in_specs=[VMEM] * 5,
        out_specs=(HBM, VMEM, VMEM),
        out_shape=(
            shape((groups, NODE_DEV, 3 * LANES), BF),
            shape((NODE_DEV, model), F32),
            shape((NODE_DEV, LANES), BF),
        ),
        scratch_shapes=[
            pltpu.VMEM((groups, NODE_DEV, 3 * LANES), BF),
            pltpu.SemaphoreType.DMA((groups // 2,)),
        ],
        compiler_params=params(),
        name="project",
    )(own, mid, far, gain_row, w_qkv)


def side_kernel(enc_ref, s_ref, dec_ref, send_hbm, node_ref, send, sem):
    groups = send.shape[0]
    enc = enc_ref[...]
    summed = s_ref[...]
    high = enc.astype(BF)
    low = (enc - high.astype(F32)).astype(BF)
    node_ref[...] = dot(high, dec_ref[...], 1, 1)
    grad = (dot(summed, high, 0, 0) + dot(summed, low, 0, 0)).astype(BF)
    for group in range(groups):
        send[group, :NODE_DEV, :] = summed
        send[group, NODE_DEV:, :] = grad[:, group * LANES : (group + 1) * LANES]
    copy = pltpu.make_async_copy(send, send_hbm, sem)
    copy.start()
    copy.wait()


def side(enc, summed, dec_pad):
    groups = enc.shape[1] // LANES
    send_shape = (groups, NODE_DEV + LANES, LANES)
    return pl.pallas_call(
        side_kernel,
        in_specs=[VMEM] * 3,
        out_specs=(HBM, VMEM),
        out_shape=(shape(send_shape, BF), shape((NODE_DEV, LANES), F32)),
        scratch_shapes=[pltpu.VMEM(send_shape, BF), pltpu.SemaphoreType.DMA],
        compiler_params=params(),
        name="side",
    )(enc, summed, dec_pad)


def limits(win, reach, start, first_node, node_total):
    column = lax.broadcasted_iota(jnp.int32, (1, QB), 1) + reach
    bottom = jnp.maximum(column - win[0:1], reach - start - first_node)
    top = jnp.minimum(column + win[1:2], reach - start - first_node + node_total - 1)
    return jnp.concatenate([bottom, bottom], axis=1), jnp.concatenate([top, top], axis=1)


def masked(scores, at, reach, bottom, top):
    key = lax.broadcasted_iota(jnp.int32, scores.shape, 0) + at
    if at + KC - 1 <= reach:
        keep = key >= bottom
    elif at >= reach + QB - 1:
        keep = key <= top
    else:
        keep = (key >= bottom) & (key <= top)
    return jnp.where(keep, scores, NEG)


def fold(scores):
    return jnp.max(scores.reshape(KC // 8, 8, 2 * QB), axis=0)


def near_kernel(reach, qkv_ref, win_ref, acc_ref, top_ref, q_ref, k_ref, v_ref, vt_ref, score_ref, prob_ref):
    groups = qkv_ref.shape[0]
    band_rows = groups * NODE_DEV
    first_node = lax.axis_index("band") * band_rows
    node_total = lax.axis_size("band") * band_rows
    lane = lax.broadcasted_iota(jnp.int32, (NODE_DEV, LANES), 1)
    zero = jnp.zeros((NODE_DEV, LANES), BF)
    for group in range(groups):
        rows = pl.ds((group ^ 1) * NODE_DEV, NODE_DEV)
        queries = qkv_ref[group, :, :LANES]
        q_ref[0, rows, :] = jnp.where(lane < HDIM, queries, zero)
        q_ref[1, rows, :] = jnp.where(lane >= HDIM, queries, zero)
        k_ref[rows, :] = qkv_ref[group, :, LANES : 2 * LANES]
        v_ref[rows, :] = qkv_ref[group, :, 2 * LANES :].astype(F32)
    vt = v_ref[...].T.astype(BF)
    for head in range(2):
        vt_ref[head, :HDIM, :] = vt[head * HDIM : (head + 1) * HDIM]
        vt_ref[head, HDIM:, :] = jnp.ones((16, band_rows), BF)
    for block in range(band_rows // QB):
        start = block * QB
        both = jnp.concatenate([q_ref[0, start : start + QB, :], q_ref[1, start : start + QB, :]], axis=0)
        bottom, top = limits(win_ref[:, start : start + QB], reach, start, first_node, node_total)
        first = max(0, reach - start)
        last = min(QB + 2 * reach, band_rows + reach - start)
        largest = jnp.full((8, 2 * QB), NEG, F32)
        for at in range(first, last, KC):
            key = start + at - reach
            scores = masked(dot(k_ref[key : key + KC, :], both, 1, 1), at, reach, bottom, top)
            score_ref[at - first : at - first + KC, :] = scores
            largest = jnp.maximum(largest, fold(scores))
        largest = jnp.max(largest, axis=0, keepdims=True)
        top_ref[block] = largest
        for at in range(0, last - first, KC):
            prob_ref[at : at + KC, :] = jnp.exp2(score_ref[at : at + KC, :] - largest).astype(BF)
        key = start + first - reach
        for head in range(2):
            acc_ref[block, head] = dot(
                vt_ref[head, :, key : key + last - first],
                prob_ref[: last - first, head * QB : (head + 1) * QB],
                1,
                0,
            )


def near(qkv, win, reach):
    groups = qkv.shape[0]
    band_rows = groups * NODE_DEV
    blocks = band_rows // QB
    keys = min(QB + 2 * reach, band_rows)
    return pl.pallas_call(
        functools.partial(near_kernel, reach),
        in_specs=[VMEM] * 2,
        out_specs=(VMEM,) * 3,
        out_shape=(
            shape((blocks, 2, HDIM + 16, QB), F32),
            shape((blocks, 1, 2 * QB), F32),
            shape((2, band_rows, LANES), BF),
        ),
        scratch_shapes=[
            pltpu.VMEM((band_rows, LANES), BF),
            pltpu.VMEM((band_rows, LANES), F32),
            pltpu.VMEM((2, HDIM + 16, band_rows), BF),
            pltpu.VMEM((keys, 2 * QB), F32),
            pltpu.VMEM((keys, 2 * QB), BF),
        ],
        compiler_params=params(),
        cost_estimate=pl.CostEstimate(flops=6_000_000_000, bytes_accessed=4_000_000, transcendentals=3_000_000),
        name="near",
    )(qkv, win)


def far_kernel(reach, q_ref, acc_ref, top_ref, low_ref, high_ref, win_ref, extra_ref, mix_ref,
               node_hbm, grad_ref, k_ref, v_ref, vt_ref, score_ref, prob_ref, out_ref, node_ref, sem):
    groups = extra_ref.shape[0]
    band_rows = groups * NODE_DEV
    first_node = lax.axis_index("band") * band_rows
    node_total = lax.axis_size("band") * band_rows
    for side_at, half in enumerate((low_ref, high_ref)):
        for group in range(groups // 2):
            rows = pl.ds(side_at * reach + (group ^ 1) * NODE_DEV, NODE_DEV)
            k_ref[rows, :] = half[group, :, :LANES]
            v_ref[rows, :] = half[group, :, LANES:].astype(F32)
    vt = v_ref[...].T.astype(BF)
    for head in range(2):
        vt_ref[head, :HDIM, :] = vt[head * HDIM : (head + 1) * HDIM]
        vt_ref[head, HDIM:, :] = jnp.ones((16, 2 * reach), BF)
    for block in range(band_rows // QB):
        start = block * QB
        both = jnp.concatenate([q_ref[0, start : start + QB, :], q_ref[1, start : start + QB, :]], axis=0)
        bottom, top = limits(win_ref[:, start : start + QB], reach, start, first_node, node_total)
        low_to = max(0, reach - start)
        high_from = min(QB + 2 * reach, band_rows + reach - start)
        pieces = [(at, start + at) for at in range(0, low_to, KC)]
        pieces += [(at, start + at - band_rows) for at in range(high_from, QB + 2 * reach, KC)]
        before = top_ref[block]
        largest = jnp.full((8, 2 * QB), NEG, F32)
        for row, (at, key) in enumerate(pieces):
            scores = masked(dot(k_ref[key : key + KC, :], both, 1, 1), at, reach, bottom, top)
            score_ref[row * KC : (row + 1) * KC, :] = scores
            largest = jnp.maximum(largest, fold(scores))
        largest = jnp.maximum(jnp.max(largest, axis=0, keepdims=True), before)
        decay = jnp.exp2(before - largest)
        for row in range(len(pieces)):
            prob_ref[row * KC : (row + 1) * KC, :] = jnp.exp2(score_ref[row * KC : (row + 1) * KC, :] - largest).astype(BF)
        low_rows, high_rows = low_to, QB + 2 * reach - high_from
        for head in range(2):
            cols = slice(head * QB, (head + 1) * QB)
            mixed = acc_ref[block, head] * decay[:, cols]
            if low_rows:
                mixed += dot(vt_ref[head, :, start:reach], prob_ref[:low_rows, cols], 1, 0)
            if high_rows:
                at = reach
                mixed += dot(vt_ref[head, :, at : at + high_rows], prob_ref[low_rows : low_rows + high_rows, cols], 1, 0)
            out_ref[head * HDIM : (head + 1) * HDIM, start : start + QB] = (
                mixed[:HDIM] / mixed[HDIM : HDIM + 1]
            ).astype(BF)
    attended = out_ref[...]
    node = dot(mix_ref[...], attended, 0, 0).T.astype(BF)
    for group in range(groups):
        node_ref[group] = node[(group ^ 1) * NODE_DEV : ((group ^ 1) + 1) * NODE_DEV]
    copy = pltpu.make_async_copy(node_ref, node_hbm, sem)
    copy.start()
    grad = jnp.zeros((LANES, LANES), F32)
    total = jnp.zeros((LANES, LANES), F32)
    for group in range(groups):
        at = (group ^ 1) * NODE_DEV
        grad += dot(extra_ref[group, :NODE_DEV, :], attended[:, at : at + NODE_DEV], 0, 1)
        total += extra_ref[group, NODE_DEV:, :].astype(F32)
    grad_ref[:LANES, :] = grad
    grad_ref[LANES:, :] = total
    copy.wait()


def far(queries, acc, top, low, high, win, extra, mix):
    groups = extra.shape[0]
    reach = low.shape[0] * NODE_DEV
    band_rows = groups * NODE_DEV
    return pl.pallas_call(
        functools.partial(far_kernel, reach),
        in_specs=[VMEM] * 8,
        out_specs=(HBM, VMEM),
        out_shape=(shape((groups, NODE_DEV, LANES), BF), shape((2 * LANES, LANES), F32)),
        scratch_shapes=[
            pltpu.VMEM((2 * reach, LANES), BF),
            pltpu.VMEM((2 * reach, LANES), F32),
            pltpu.VMEM((2, HDIM + 16, 2 * reach), BF),
            pltpu.VMEM((reach, 2 * QB), F32),
            pltpu.VMEM((reach, 2 * QB), BF),
            pltpu.VMEM((LANES, band_rows), BF),
            pltpu.VMEM((groups, NODE_DEV, LANES), BF),
            pltpu.SemaphoreType.DMA,
        ],
        compiler_params=params(),
        name="far",
    )(queries, acc, top, low, high, win, extra, mix)


def nodes_kernel(parts_ref, node_ref, out_ref):
    total = node_ref[...]
    for group in range(parts_ref.shape[0]):
        total += parts_ref[group].astype(F32)
    out_ref[...] = total.astype(BF)


def sum_nodes(parts, node):
    return pl.pallas_call(
        nodes_kernel,
        in_specs=[VMEM] * 2,
        out_specs=VMEM,
        out_shape=shape(node.shape, BF),
        compiler_params=params(),
        name="sum_nodes",
    )(parts, node)


def decode_kernel(far_ref, mid_ref, own_ref, dec_ref, grid_ref, pred_ref):
    channels, points = grid_ref.shape
    nodes = NODE_DEV
    rows = 4 * LANES
    table = jnp.concatenate(
        [
            far_ref[...].astype(F32),
            mid_ref[...].astype(F32),
            own_ref[...].astype(F32),
            jnp.zeros((rows - 3 * nodes, LANES), F32),
        ],
        axis=0,
    ).T.astype(BF)
    width = 512
    bases = chunk_bases()
    node_id = lax.broadcasted_iota(jnp.int32, (nodes, width), 0)
    for at in range(0, points, width):
        target = dec_ref[:, at : at + width]
        pick = [jnp.where(node_id == target - base, 1.0, 0.0) for base in bases]
        pick = jnp.concatenate(pick + [jnp.zeros((rows - 3 * nodes, width), F32)], axis=0).astype(BF)
        decoded = dot(table, pick, 1, 0)
        pred_ref[:, at : at + width] = (
            grid_ref[:, at : at + width].astype(F32) + decoded[:channels]
        ).astype(BF)


def decode(far_rows, mid_rows, own_rows, dec_row, grid_in):
    return pl.pallas_call(
        decode_kernel,
        in_specs=[VMEM] * 5,
        out_specs=VMEM,
        out_shape=shape(grid_in.shape, BF),
        compiler_params=params(),
        name="decode",
    )(far_rows, mid_rows, own_rows, dec_row, grid_in)


def gradient_kernel(parts_ref, w_out_ref, grad_ref):
    channels, model = grad_ref.shape
    mixed = jnp.zeros((LANES, model), F32)
    for group in range(parts_ref.shape[0]):
        mixed += dot(parts_ref[group, :LANES, :], w_out_ref[group * LANES : (group + 1) * LANES, :], 1, 0)
    for group in range(parts_ref.shape[0]):
        cols = slice(group * LANES, (group + 1) * LANES)
        whole = mixed[:, cols] + parts_ref[group, LANES:, :].astype(F32)
        grad_ref[:, cols] = whole[:channels]


def gradient(parts, w_out, channels):
    return pl.pallas_call(
        gradient_kernel,
        in_specs=[VMEM] * 2,
        out_specs=VMEM,
        out_shape=shape((channels, w_out.shape[0]), F32),
        compiler_params=params(),
        name="gradient",
    )(parts, w_out)


def total_devices():
    return lax.axis_size("band") * lax.axis_size("head")


def to_partner(block):
    return lax.ppermute(block, BOTH, [(i, i ^ 1) for i in range(total_devices())])


def two_over(block, sign):
    count = total_devices()
    pairs = [(i, i + sign * (2 - 4 * (i % 2))) for i in range(count)]
    return lax.ppermute(block, BOTH, [(i, j) for i, j in pairs if 0 <= j < count])


def along_band(block, shift):
    count = lax.axis_size("band")
    return lax.ppermute(block, "band", [(i, i + shift) for i in range(count) if 0 <= i + shift < count])


def swap(block):
    return lax.all_to_all(block, "head", split_axis=0, concat_axis=0, tiled=True)


def shards(
    grid_in, enc_node, dec_node, win_offsets, w_in, b_in, w_qkv, w_out, norm_gain, w_dec, cotangent
):
    channels = grid_in.shape[0]
    groups = lax.axis_size("head")
    dec_row = dec_node[None]
    far_part, mid_part, own = encode(grid_in, enc_node[None], w_in, b_in[None], cotangent, dec_row)
    weights, dec_pad, mix = load(w_qkv, w_out, w_dec.T, far_part)
    mid_in = to_partner(mid_part)
    far_in = two_over(far_part, -1)
    packed, enc, summed = project(own, mid_in, far_in, norm_gain[None], weights)
    qkv = swap(packed)
    send, node = side(enc, summed, dec_pad)
    half = groups // 2
    reach = half * NODE_DEV
    from_low = along_band(qkv[half:, :, LANES:], 1)
    from_high = along_band(qkv[:half, :, LANES:], -1)
    extra = swap(send)
    acc, top, queries = near(qkv, win_offsets, reach)
    node_parts, grad_part = far(queries, acc, top, from_low, from_high, win_offsets, extra, mix)
    table = sum_nodes(swap(node_parts), node)
    prediction = decode(two_over(table, 1), to_partner(table), table, dec_row, grid_in)
    shift = 1
    count = lax.axis_size("band")
    while shift < count:
        other = lax.ppermute(grad_part, "band", [(i, i ^ shift) for i in range(count)])
        grad_part = (grad_part.astype(F32) + other.astype(F32)).astype(BF)
        shift *= 2
    parts = swap(jnp.broadcast_to(grad_part[None], (groups,) + grad_part.shape))
    grad_dec = gradient(parts, w_out, channels).T
    return (prediction, grad_dec)


def solution(mesh):
    placed = (
        P(None, BOTH),
        P(BOTH),
        P(BOTH),
        P(None, "band"),
        P(),
        P(),
        P(),
        P(),
        P(),
        P(),
        P(None, BOTH),
    )
    return jax.shard_map(
        shards,
        mesh=mesh,
        in_specs=placed,
        out_specs=(P(None, BOTH), P()),
        check_vma=False,
    )
```

time: 150 us -> 130 us (0.87)
  local copies, waits for them, and re-layouts: 22.5 us -> 9.82 us
  starting transfers between devices: 60.6 us -> 48.1 us
  Pallas kernels: 20.3 us -> 25.3 us
    unnamed x50 -> x30, local copies, waits for them, and re-layouts: 20.8 us -> 8.07 us
    ppermute x6, starting transfers between devices: 27.7 us -> 17.5 us  [the longest x2 9.16 us: two_over(): lax.ppermute(block, BOTH, [(i, j) for i, j in pairs if 0 <= j < count])]
    all_to_all x4, waiting for transfers between devices: 14.8 us -> 24.5 us  [swap(): lax.all_to_all(block, 'head', split_axis=0, concat_axis=0, tiled=True)]
    ppermute x6, waiting for transfers between devices: 17.5 us -> 8.91 us  [the longest x2 6.99 us: two_over(): lax.ppermute(block, BOTH, [(i, j) for i, j in pairs if 0 <= j < count])]
    pallas_call x7 -> x9, Pallas kernels: 20.3 us -> 25.3 us  [the longest x1 6.71 us: encode(): pl.pallas_call(encode_kernel, in_specs=[HBM] * 6, out_specs=(VMEM,) * 3,...]
    all_to_all x4, starting transfers between devices: 18 us -> 16.4 us  [swap(): lax.all_to_all(block, 'head', split_axis=0, concat_axis=0, tiled=True)]
  transfers between devices with their start and end apart: 15 -> 15, of which waited for: 12 -> 10; matrix products, arithmetic and copies ran while one was open for 2% -> 1% of each run, Pallas kernels for 1% -> 8%
where the time goes in v2:
time: 130 us; the launch traced here: 128 us
  starting transfers between devices  48.1 us (37%)
  waiting for transfers between devices  43.8 us (34%)
  Pallas kernels  25.3 us (19%)
  local copies, waits for them, and re-layouts  9.82 us (8%)
    all_to_all x4, waiting for transfers between devices, swap(): lax.all_to_all(block, 'head', split_axis=0, concat_axis=0, tiled=True)  24.5 us
    all_to_all x4, starting transfers between devices, swap(): lax.all_to_all(block, 'head', split_axis=0, concat_axis=0, tiled=True)  16.4 us
    ppermute x5, starting transfers between devices, shards(): lax.ppermute(grad_part, 'band', [(i, i ^ shift) for i in range(count)])  14.1 us
    ppermute x5, waiting for transfers between devices, shards(): lax.ppermute(grad_part, 'band', [(i, i ^ shift) for i in range(count)])  10.4 us
    ppermute x2, starting transfers between devices, two_over(): lax.ppermute(block, BOTH, [(i, j) for i, j in pairs if 0 <= j < count])  9.16 us
    unnamed x30, local copies, waits for them, and re-layouts  8.07 us
    ppermute x2, waiting for transfers between devices, two_over(): lax.ppermute(block, BOTH, [(i, j) for i, j in pairs if 0 <= j < count])  6.99 us
    pallas_call x1, Pallas kernels, encode(): pl.pallas_call(encode_kernel, in_specs=[HBM] * 6, out_specs=(VMEM,) * 3,...  6.71 us
  transfers between devices with their start and end apart: 15, of which 10 were waited for; matrix products, arithmetic and copies ran while one was open for 1% of the time, Pallas kernels for 8%

profile of v2, /device:TPU:32, one launch (start us, length us, event | category | flops | bytes accessed | tf_op | source)
XLA Modules:
  0.0 128.0 jit_solution(17648839003026078469)
XLA Ops:
  0.6 6.7 %encode.1 = (bf16[160,1152]{1,0:T(8,128)(2,1)S(1)}, bf16[160,1152]{1,0:T(8,128)(2,1)S(1)}, f32[160,1152]{1,0:T(8,128)S(1)}) custom-call(bf16[110,2048]{1,0:T(8,128)(2,1)} %grid_ref.1, s32[1,2048]{1,0:T(1,128)} %bitcast.11, bf16[110,1024]{1,0:T(8,128)(2,1)} %w_hbm.2, f32[1,1024]{1,0:T(1,128)} %bitcast.12, bf16[110,2048]{1,0:T(8,128)(2,1)} %cot_hbm.1, ...), custom_call_target="tpu_custom_call" | custom-call | tf_op jit(solution)/shard_map/encode/pallas_call | solution.py:107
  7.4 1.6 %collective-permute-start = (bf16[160,1152]{1,0:T(8,128)(2,1)S(1)}, bf16[160,1152]{1,0:T(8,128)(2,1)S(1)}, u32[]{:S(2)}, u32[]{:S(2)}) collective-permute-start(bf16[160,1152]{1,0:T(8,128)(2,1)S(1)} %get-tuple-element.19), channel_id=1, source_target_pairs={{0,1},{1,0},{2,3},{3,2},{4,5},{5,4},{6,7},{7,6},{8,9},{9,8},{10,11... | collective-permute-start | bytes 1105928 | tf_op jit(solution)/shard_map/ppermute | solution.py:499
  8.9 5.8 %collective-permute-start.1 = (bf16[160,1152]{1,0:T(8,128)(2,1)S(1)}, bf16[160,1152]{1,0:T(8,128)(2,1)S(1)}, u32[]{:S(2)}, u32[]{:S(2)}) collective-permute-start(bf16[160,1152]{1,0:T(8,128)(2,1)S(1)} %get-tuple-element.20.after_ref), channel_id=1, source_target_pairs={{1,3},{2,0},{3,5},{4,2},{5,7},{6,4},{7,9},{8,6},{9,11},{10,8},{11,... | collective-permute-start | bytes 1105928 | tf_op jit(solution)/shard_map/ppermute | solution.py:505
  14.7 3.1 %load.1 = (bf16[1024,3072]{1,0:T(8,128)(2,1)S(1)}, bf16[128,1024]{1,0:T(8,128)(2,1)S(1)}, bf16[128,128]{1,0:T(8,128)(2,1)S(1)}) custom-call(bf16[1024,3072]{1,0:T(8,128)(2,1)} %w_hbm.3, bf16[1024,1024]{1,0:T(8,128)(2,1)} %w_out_ref.1, bf16[110,1024]{1,0:T(8,128)(2,1)} %bitcast.10, bf16[160,1152]{1,0:T(8,128)(2,1)S(1)} %get-tuple-element.20.after_ref), custom_call_target="tpu_custom_call" | custom-call | flops 33554432 | bytes 6291456 | tf_op jit(solution)/shard_map/load/pallas_call | solution.py:145
  18.4 2.5 %collective-permute-done.1.far_ref = bf16[160,1152]{1,0:T(8,128)(2,1)S(1)} collective-permute-done((bf16[160,1152]{1,0:T(8,128)(2,1)S(1)}, bf16[160,1152]{1,0:T(8,128)(2,1)S(1)}, u32[]{:S(2)}, u32[]{:S(2)}) %collective-permute-start.1) | collective-permute-done | bytes 368672 | tf_op jit(solution)/shard_map/ppermute | solution.py:505
  20.9 2.2 %project.1 = (bf16[8,160,384]{2,1,0:T(8,128)(2,1)}, f32[160,1024]{1,0:T(8,128)S(1)}, bf16[160,128]{1,0:T(8,128)(2,1)S(1)}) custom-call(f32[160,1152]{1,0:T(8,128)S(1)} %get-tuple-element.18.own_ref, bf16[160,1152]{1,0:T(8,128)(2,1)S(1)} %collective-permute-done.mid_ref, bf16[160,1152]{1,0:T(8,128)(2,1)S(1)} %collective-permute-done.1.far_ref, ...), custom_call_target="tpu_custom_call" | custom-call | tf_op jit(solution)/shard_map/project/pallas_call | solution.py:190
  23.1 4.5 %all-to-all-start = ((bf16[8,160,384]{2,1,0:T(8,128)(2,1)}), bf16[8,160,384]{2,1,0:T(8,128)(2,1)S(1)}, u32[]{:S(2)}, u32[]{:S(2)}) async-start(bf16[8,160,384]{2,1,0:T(8,128)(2,1)} %get-tuple-element.22), calls=%async_computation | async-start | bytes 1966080 | tf_op jit(solution)/shard_map/all_to_all | solution.py:514
  27.6 1.3 side.1
  28.8 14.0 %all-to-all-done.qkv_ref = bf16[8,160,384]{2,1,0:T(8,128)(2,1)S(1)} async-done(((bf16[8,160,384]{2,1,0:T(8,128)(2,1)}), bf16[8,160,384]{2,1,0:T(8,128)(2,1)S(1)}, u32[]{:S(2)}, u32[]{:S(2)}) %all-to-all-start) | async-done | bytes 983072 | tf_op jit(solution)/shard_map/all_to_all | solution.py:514
  42.9 3.7 %all-to-all-start.1 = ((bf16[8,288,128]{2,1,0:T(8,128)(2,1)}), bf16[8,288,128]{2,1,0:T(8,128)(2,1)S(1)}, u32[]{:S(2)}, u32[]{:S(2)}) async-start(bf16[8,288,128]{2,1,0:T(8,128)(2,1)} %get-tuple-element.29), calls=%async_computation.1 | async-start | bytes 1179648 | tf_op jit(solution)/shard_map/all_to_all | solution.py:514
  47.5 2.3 %collective-permute-start.3 = (bf16[4,160,256]{2,1,0:T(8,128)(2,1)}, bf16[4,160,256]{2,1,0:T(8,128)(2,1)S(1)}, u32[]{:S(2)}, u32[]{:S(2)}) collective-permute-start(bf16[4,160,256]{2,1,0:T(8,128)(2,1)} %get-tuple-element.34), channel_id=1, source_target_pairs={{8,0},{16,8},{24,16},{32,24},{40,32},{48,40},{56,48},{64,56},{72,6... | collective-permute-start | bytes 983048 | tf_op jit(solution)/shard_map/ppermute | solution.py:510
  49.8 2.4 %collective-permute-start.2 = (bf16[4,160,256]{2,1,0:T(8,128)(2,1)}, bf16[4,160,256]{2,1,0:T(8,128)(2,1)}, u32[]{:S(2)}, u32[]{:S(2)}) collective-permute-start(bf16[4,160,256]{2,1,0:T(8,128)(2,1)} %get-tuple-element.35), channel_id=1, source_target_pairs={{0,8},{8,16},{16,24},{24,32},{32,40},{40,48},{48,56},{56,64},{64,7... | collective-permute-start | bytes 983048 | tf_op jit(solution)/shard_map/ppermute | solution.py:510
  52.3 4.9 %near.1 = (f32[5,2,80,256]{3,2,1,0:T(8,128)S(1)}, f32[5,1,512]{2,1,0:T(1,128)S(1)}, bf16[2,1280,128]{2,1,0:T(8,128)(2,1)S(1)}) custom-call(bf16[8,160,384]{2,1,0:T(8,128)(2,1)S(1)} %all-to-all-done.qkv_ref, s32[2,1280]{1,0:T(2,128)S(1)} %copy-done.10), custom_call_target="tpu_custom_call" | custom-call | flops 6000000000 | bytes 4000000 | tf_op jit(solution)/shard_map/near/pallas_call | solution.py:309
  59.5 2.8 %all-to-all-done.1.extra_ref = bf16[8,288,128]{2,1,0:T(8,128)(2,1)S(1)} async-done(((bf16[8,288,128]{2,1,0:T(8,128)(2,1)}), bf16[8,288,128]{2,1,0:T(8,128)(2,1)S(1)}, u32[]{:S(2)}, u32[]{:S(2)}) %all-to-all-start.1) | async-done | bytes 589856 | tf_op jit(solution)/shard_map/all_to_all | solution.py:514
  62.4 1.1 copy-done.3
  63.5 1.1 copy-done.5
  66.8 4.3 %far.1 = (bf16[8,160,128]{2,1,0:T(8,128)(2,1)S(1)}, f32[256,128]{1,0:T(8,128)S(1)}) custom-call(bf16[2,1280,128]{2,1,0:T(8,128)(2,1)S(1)} %copy-done.5, f32[5,2,80,256]{3,2,1,0:T(8,128)S(1)} %copy-done.3, f32[5,1,512]{2,1,0:T(1,128)S(1)} %copy-done.13, bf16[4,160,256]{2,1,0:T(8,128)(2,1)} %collective-permute-done.2.low_ref, ...), custom_call_target="tpu_custom_call" | custom-call | tf_op jit(solution)/shard_map/far/pallas_call | solution.py:397
  72.7 2.9 %collective-permute-start.7 = (bf16[256,128]{1,0:T(8,128)(2,1)S(1)}, bf16[256,128]{1,0:T(8,128)(2,1)S(1)}, u32[]{:S(2)}, u32[]{:S(2)}) collective-permute-start(bf16[256,128]{1,0:T(8,128)(2,1)S(1)} %add_convert_fusion.4), channel_id=1, source_target_pairs={{0,16},{8,24},{16,0},{24,8},{32,48},{40,56},{48,32},{56,40},{64,80... | collective-permute-start | bytes 196616 | tf_op jit(solution)/shard_map/ppermute | solution.py:542
  75.7 3.0 %collective-permute-done.7 = bf16[256,128]{1,0:T(8,128)(2,1)S(1)} collective-permute-done((bf16[256,128]{1,0:T(8,128)(2,1)S(1)}, bf16[256,128]{1,0:T(8,128)(2,1)S(1)}, u32[]{:S(2)}, u32[]{:S(2)}) %collective-permute-start.7) | collective-permute-done | bytes 65568 | tf_op jit(solution)/shard_map/ppermute | solution.py:542
  78.9 4.2 %collective-permute-done.8 = bf16[256,128]{1,0:T(8,128)(2,1)S(1)} collective-permute-done((bf16[256,128]{1,0:T(8,128)(2,1)S(1)}, bf16[256,128]{1,0:T(8,128)(2,1)S(1)}, u32[]{:S(2)}, u32[]{:S(2)}) %collective-permute-start.8) | collective-permute-done | bytes 65568 | tf_op jit(solution)/shard_map/ppermute | solution.py:542
  83.1 5.2 %collective-permute-start.9 = (bf16[256,128]{1,0:T(8,128)(2,1)S(1)}, bf16[256,128]{1,0:T(8,128)(2,1)S(1)}, u32[]{:S(2)}, u32[]{:S(2)}) collective-permute-start(bf16[256,128]{1,0:T(8,128)(2,1)S(1)} %add_convert_fusion.2), channel_id=1, source_target_pairs={{0,64},{8,72},{16,80},{24,88},{32,96},{40,104},{48,112},{56,120},{... | collective-permute-start | bytes 196616 | tf_op jit(solution)/shard_map/ppermute | solution.py:542
  88.3 2.2 %collective-permute-done.9 = bf16[256,128]{1,0:T(8,128)(2,1)S(1)} collective-permute-done((bf16[256,128]{1,0:T(8,128)(2,1)S(1)}, bf16[256,128]{1,0:T(8,128)(2,1)S(1)}, u32[]{:S(2)}, u32[]{:S(2)}) %collective-permute-start.9) | collective-permute-done | bytes 65568 | tf_op jit(solution)/shard_map/ppermute | solution.py:542
  90.6 5.2 %collective-permute-start.10 = (bf16[256,128]{1,0:T(8,128)(2,1)S(1)}, bf16[256,128]{1,0:T(8,128)(2,1)S(1)}, u32[]{:S(2)}, u32[]{:S(2)}) collective-permute-start(bf16[256,128]{1,0:T(8,128)(2,1)S(1)} %add_convert_fusion.1), channel_id=1, source_target_pairs={{0,128},{8,136},{16,144},{24,152},{32,160},{40,168},{48,176},{56,1... | collective-permute-start | bytes 196616 | tf_op jit(solution)/shard_map/ppermute | solution.py:542
  95.8 4.7 %all-to-all-start.2 = ((bf16[8,160,128]{2,1,0:T(8,128)(2,1)}), bf16[8,160,128]{2,1,0:T(8,128)(2,1)S(1)}, u32[]{:S(2)}, u32[]{:S(2)}) async-start(bf16[8,160,128]{2,1,0:T(8,128)(2,1)} %copy-done.6), calls=%async_computation.2 | async-start | bytes 655360 | tf_op jit(solution)/shard_map/all_to_all | solution.py:514
  100.5 7.6 %all-to-all-done.2.parts_ref = bf16[8,160,128]{2,1,0:T(8,128)(2,1)S(1)} async-done(((bf16[8,160,128]{2,1,0:T(8,128)(2,1)}), bf16[8,160,128]{2,1,0:T(8,128)(2,1)S(1)}, u32[]{:S(2)}, u32[]{:S(2)}) %all-to-all-start.2) | async-done | bytes 327712 | tf_op jit(solution)/shard_map/all_to_all | solution.py:514
  109.0 3.5 %all-to-all-start.3 = ((bf16[8,256,128]{2,1,0:T(8,128)(2,1)}), bf16[8,256,128]{2,1,0:T(8,128)(2,1)S(1)}, u32[]{:S(2)}, u32[]{:S(2)}) async-start(bf16[8,256,128]{2,1,0:T(8,128)(2,1)} %broadcast_in_dim.22), calls=%async_computation.3 | async-start | bytes 1048576 | tf_op jit(solution)/shard_map/all_to_all | solution.py:514
  112.6 2.0 %collective-permute-start.5 = (bf16[160,128]{1,0:T(8,128)(2,1)S(1)}, bf16[160,128]{1,0:T(8,128)(2,1)S(1)}, u32[]{:S(2)}, u32[]{:S(2)}) collective-permute-start(bf16[160,128]{1,0:T(8,128)(2,1)S(1)} %sum_nodes.1.own_ref), channel_id=1, source_target_pairs={{0,1},{1,0},{2,3},{3,2},{4,5},{5,4},{6,7},{7,6},{8,9},{9,8},{10,11... | collective-permute-start | bytes 122888 | tf_op jit(solution)/shard_map/ppermute | solution.py:499
  114.6 3.4 %collective-permute-start.4 = (bf16[160,128]{1,0:T(8,128)(2,1)S(1)}, bf16[160,128]{1,0:T(8,128)(2,1)S(1)}, u32[]{:S(2)}, u32[]{:S(2)}) collective-permute-start(bf16[160,128]{1,0:T(8,128)(2,1)S(1)} %sum_nodes.1.own_ref), channel_id=1, source_target_pairs={{0,2},{2,4},{3,1},{4,6},{5,3},{6,8},{7,5},{8,10},{9,7},{10,12},{11... | collective-permute-start | bytes 122888 | tf_op jit(solution)/shard_map/ppermute | solution.py:505
  117.9 1.9 %collective-permute-done.5.mid_ref = bf16[160,128]{1,0:T(8,128)(2,1)S(1)} collective-permute-done((bf16[160,128]{1,0:T(8,128)(2,1)S(1)}, bf16[160,128]{1,0:T(8,128)(2,1)S(1)}, u32[]{:S(2)}, u32[]{:S(2)}) %collective-permute-start.5) | collective-permute-done | bytes 40992 | tf_op jit(solution)/shard_map/ppermute | solution.py:499
  119.9 4.5 %collective-permute-done.4.far_ref = bf16[160,128]{1,0:T(8,128)(2,1)S(1)} collective-permute-done((bf16[160,128]{1,0:T(8,128)(2,1)S(1)}, bf16[160,128]{1,0:T(8,128)(2,1)S(1)}, u32[]{:S(2)}, u32[]{:S(2)}) %collective-permute-start.4) | collective-permute-done | bytes 40992 | tf_op jit(solution)/shard_map/ppermute | solution.py:505
  125.1 1.4 %decode.1 = bf16[110,2048]{1,0:T(8,128)(2,1)} custom-call(bf16[160,128]{1,0:T(8,128)(2,1)S(1)} %collective-permute-done.4.far_ref, bf16[160,128]{1,0:T(8,128)(2,1)S(1)} %collective-permute-done.5.mid_ref, bf16[160,128]{1,0:T(8,128)(2,1)S(1)} %sum_nodes.1.own_ref, s32[1,2048]{1,0:T(1,128)S(1)} %bitcast.7, bf16[110,2048]{1,0:T(8,128)(2,1)S(1)} %copy-done.1), custom_call_target="tpu_custom_call" | custom-call | tf_op jit(solution)/shard_map/decode/pallas_call | solution.py:462
  126.5 1.5 %gradient.1 = f32[110,1024]{1,0:T(8,128)} custom-call(bf16[8,256,128]{2,1,0:T(8,128)(2,1)S(1)} %all-to-all-done.3.parts_ref, bf16[1024,1024]{1,0:T(8,128)(2,1)S(1)} %copy-done), custom_call_target="tpu_custom_call" | custom-call | tf_op jit(solution)/shard_map/gradient/pallas_call | solution.py:484
  (44 shorter events, 9.6 us)
Async XLA Ops:
  0.6 20.2 %copy-start.14 = (f32[1024]{0:T(1024)S(1)}, f32[1024]{0:T(1024)}, u32[]{:S(2)}) copy-start(f32[1024]{0:T(1024)} %param.19) | copy-start | bytes 12292
  7.4 11.0 %collective-permute-start = (bf16[160,1152]{1,0:T(8,128)(2,1)S(1)}, bf16[160,1152]{1,0:T(8,128)(2,1)S(1)}, u32[]{:S(2)}, u32[]{:S(2)}) collective-permute-start(bf16[160,1152]{1,0:T(8,128)(2,1)S(1)} %get-tuple-element.19), channel_id=1, source_target_pairs={{0,1},{1,0},{2,3},{3,2},{4,5},{5,4},{6,7},{7,6},{8,9},{9,8},{10,11... | collective-permute-start | bytes 1105928 | tf_op jit(solution)/shard_map/ppermute | solution.py:499
  8.9 11.9 %collective-permute-start.1 = (bf16[160,1152]{1,0:T(8,128)(2,1)S(1)}, bf16[160,1152]{1,0:T(8,128)(2,1)S(1)}, u32[]{:S(2)}, u32[]{:S(2)}) collective-permute-start(bf16[160,1152]{1,0:T(8,128)(2,1)S(1)} %get-tuple-element.20.after_ref), channel_id=1, source_target_pairs={{1,3},{2,0},{3,5},{4,2},{5,7},{6,4},{7,9},{8,6},{9,11},{10,8},{11,... | collective-permute-start | bytes 1105928 | tf_op jit(solution)/shard_map/ppermute | solution.py:505
  17.8 0.6 copy-start.7
  20.9 31.4 %copy-start.10 = (s32[2,1280]{1,0:T(2,128)S(1)}, s32[2,1280]{1,0:T(2,128)}, u32[]{:S(2)}) copy-start(s32[2,1280]{1,0:T(2,128)} %win_ref.3) | copy-start | bytes 30724
  23.1 19.8 %all-to-all-start = ((bf16[8,160,384]{2,1,0:T(8,128)(2,1)}), bf16[8,160,384]{2,1,0:T(8,128)(2,1)S(1)}, u32[]{:S(2)}, u32[]{:S(2)}) async-start(bf16[8,160,384]{2,1,0:T(8,128)(2,1)} %get-tuple-element.22), calls=%async_computation | async-start | bytes 1966080 | tf_op jit(solution)/shard_map/all_to_all | solution.py:514
  42.9 19.5 %all-to-all-start.1 = ((bf16[8,288,128]{2,1,0:T(8,128)(2,1)}), bf16[8,288,128]{2,1,0:T(8,128)(2,1)S(1)}, u32[]{:S(2)}, u32[]{:S(2)}) async-start(bf16[8,288,128]{2,1,0:T(8,128)(2,1)} %get-tuple-element.29), calls=%async_computation.1 | async-start | bytes 1179648 | tf_op jit(solution)/shard_map/all_to_all | solution.py:514
  47.5 14.9 %collective-permute-start.3 = (bf16[4,160,256]{2,1,0:T(8,128)(2,1)}, bf16[4,160,256]{2,1,0:T(8,128)(2,1)S(1)}, u32[]{:S(2)}, u32[]{:S(2)}) collective-permute-start(bf16[4,160,256]{2,1,0:T(8,128)(2,1)} %get-tuple-element.34), channel_id=1, source_target_pairs={{8,0},{16,8},{24,16},{32,24},{40,32},{48,40},{56,48},{64,56},{72,6... | collective-permute-start | bytes 983048 | tf_op jit(solution)/shard_map/ppermute | solution.py:510
  49.8 12.5 %collective-permute-start.2 = (bf16[4,160,256]{2,1,0:T(8,128)(2,1)}, bf16[4,160,256]{2,1,0:T(8,128)(2,1)}, u32[]{:S(2)}, u32[]{:S(2)}) collective-permute-start(bf16[4,160,256]{2,1,0:T(8,128)(2,1)} %get-tuple-element.35), channel_id=1, source_target_pairs={{0,8},{8,16},{16,24},{24,32},{32,40},{40,48},{48,56},{56,64},{64,7... | collective-permute-start | bytes 983048 | tf_op jit(solution)/shard_map/ppermute | solution.py:510
  57.1 0.9 copy-start.2
  58.1 0.9 copy-start.4
  58.9 0.6 copy-start.12
  59.5 64.9 %copy-start.1 = (bf16[110,2048]{1,0:T(8,128)(2,1)S(1)}, bf16[110,2048]{1,0:T(8,128)(2,1)}, u32[]{:S(2)}) copy-start(bf16[110,2048]{1,0:T(8,128)(2,1)} %grid_ref.1) | copy-start | bytes 1351684
  59.5 67.0 %copy-start = (bf16[1024,1024]{1,0:T(8,128)(2,1)S(1)}, bf16[1024,1024]{1,0:T(8,128)(2,1)}, u32[]{:S(2)}) copy-start(bf16[1024,1024]{1,0:T(8,128)(2,1)} %w_out_ref.1) | copy-start | bytes 6291460
  62.4 1.1 copy-start.3
  63.5 1.1 copy-start.5
  64.6 0.8 copy-start.8
  65.4 0.7 copy-start.11
  66.1 0.7 copy-start.13
  71.1 24.7 %copy-start.6 = (bf16[8,160,128]{2,1,0:T(8,128)(2,1)}, bf16[8,160,128]{2,1,0:T(8,128)(2,1)S(1)}, u32[]{:S(2)}) copy-start(bf16[8,160,128]{2,1,0:T(8,128)(2,1)S(1)} %get-tuple-element.31) | copy-start | bytes 983044
  71.1 1.6 %collective-permute-start.6 = (f32[256,128]{1,0:T(8,128)S(1)}, f32[256,128]{1,0:T(8,128)S(1)}, u32[]{:S(2)}, u32[]{:S(2)}) collective-permute-start(f32[256,128]{1,0:T(8,128)S(1)} %get-tuple-element.33), channel_id=1, source_target_pairs={{0,8},{8,0},{16,24},{24,16},{32,40},{40,32},{48,56},{56,48},{64,72... | collective-permute-start | bytes 393224 | tf_op jit(solution)/shard_map/ppermute | solution.py:542
  72.7 5.9 %collective-permute-start.7 = (bf16[256,128]{1,0:T(8,128)(2,1)S(1)}, bf16[256,128]{1,0:T(8,128)(2,1)S(1)}, u32[]{:S(2)}, u32[]{:S(2)}) collective-permute-start(bf16[256,128]{1,0:T(8,128)(2,1)S(1)} %add_convert_fusion.4), channel_id=1, source_target_pairs={{0,16},{8,24},{16,0},{24,8},{32,48},{40,56},{48,32},{56,40},{64,80... | collective-permute-start | bytes 196616 | tf_op jit(solution)/shard_map/ppermute | solution.py:542
  78.7 4.4 %collective-permute-start.8 = (bf16[256,128]{1,0:T(8,128)(2,1)S(1)}, bf16[256,128]{1,0:T(8,128)(2,1)S(1)}, u32[]{:S(2)}, u32[]{:S(2)}) collective-permute-start(bf16[256,128]{1,0:T(8,128)(2,1)S(1)} %add_convert_fusion.3), channel_id=1, source_target_pairs={{0,32},{8,40},{16,48},{24,56},{32,0},{40,8},{48,16},{56,24},{64,96... | collective-permute-start | bytes 196616 | tf_op jit(solution)/shard_map/ppermute | solution.py:542
  83.1 7.5 %collective-permute-start.9 = (bf16[256,128]{1,0:T(8,128)(2,1)S(1)}, bf16[256,128]{1,0:T(8,128)(2,1)S(1)}, u32[]{:S(2)}, u32[]{:S(2)}) collective-permute-start(bf16[256,128]{1,0:T(8,128)(2,1)S(1)} %add_convert_fusion.2), channel_id=1, source_target_pairs={{0,64},{8,72},{16,80},{24,88},{32,96},{40,104},{48,112},{56,120},{... | collective-permute-start | bytes 196616 | tf_op jit(solution)/shard_map/ppermute | solution.py:542
  90.6 9.9 %collective-permute-start.10 = (bf16[256,128]{1,0:T(8,128)(2,1)S(1)}, bf16[256,128]{1,0:T(8,128)(2,1)S(1)}, u32[]{:S(2)}, u32[]{:S(2)}) collective-permute-start(bf16[256,128]{1,0:T(8,128)(2,1)S(1)} %add_convert_fusion.1), channel_id=1, source_target_pairs={{0,128},{8,136},{16,144},{24,152},{32,160},{40,168},{48,176},{56,1... | collective-permute-start | bytes 196616 | tf_op jit(solution)/shard_map/ppermute | solution.py:542
  95.8 12.4 %all-to-all-start.2 = ((bf16[8,160,128]{2,1,0:T(8,128)(2,1)}), bf16[8,160,128]{2,1,0:T(8,128)(2,1)S(1)}, u32[]{:S(2)}, u32[]{:S(2)}) async-start(bf16[8,160,128]{2,1,0:T(8,128)(2,1)} %copy-done.6), calls=%async_computation.2 | async-start | bytes 655360 | tf_op jit(solution)/shard_map/all_to_all | solution.py:514
  109.0 17.5 %all-to-all-start.3 = ((bf16[8,256,128]{2,1,0:T(8,128)(2,1)}), bf16[8,256,128]{2,1,0:T(8,128)(2,1)S(1)}, u32[]{:S(2)}, u32[]{:S(2)}) async-start(bf16[8,256,128]{2,1,0:T(8,128)(2,1)} %broadcast_in_dim.22), calls=%async_computation.3 | async-start | bytes 1048576 | tf_op jit(solution)/shard_map/all_to_all | solution.py:514
  112.6 7.3 %collective-permute-start.5 = (bf16[160,128]{1,0:T(8,128)(2,1)S(1)}, bf16[160,128]{1,0:T(8,128)(2,1)S(1)}, u32[]{:S(2)}, u32[]{:S(2)}) collective-permute-start(bf16[160,128]{1,0:T(8,128)(2,1)S(1)} %sum_nodes.1.own_ref), channel_id=1, source_target_pairs={{0,1},{1,0},{2,3},{3,2},{4,5},{5,4},{6,7},{7,6},{8,9},{9,8},{10,11... | collective-permute-start | bytes 122888 | tf_op jit(solution)/shard_map/ppermute | solution.py:499
  114.6 9.8 %collective-permute-start.4 = (bf16[160,128]{1,0:T(8,128)(2,1)S(1)}, bf16[160,128]{1,0:T(8,128)(2,1)S(1)}, u32[]{:S(2)}, u32[]{:S(2)}) collective-permute-start(bf16[160,128]{1,0:T(8,128)(2,1)S(1)} %sum_nodes.1.own_ref), channel_id=1, source_target_pairs={{0,2},{2,4},{3,1},{4,6},{5,3},{6,8},{7,5},{8,10},{9,7},{10,12},{11... | collective-permute-start | bytes 122888 | tf_op jit(solution)/shard_map/ppermute | solution.py:505
  124.4 0.7 copy-start.9

commit v3 on v2

--- a/solution.py
+++ b/solution.py
@@ -13,6 +13,7 @@
 LANES = 128
 QB = 256
 KC = 128
+ROWS = 112
 BF = jnp.bfloat16
 F32 = jnp.float32
 LOG2E = 1.4426950408889634
@@ -31,6 +32,10 @@
 
 def shape(dims, dtype):
     return jax.ShapeDtypeStruct(dims, dtype)
+
+
+def in_hbm(a):
+    return pltpu.HBM(a.shape, a.dtype)
 
 
 def pinned(*arrays):
@@ -122,7 +127,7 @@
     )(*pinned(*operands))
 
 
-def load_kernel(w_hbm, out_hbm, dec_hbm, after_ref, w_ref, dec_ref, mix_ref, out_rows, dec_rows, sem):
+def load_kernel(w_hbm, out_hbm, dec_hbm, after_ref, w_ref, dec_ref, mix_hbm, mix_ref, out_rows, dec_rows, sem):
     channels = dec_rows.shape[0]
     at = pl.multiple_of(lax.axis_index("head") * LANES, LANES)
     copies = started(
@@ -137,6 +142,9 @@
     dec_ref[...] = jnp.zeros_like(dec_ref)
     dec_ref[:channels, :] = dec_rows[...]
     mix_ref[...] = dot(out_rows[...], dec_ref[...], 1, 1).astype(BF)
+    copy = pltpu.make_async_copy(mix_ref, mix_hbm, sem.at[3])
+    copy.start()
+    copy.wait()
     copies[2].wait()
 
 
@@ -145,12 +153,13 @@
     return pl.pallas_call(
         load_kernel,
         in_specs=[HBM] * 3 + [pl.BlockSpec(memory_space=pl.ANY)],
-        out_specs=(VMEM,) * 3,
-        out_shape=(shape(w_qkv.shape, BF), shape((LANES, model), BF), shape((LANES, LANES), BF)),
+        out_specs=(VMEM, VMEM, HBM),
+        out_shape=(shape(w_qkv.shape, BF), shape((LANES, model), BF), in_hbm(shape((LANES, LANES), BF))),
         scratch_shapes=[
+            pltpu.VMEM((LANES, LANES), BF),
             pltpu.VMEM((LANES, model), BF),
             pltpu.VMEM(dec_cols.shape, BF),
-            pltpu.SemaphoreType.DMA((3,)),
+            pltpu.SemaphoreType.DMA((4,)),
         ],
         compiler_params=params(),
         cost_estimate=pl.CostEstimate(flops=2 * model * LANES * LANES, bytes_accessed=2 * w_qkv.size, transcendentals=0),
@@ -192,7 +201,7 @@
         in_specs=[VMEM] * 5,
         out_specs=(HBM, VMEM, VMEM),
         out_shape=(
-            shape((groups, NODE_DEV, 3 * LANES), BF),
+            in_hbm(shape((groups, NODE_DEV, 3 * LANES), BF)),
             shape((NODE_DEV, model), F32),
             shape((NODE_DEV, LANES), BF),
         ),
@@ -215,7 +224,7 @@
     grad = (dot(summed, high, 0, 0) + dot(summed, low, 0, 0)).astype(BF)
     for group in range(groups):
         send[group, :NODE_DEV, :] = summed
-        send[group, NODE_DEV:, :] = grad[:, group * LANES : (group + 1) * LANES]
+        send[group, NODE_DEV:, :] = grad[:ROWS, group * LANES : (group + 1) * LANES]
     copy = pltpu.make_async_copy(send, send_hbm, sem)
     copy.start()
     copy.wait()
@@ -223,12 +232,12 @@
 
 def side(enc, summed, dec_pad):
     groups = enc.shape[1] // LANES
-    send_shape = (groups, NODE_DEV + LANES, LANES)
+    send_shape = (groups, NODE_DEV + ROWS, LANES)
     return pl.pallas_call(
         side_kernel,
         in_specs=[VMEM] * 3,
         out_specs=(HBM, VMEM),
-        out_shape=(shape(send_shape, BF), shape((NODE_DEV, LANES), F32)),
+        out_shape=(in_hbm(shape(send_shape, BF)), shape((NODE_DEV, LANES), F32)),
         scratch_shapes=[pltpu.VMEM(send_shape, BF), pltpu.SemaphoreType.DMA],
         compiler_params=params(),
         name="side",
@@ -257,8 +266,11 @@
     return jnp.max(scores.reshape(KC // 8, 8, 2 * QB), axis=0)
 
 
-def near_kernel(reach, qkv_ref, win_ref, acc_ref, top_ref, q_ref, k_ref, v_ref, vt_ref, score_ref, prob_ref):
+def near_kernel(reach, qkv_ref, win_hbm, acc_hbm, top_hbm, q_hbm,
+                win_ref, acc_ref, top_ref, q_ref, k_ref, v_ref, vt_ref, score_ref, prob_ref, sem):
     groups = qkv_ref.shape[0]
+    win_copy = pltpu.make_async_copy(win_hbm, win_ref, sem.at[0])
+    win_copy.start()
     band_rows = groups * NODE_DEV
     first_node = lax.axis_index("band") * band_rows
     node_total = lax.axis_size("band") * band_rows
@@ -275,6 +287,8 @@
     for head in range(2):
         vt_ref[head, :HDIM, :] = vt[head * HDIM : (head + 1) * HDIM]
         vt_ref[head, HDIM:, :] = jnp.ones((16, band_rows), BF)
+    copies = started([pltpu.make_async_copy(q_ref, q_hbm, sem.at[1])])
+    win_copy.wait()
     for block in range(band_rows // QB):
         start = block * QB
         both = jnp.concatenate([q_ref[0, start : start + QB, :], q_ref[1, start : start + QB, :]], axis=0)
@@ -299,6 +313,10 @@
                 1,
                 0,
             )
+        copies += started([pltpu.make_async_copy(acc_ref.at[block], acc_hbm.at[block], sem.at[3 + block])])
+    copies += started([pltpu.make_async_copy(top_ref, top_hbm, sem.at[2])])
+    for copy in copies:
+        copy.wait()
 
 
 def near(qkv, win, reach):
@@ -306,34 +324,49 @@
     band_rows = groups * NODE_DEV
     blocks = band_rows // QB
     keys = min(QB + 2 * reach, band_rows)
+    outs = (
+        shape((blocks, 2, HDIM + 16, QB), F32),
+        shape((blocks, 1, 2 * QB), F32),
+        shape((2, band_rows, LANES), BF),
+    )
     return pl.pallas_call(
         functools.partial(near_kernel, reach),
-        in_specs=[VMEM] * 2,
-        out_specs=(VMEM,) * 3,
-        out_shape=(
-            shape((blocks, 2, HDIM + 16, QB), F32),
-            shape((blocks, 1, 2 * QB), F32),
-            shape((2, band_rows, LANES), BF),
-        ),
+        in_specs=[VMEM, HBM],
+        out_specs=(HBM,) * 3,
+        out_shape=tuple(in_hbm(a) for a in outs),
         scratch_shapes=[
+            pltpu.VMEM(win.shape, win.dtype),
+            *[pltpu.VMEM(a.shape, a.dtype) for a in outs],
             pltpu.VMEM((band_rows, LANES), BF),
             pltpu.VMEM((band_rows, LANES), F32),
             pltpu.VMEM((2, HDIM + 16, band_rows), BF),
             pltpu.VMEM((keys, 2 * QB), F32),
             pltpu.VMEM((keys, 2 * QB), BF),
+            pltpu.SemaphoreType.DMA((3 + blocks,)),
         ],
         compiler_params=params(),
         cost_estimate=pl.CostEstimate(flops=6_000_000_000, bytes_accessed=4_000_000, transcendentals=3_000_000),
         name="near",
-    )(qkv, win)
-
-
-def far_kernel(reach, q_ref, acc_ref, top_ref, low_ref, high_ref, win_ref, extra_ref, mix_ref,
-               node_hbm, grad_ref, k_ref, v_ref, vt_ref, score_ref, prob_ref, out_ref, node_ref, sem):
-    groups = extra_ref.shape[0]
-    band_rows = groups * NODE_DEV
+    )(qkv, *pinned(win))
+
+
+def far_kernel(reach, q_hbm, acc_hbm, top_hbm, win_hbm, mix_hbm, low_hbm, high_hbm, node_hbm, out_ref,
+               q_ref, acc_ref, top_ref, win_ref, mix_ref, low_ref, high_ref,
+               k_ref, v_ref, vt_ref, score_ref, prob_ref, node_ref, sem):
+    band_rows = q_ref.shape[1]
+    groups = band_rows // NODE_DEV
     first_node = lax.axis_index("band") * band_rows
     node_total = lax.axis_size("band") * band_rows
+    copies = started(
+        [
+            pltpu.make_async_copy(source, target, sem.at[at])
+            for at, (source, target) in enumerate(
+                [(low_hbm, low_ref), (high_hbm, high_ref), (q_hbm, q_ref), (acc_hbm, acc_ref), (top_hbm, top_ref), (win_hbm, win_ref), (mix_hbm, mix_ref)]
+            )
+        ]
+    )
+    copies[0].wait()
+    copies[1].wait()
     for side_at, half in enumerate((low_ref, high_ref)):
         for group in range(groups // 2):
             rows = pl.ds(side_at * reach + (group ^ 1) * NODE_DEV, NODE_DEV)
@@ -343,6 +376,8 @@
     for head in range(2):
         vt_ref[head, :HDIM, :] = vt[head * HDIM : (head + 1) * HDIM]
         vt_ref[head, HDIM:, :] = jnp.ones((16, 2 * reach), BF)
+    for copy in copies[2:]:
+        copy.wait()
     for block in range(band_rows // QB):
         start = block * QB
         both = jnp.concatenate([q_ref[0, start : start + QB, :], q_ref[1, start : start + QB, :]], axis=0)
@@ -373,62 +408,89 @@
             out_ref[head * HDIM : (head + 1) * HDIM, start : start + QB] = (
                 mixed[:HDIM] / mixed[HDIM : HDIM + 1]
             ).astype(BF)
-    attended = out_ref[...]
-    node = dot(mix_ref[...], attended, 0, 0).T.astype(BF)
-    for group in range(groups):
-        node_ref[group] = node[(group ^ 1) * NODE_DEV : ((group ^ 1) + 1) * NODE_DEV]
-    copy = pltpu.make_async_copy(node_ref, node_hbm, sem)
-    copy.start()
-    grad = jnp.zeros((LANES, LANES), F32)
-    total = jnp.zeros((LANES, LANES), F32)
-    for group in range(groups):
-        at = (group ^ 1) * NODE_DEV
-        grad += dot(extra_ref[group, :NODE_DEV, :], attended[:, at : at + NODE_DEV], 0, 1)
-        total += extra_ref[group, NODE_DEV:, :].astype(F32)
-    grad_ref[:LANES, :] = grad
-    grad_ref[LANES:, :] = total
-    copy.wait()
-
-
-def far(queries, acc, top, low, high, win, extra, mix):
-    groups = extra.shape[0]
+    node_ref[...] = dot(mix_ref[...], out_ref[...], 0, 0).T.astype(BF)
+    rows = pl.ds(0, NODE_DEV)
+    sends = started(
+        [
+            pltpu.make_async_copy(
+                node_ref.at[pl.ds((group ^ 1) * NODE_DEV, NODE_DEV), :],
+                node_hbm.at[group, rows, :],
+                sem.at[len(copies) + group],
+            )
+            for group in range(groups)
+        ]
+    )
+    for copy in sends:
+        copy.wait()
+
+
+def far(queries, acc, top, low, high, win, mix):
+    band_rows = queries.shape[1]
+    groups = band_rows // NODE_DEV
     reach = low.shape[0] * NODE_DEV
-    band_rows = groups * NODE_DEV
+    held = (queries, acc, top, win, mix, low, high)
     return pl.pallas_call(
         functools.partial(far_kernel, reach),
-        in_specs=[VMEM] * 8,
+        in_specs=[HBM] * 7,
         out_specs=(HBM, VMEM),
-        out_shape=(shape((groups, NODE_DEV, LANES), BF), shape((2 * LANES, LANES), F32)),
-        scratch_shapes=[
+        out_shape=(
+            in_hbm(shape((groups, NODE_DEV + 2 * ROWS, LANES), BF)),
+            shape((LANES, band_rows), BF),
+        ),
+        scratch_shapes=[pltpu.VMEM(a.shape, a.dtype) for a in held]
+        + [
             pltpu.VMEM((2 * reach, LANES), BF),
             pltpu.VMEM((2 * reach, LANES), F32),
             pltpu.VMEM((2, HDIM + 16, 2 * reach), BF),
             pltpu.VMEM((reach, 2 * QB), F32),
             pltpu.VMEM((reach, 2 * QB), BF),
-            pltpu.VMEM((LANES, band_rows), BF),
-            pltpu.VMEM((groups, NODE_DEV, LANES), BF),
-            pltpu.SemaphoreType.DMA,
+            pltpu.VMEM((band_rows, LANES), BF),
+            pltpu.SemaphoreType.DMA((len(held) + groups,)),
         ],
         compiler_params=params(),
+        cost_estimate=pl.CostEstimate(flops=6_000_000_000, bytes_accessed=2_000_000, transcendentals=1_000_000),
         name="far",
-    )(queries, acc, top, low, high, win, extra, mix)
-
-
-def nodes_kernel(parts_ref, node_ref, out_ref):
+    )(*pinned(*held))
+
+
+def grads_kernel(out_ref, extra_ref, grad_ref):
+    groups = extra_ref.shape[0]
+    grad = jnp.zeros((LANES, LANES), F32)
+    total = jnp.zeros((ROWS, LANES), F32)
+    for group in range(groups):
+        at = (group ^ 1) * NODE_DEV
+        grad += dot(extra_ref[group, :NODE_DEV, :], out_ref[:, at : at + NODE_DEV], 0, 1)
+        total += extra_ref[group, NODE_DEV:, :].astype(F32)
+    grad_ref[:ROWS, :] = grad[:ROWS]
+    grad_ref[ROWS:, :] = total
+
+
+def grads(out, extra):
+    return pl.pallas_call(
+        grads_kernel,
+        in_specs=[VMEM] * 2,
+        out_specs=VMEM,
+        out_shape=shape((2 * ROWS, LANES), F32),
+        compiler_params=params(),
+        name="grads",
+    )(out, extra)
+
+
+def table_kernel(parts_ref, node_ref, table_ref):
     total = node_ref[...]
     for group in range(parts_ref.shape[0]):
-        total += parts_ref[group].astype(F32)
-    out_ref[...] = total.astype(BF)
-
-
-def sum_nodes(parts, node):
-    return pl.pallas_call(
-        nodes_kernel,
+        total += parts_ref[group, :NODE_DEV, :].astype(F32)
+    table_ref[...] = total.astype(BF)
+
+
+def make_table(parts, node):
+    return pl.pallas_call(
+        table_kernel,
         in_specs=[VMEM] * 2,
         out_specs=VMEM,
         out_shape=shape(node.shape, BF),
         compiler_params=params(),
-        name="sum_nodes",
+        name="make_table",
     )(parts, node)
 
 
@@ -469,14 +531,37 @@
     )(far_rows, mid_rows, own_rows, dec_row, grid_in)
 
 
+def spread_kernel(grad_ref, more_ref, parts_hbm, filled_hbm, sum_ref, sem):
+    sum_ref[...] = (grad_ref[...].astype(F32) + more_ref[...].astype(F32)).astype(BF)
+    rows = pl.ds(NODE_DEV, sum_ref.shape[0])
+    copies = [
+        pltpu.make_async_copy(sum_ref, filled_hbm.at[at, rows, :], sem.at[at]) for at in range(filled_hbm.shape[0])
+    ]
+    for copy in started(copies):
+        copy.wait()
+
+
+def spread(grad, more, parts):
+    return pl.pallas_call(
+        spread_kernel,
+        in_specs=[VMEM, VMEM, HBM],
+        out_specs=HBM,
+        out_shape=in_hbm(parts),
+        input_output_aliases={2: 0},
+        scratch_shapes=[pltpu.VMEM(grad.shape, BF), pltpu.SemaphoreType.DMA((parts.shape[0],))],
+        compiler_params=params(),
+        name="spread",
+    )(grad, more, *pinned(parts))
+
+
 def gradient_kernel(parts_ref, w_out_ref, grad_ref):
     channels, model = grad_ref.shape
-    mixed = jnp.zeros((LANES, model), F32)
+    mixed = jnp.zeros((ROWS, model), F32)
     for group in range(parts_ref.shape[0]):
-        mixed += dot(parts_ref[group, :LANES, :], w_out_ref[group * LANES : (group + 1) * LANES, :], 1, 0)
+        mixed += dot(parts_ref[group, NODE_DEV : NODE_DEV + ROWS, :], w_out_ref[group * LANES : (group + 1) * LANES, :], 1, 0)
     for group in range(parts_ref.shape[0]):
         cols = slice(group * LANES, (group + 1) * LANES)
-        whole = mixed[:, cols] + parts_ref[group, LANES:, :].astype(F32)
+        whole = mixed[:, cols] + parts_ref[group, NODE_DEV + ROWS :, :].astype(F32)
         grad_ref[:, cols] = whole[:channels]
 
 
@@ -508,6 +593,10 @@
 def along_band(block, shift):
     count = lax.axis_size("band")
     return lax.ppermute(block, "band", [(i, i + shift) for i in range(count) if 0 <= i + shift < count])
+
+
+def flipped(block, axis, bit):
+    return lax.ppermute(block, axis, [(i, i ^ (1 << bit)) for i in range(lax.axis_size(axis))])
 
 
 def swap(block):
@@ -527,22 +616,21 @@
     packed, enc, summed = project(own, mid_in, far_in, norm_gain[None], weights)
     qkv = swap(packed)
     send, node = side(enc, summed, dec_pad)
+    qkv, send, node = lax.optimization_barrier((qkv, send, node))
     half = groups // 2
     reach = half * NODE_DEV
     from_low = along_band(qkv[half:, :, LANES:], 1)
     from_high = along_band(qkv[:half, :, LANES:], -1)
     extra = swap(send)
     acc, top, queries = near(qkv, win_offsets, reach)
-    node_parts, grad_part = far(queries, acc, top, from_low, from_high, win_offsets, extra, mix)
-    table = sum_nodes(swap(node_parts), node)
+    parts, attended = far(queries, acc, top, from_low, from_high, win_offsets, mix)
+    grad = grads(attended, extra)
+    grad = (grad + flipped(grad, "band", 0)).astype(BF)
+    for bit in (1, 2, 3):
+        grad = (grad.astype(F32) + flipped(grad, "band", bit).astype(F32)).astype(BF)
+    parts = swap(spread(grad, flipped(grad, "band", 4), parts))
+    table = make_table(parts, node)
     prediction = decode(two_over(table, 1), to_partner(table), table, dec_row, grid_in)
-    shift = 1
-    count = lax.axis_size("band")
-    while shift < count:
-        other = lax.ppermute(grad_part, "band", [(i, i ^ shift) for i in range(count)])
-        grad_part = (grad_part.astype(F32) + other.astype(F32)).astype(BF)
-        shift *= 2
-    parts = swap(jnp.broadcast_to(grad_part[None], (groups,) + grad_part.shape))
     grad_dec = gradient(parts, w_out, channels).T
     return (prediction, grad_dec)
 

time: 130 us -> 125 us (0.962)
  blocking collectives: 0 us -> 15.3 us
  starting transfers between devices: 48.1 us -> 39 us
  local copies, waits for them, and re-layouts: 9.82 us -> 0.79 us
  waiting for transfers between devices: 43.8 us -> 38.8 us
  Pallas kernels: 25.3 us -> 28.8 us
    all_to_all x0 -> x1, blocking collectives: none -> 15.3 us  [swap(): lax.all_to_all(block, 'head', split_axis=0, concat_axis=0, tiled=True)]
    all_to_all x4 -> x2, waiting for transfers between devices: 24.5 us -> 14.1 us  [swap(): lax.all_to_all(block, 'head', split_axis=0, concat_axis=0, tiled=True)]
    all_to_all x4 -> x2, starting transfers between devices: 16.4 us -> 8.19 us  [swap(): lax.all_to_all(block, 'head', split_axis=0, concat_axis=0, tiled=True)]
    unnamed x30 -> x12, local copies, waits for them, and re-layouts: 8.07 us -> 0.75 us
    pallas_call x3 -> x5, Pallas kernels: 9.22 us -> 12.8 us  [the longest x1 6.27 us: near(): pl.pallas_call(functools.partial(near_kernel, reach), in_specs=[VMEM, HBM...]
    ppermute x5, waiting for transfers between devices: 10.4 us -> 13.5 us  [flipped(): lax.ppermute(block, axis, [(i, i ^ 1 << bit) for i in range(lax.axis_size...]
    ppermute x2, waiting for transfers between devices: 0.01 us -> 2.17 us  [along_band(): lax.ppermute(block, 'band', [(i, i + shift) for i in range(count) if 0 <=...]
    ppermute x2, waiting for transfers between devices: 6.99 us -> 8.99 us  [two_over(): lax.ppermute(block, BOTH, [(i, j) for i, j in pairs if 0 <= j < count])]
  transfers between devices with their start and end apart: 15 -> 13, of which waited for: 10 -> 9; matrix products, arithmetic and copies ran while one was open for 1% -> 0% of each run, Pallas kernels for 8% -> 14%
where the time goes in v3:
time: 125 us; the launch traced here: 124 us
  starting transfers between devices  39 us (31%)
  waiting for transfers between devices  38.8 us (31%)
  Pallas kernels  28.8 us (23%)
  blocking collectives  15.3 us (12%)
    ppermute x5, starting transfers between devices, flipped(): lax.ppermute(block, axis, [(i, i ^ 1 << bit) for i in range(lax.axis_size...  15.6 us
    all_to_all x1, blocking collectives, swap(): lax.all_to_all(block, 'head', split_axis=0, concat_axis=0, tiled=True)  15.3 us
    all_to_all x2, waiting for transfers between devices, swap(): lax.all_to_all(block, 'head', split_axis=0, concat_axis=0, tiled=True)  14.1 us
    ppermute x5, waiting for transfers between devices, flipped(): lax.ppermute(block, axis, [(i, i ^ 1 << bit) for i in range(lax.axis_size...  13.5 us
    ppermute x2, waiting for transfers between devices, two_over(): lax.ppermute(block, BOTH, [(i, j) for i, j in pairs if 0 <= j < count])  8.99 us
    ppermute x2, starting transfers between devices, two_over(): lax.ppermute(block, BOTH, [(i, j) for i, j in pairs if 0 <= j < count])  8.24 us
    all_to_all x2, starting transfers between devices, swap(): lax.all_to_all(block, 'head', split_axis=0, concat_axis=0, tiled=True)  8.19 us
    pallas_call x1, Pallas kernels, encode(): pl.pallas_call(encode_kernel, in_specs=[HBM] * 6, out_specs=(VMEM,) * 3,...  6.71 us
  transfers between devices with their start and end apart: 13, of which 9 were waited for; matrix products, arithmetic and copies ran while one was open for 0% of the time, Pallas kernels for 14%

profile of v3, /device:TPU:32, one launch (start us, length us, event | category | flops | bytes accessed | tf_op | source)
XLA Modules:
  0.0 123.7 jit_solution(9232947978913432259)
XLA Ops:
  0.6 6.7 %encode.1 = (bf16[160,1152]{1,0:T(8,128)(2,1)S(1)}, bf16[160,1152]{1,0:T(8,128)(2,1)S(1)}, f32[160,1152]{1,0:T(8,128)S(1)}) custom-call(bf16[110,2048]{1,0:T(8,128)(2,1)} %grid_ref.1, s32[1,2048]{1,0:T(1,128)} %bitcast.11, bf16[110,1024]{1,0:T(8,128)(2,1)} %w_hbm.2, f32[1,1024]{1,0:T(1,128)} %bitcast.12, bf16[110,2048]{1,0:T(8,128)(2,1)} %cot_hbm.1, ...), custom_call_target="tpu_custom_call" | custom-call | tf_op jit(solution)/shard_map/encode/pallas_call | solution.py:112
  7.4 1.6 %collective-permute-start = (bf16[160,1152]{1,0:T(8,128)(2,1)S(1)}, bf16[160,1152]{1,0:T(8,128)(2,1)S(1)}, u32[]{:S(2)}, u32[]{:S(2)}) collective-permute-start(bf16[160,1152]{1,0:T(8,128)(2,1)S(1)} %get-tuple-element.22), channel_id=1, source_target_pairs={{0,1},{1,0},{2,3},{3,2},{4,5},{5,4},{6,7},{7,6},{8,9},{9,8},{10,11... | collective-permute-start | bytes 1105928 | tf_op jit(solution)/shard_map/ppermute | solution.py:584
  8.9 5.8 %collective-permute-start.1 = (bf16[160,1152]{1,0:T(8,128)(2,1)S(1)}, bf16[160,1152]{1,0:T(8,128)(2,1)S(1)}, u32[]{:S(2)}, u32[]{:S(2)}) collective-permute-start(bf16[160,1152]{1,0:T(8,128)(2,1)S(1)} %get-tuple-element.23.after_ref), channel_id=1, source_target_pairs={{1,3},{2,0},{3,5},{4,2},{5,7},{6,4},{7,9},{8,6},{9,11},{10,8},{11,... | collective-permute-start | bytes 1105928 | tf_op jit(solution)/shard_map/ppermute | solution.py:590
  14.7 3.1 %load.1 = (bf16[1024,3072]{1,0:T(8,128)(2,1)S(1)}, bf16[128,1024]{1,0:T(8,128)(2,1)S(1)}, bf16[128,128]{1,0:T(8,128)(2,1)}) custom-call(bf16[1024,3072]{1,0:T(8,128)(2,1)} %w_hbm.3, bf16[1024,1024]{1,0:T(8,128)(2,1)} %w_out_ref.1, bf16[110,1024]{1,0:T(8,128)(2,1)} %bitcast.10, bf16[160,1152]{1,0:T(8,128)(2,1)S(1)} %get-tuple-element.23.after_ref), custom_call_target="tpu_custom_call" | custom-call | flops 33554432 | bytes 6291456 | tf_op jit(solution)/shard_map/load/pallas_call | solution.py:153
  17.8 3.0 %collective-permute-done.1.far_ref = bf16[160,1152]{1,0:T(8,128)(2,1)S(1)} collective-permute-done((bf16[160,1152]{1,0:T(8,128)(2,1)S(1)}, bf16[160,1152]{1,0:T(8,128)(2,1)S(1)}, u32[]{:S(2)}, u32[]{:S(2)}) %collective-permute-start.1) | collective-permute-done | bytes 368672 | tf_op jit(solution)/shard_map/ppermute | solution.py:590
  20.9 2.2 %project.1 = (bf16[8,160,384]{2,1,0:T(8,128)(2,1)}, f32[160,1024]{1,0:T(8,128)S(1)}, bf16[160,128]{1,0:T(8,128)(2,1)S(1)}) custom-call(f32[160,1152]{1,0:T(8,128)S(1)} %get-tuple-element.21.own_ref, bf16[160,1152]{1,0:T(8,128)(2,1)S(1)} %collective-permute-done.mid_ref, bf16[160,1152]{1,0:T(8,128)(2,1)S(1)} %collective-permute-done.1.far_ref, ...), custom_call_target="tpu_custom_call" | custom-call | tf_op jit(solution)/shard_map/project/pallas_call | solution.py:199
  23.1 4.5 %all-to-all-start = ((bf16[8,160,384]{2,1,0:T(8,128)(2,1)}), bf16[8,160,384]{2,1,0:T(8,128)(2,1)S(1)}, u32[]{:S(2)}, u32[]{:S(2)}) async-start(bf16[8,160,384]{2,1,0:T(8,128)(2,1)} %get-tuple-element.25), calls=%async_computation | async-start | bytes 1966080 | tf_op jit(solution)/shard_map/all_to_all | solution.py:603
  27.5 1.3 %side.1 = (bf16[8,272,128]{2,1,0:T(8,128)(2,1)}, f32[160,128]{1,0:T(8,128)S(1)}) custom-call(f32[160,1024]{1,0:T(8,128)S(1)} %get-tuple-element.26.enc_ref, bf16[160,128]{1,0:T(8,128)(2,1)S(1)} %get-tuple-element.27.s_ref, bf16[128,1024]{1,0:T(8,128)(2,1)S(1)} %get-tuple-element.28.dec_ref), custom_call_target="tpu_custom_call" | custom-call | tf_op jit(solution)/shard_map/side/pallas_call | solution.py:236
  28.8 14.1 %all-to-all-done.qkv_ref = bf16[8,160,384]{2,1,0:T(8,128)(2,1)S(1)} async-done(((bf16[8,160,384]{2,1,0:T(8,128)(2,1)}), bf16[8,160,384]{2,1,0:T(8,128)(2,1)S(1)}, u32[]{:S(2)}, u32[]{:S(2)}) %all-to-all-start) | async-done | bytes 983072 | tf_op jit(solution)/shard_map/all_to_all | solution.py:603
  42.9 3.7 %all-to-all-start.1 = ((bf16[8,272,128]{2,1,0:T(8,128)(2,1)}), bf16[8,272,128]{2,1,0:T(8,128)(2,1)S(1)}, u32[]{:S(2)}, u32[]{:S(2)}) async-start(bf16[8,272,128]{2,1,0:T(8,128)(2,1)} %get-tuple-element.37), calls=%async_computation.1 | async-start | bytes 1114112 | tf_op jit(solution)/shard_map/all_to_all | solution.py:603
  46.6 2.4 %collective-permute-start.3 = (bf16[4,160,256]{2,1,0:T(8,128)(2,1)S(1)}, bf16[4,160,256]{2,1,0:T(8,128)(2,1)S(1)}, u32[]{:S(2)}, u32[]{:S(2)}) collective-permute-start(bf16[4,160,256]{2,1,0:T(8,128)(2,1)S(1)} %get-tuple-element.40), channel_id=1, source_target_pairs={{8,0},{16,8},{24,16},{32,24},{40,32},{48,40},{56,48},{64,56},{72,6... | collective-permute-start | bytes 983048 | tf_op jit(solution)/shard_map/ppermute | solution.py:595
  49.0 2.4 %collective-permute-start.2 = (bf16[4,160,256]{2,1,0:T(8,128)(2,1)S(1)}, bf16[4,160,256]{2,1,0:T(8,128)(2,1)S(1)}, u32[]{:S(2)}, u32[]{:S(2)}) collective-permute-start(bf16[4,160,256]{2,1,0:T(8,128)(2,1)S(1)} %get-tuple-element.41), channel_id=1, source_target_pairs={{0,8},{8,16},{16,24},{24,32},{32,40},{40,48},{48,56},{56,64},{64,7... | collective-permute-start | bytes 983048 | tf_op jit(solution)/shard_map/ppermute | solution.py:595
  51.4 6.3 %near.1 = (f32[5,2,80,256]{3,2,1,0:T(8,128)}, f32[5,1,512]{2,1,0:T(1,128)}, bf16[2,1280,128]{2,1,0:T(8,128)(2,1)}) custom-call(bf16[8,160,384]{2,1,0:T(8,128)(2,1)S(1)} %all-to-all-done.qkv_ref, s32[2,1280]{1,0:T(2,128)} %win_hbm.3), custom_call_target="tpu_custom_call" | custom-call | flops 6000000000 | bytes 4000000 | tf_op jit(solution)/shard_map/near/pallas_call | solution.py:332
  57.7 2.2 %collective-permute-done.2.low_hbm = bf16[4,160,256]{2,1,0:T(8,128)(2,1)S(1)} collective-permute-done((bf16[4,160,256]{2,1,0:T(8,128)(2,1)S(1)}, bf16[4,160,256]{2,1,0:T(8,128)(2,1)S(1)}, u32[]{:S(2)}, u32[]{:S(2)}) %collective-permute-start.2) | collective-permute-done | bytes 327712 | tf_op jit(solution)/shard_map/ppermute | solution.py:595
  59.9 0.7 copy-done.5
  60.6 5.1 %far.1 = (bf16[8,384,128]{2,1,0:T(8,128)(2,1)}, bf16[128,1280]{1,0:T(8,128)(2,1)S(1)}) custom-call(bf16[2,1280,128]{2,1,0:T(8,128)(2,1)} %get-tuple-element.32.q_hbm, f32[5,2,80,256]{3,2,1,0:T(8,128)} %get-tuple-element.33.acc_hbm, f32[5,1,512]{2,1,0:T(1,128)} %get-tuple-element.34.top_hbm, s32[2,1280]{1,0:T(2,128)} %win_hbm.3, ...), custom_call_target="tpu_custom_call" | custom-call | flops 6000000000 | bytes 2000000 | tf_op jit(solution)/shard_map/far/pallas_call | solution.py:432
  66.3 2.4 %collective-permute-start.4 = (f32[224,128]{1,0:T(8,128)S(1)}, f32[224,128]{1,0:T(8,128)S(1)}, u32[]{:S(2)}, u32[]{:S(2)}) collective-permute-start(f32[224,128]{1,0:T(8,128)S(1)} %grads.1), channel_id=1, source_target_pairs={{0,8},{8,0},{16,24},{24,16},{32,40},{40,32},{48,56},{56,48},{64,72... | collective-permute-start | bytes 344072 | tf_op jit(solution)/shard_map/ppermute | solution.py:599
  68.7 1.0 collective-permute-done.4
  69.7 3.1 %collective-permute-start.5 = (bf16[224,128]{1,0:T(8,128)(2,1)S(1)}, bf16[224,128]{1,0:T(8,128)(2,1)S(1)}, u32[]{:S(2)}, u32[]{:S(2)}) collective-permute-start(bf16[224,128]{1,0:T(8,128)(2,1)S(1)} %add_convert_fusion.3), channel_id=1, source_target_pairs={{0,16},{8,24},{16,0},{24,8},{32,48},{40,56},{48,32},{56,40},{64,80... | collective-permute-start | bytes 172040 | tf_op jit(solution)/shard_map/ppermute | solution.py:599
  72.8 2.6 %collective-permute-done.5 = bf16[224,128]{1,0:T(8,128)(2,1)S(1)} collective-permute-done((bf16[224,128]{1,0:T(8,128)(2,1)S(1)}, bf16[224,128]{1,0:T(8,128)(2,1)S(1)}, u32[]{:S(2)}, u32[]{:S(2)}) %collective-permute-start.5) | collective-permute-done | bytes 57376 | tf_op jit(solution)/shard_map/ppermute | solution.py:599
  75.6 4.2 %collective-permute-done.6 = bf16[224,128]{1,0:T(8,128)(2,1)S(1)} collective-permute-done((bf16[224,128]{1,0:T(8,128)(2,1)S(1)}, bf16[224,128]{1,0:T(8,128)(2,1)S(1)}, u32[]{:S(2)}, u32[]{:S(2)}) %collective-permute-start.6) | collective-permute-done | bytes 57376 | tf_op jit(solution)/shard_map/ppermute | solution.py:599
  79.7 5.4 %collective-permute-start.7 = (bf16[224,128]{1,0:T(8,128)(2,1)S(1)}, bf16[224,128]{1,0:T(8,128)(2,1)S(1)}, u32[]{:S(2)}, u32[]{:S(2)}) collective-permute-start(bf16[224,128]{1,0:T(8,128)(2,1)S(1)} %add_convert_fusion.1), channel_id=1, source_target_pairs={{0,64},{8,72},{16,80},{24,88},{32,96},{40,104},{48,112},{56,120},{... | collective-permute-start | bytes 172040 | tf_op jit(solution)/shard_map/ppermute | solution.py:599
  85.2 2.2 %collective-permute-done.7 = bf16[224,128]{1,0:T(8,128)(2,1)S(1)} collective-permute-done((bf16[224,128]{1,0:T(8,128)(2,1)S(1)}, bf16[224,128]{1,0:T(8,128)(2,1)S(1)}, u32[]{:S(2)}, u32[]{:S(2)}) %collective-permute-start.7) | collective-permute-done | bytes 57376 | tf_op jit(solution)/shard_map/ppermute | solution.py:599
  87.4 4.6 %collective-permute-start.8 = (bf16[224,128]{1,0:T(8,128)(2,1)S(1)}, bf16[224,128]{1,0:T(8,128)(2,1)S(1)}, u32[]{:S(2)}, u32[]{:S(2)}) collective-permute-start(bf16[224,128]{1,0:T(8,128)(2,1)S(1)} %add_convert_fusion.grad_ref), channel_id=1, source_target_pairs={{0,128},{8,136},{16,144},{24,152},{32,160},{40,168},{48,176},{56,1... | collective-permute-start | bytes 172040 | tf_op jit(solution)/shard_map/ppermute | solution.py:599
  91.9 3.6 %collective-permute-done.8.more_ref = bf16[224,128]{1,0:T(8,128)(2,1)S(1)} collective-permute-done((bf16[224,128]{1,0:T(8,128)(2,1)S(1)}, bf16[224,128]{1,0:T(8,128)(2,1)S(1)}, u32[]{:S(2)}, u32[]{:S(2)}) %collective-permute-start.8) | collective-permute-done | bytes 57376 | tf_op jit(solution)/shard_map/ppermute | solution.py:599
  95.5 0.9 spread.1
  96.4 15.3 %all_to_all.15.parts_ref = bf16[8,384,128]{2,1,0:T(8,128)(2,1)S(1)} all-to-all(bf16[8,384,128]{2,1,0:T(8,128)(2,1)} %spread.1), channel_id=1, replica_groups=mesh['band'=32,'head'=8] {'head'}, dimensions={0} | all-to-all | bytes 1572864 | tf_op jit(solution)/shard_map/all_to_all | solution.py:603
  111.8 0.6 collective-permute-start.10
  112.4 2.5 %collective-permute-start.9 = (bf16[160,128]{1,0:T(8,128)(2,1)S(1)}, bf16[160,128]{1,0:T(8,128)(2,1)S(1)}, u32[]{:S(2)}, u32[]{:S(2)}) collective-permute-start(bf16[160,128]{1,0:T(8,128)(2,1)S(1)} %make_table.1.own_ref), channel_id=1, source_target_pairs={{0,2},{2,4},{3,1},{4,6},{5,3},{6,8},{7,5},{8,10},{9,7},{10,12},{11... | collective-permute-start | bytes 122888 | tf_op jit(solution)/shard_map/ppermute | solution.py:590
  114.9 1.4 %gradient.1 = f32[110,1024]{1,0:T(8,128)} custom-call(bf16[8,384,128]{2,1,0:T(8,128)(2,1)S(1)} %all_to_all.15.parts_ref, bf16[1024,1024]{1,0:T(8,128)(2,1)S(1)} %copy-done), custom_call_target="tpu_custom_call" | custom-call | tf_op jit(solution)/shard_map/gradient/pallas_call | solution.py:569
  116.3 5.9 %collective-permute-done.9.far_ref = bf16[160,128]{1,0:T(8,128)(2,1)S(1)} collective-permute-done((bf16[160,128]{1,0:T(8,128)(2,1)S(1)}, bf16[160,128]{1,0:T(8,128)(2,1)S(1)}, u32[]{:S(2)}, u32[]{:S(2)}) %collective-permute-start.9) | collective-permute-done | bytes 40992 | tf_op jit(solution)/shard_map/ppermute | solution.py:590
  122.2 1.4 %decode.1 = bf16[110,2048]{1,0:T(8,128)(2,1)} custom-call(bf16[160,128]{1,0:T(8,128)(2,1)S(1)} %collective-permute-done.9.far_ref, bf16[160,128]{1,0:T(8,128)(2,1)S(1)} %collective-permute-done.10.mid_ref, bf16[160,128]{1,0:T(8,128)(2,1)S(1)} %make_table.1.own_ref, s32[1,2048]{1,0:T(1,128)S(1)} %bitcast.7, bf16[110,2048]{1,0:T(8,128)(2,1)S(1)} %copy-done.1), custom_call_target="tpu_custom_call" | custom-call | tf_op jit(solution)/shard_map/decode/pallas_call | solution.py:524
  (23 shorter events, 0.8 us)
Async XLA Ops:
  0.6 20.2 %copy-start.3 = (f32[1024]{0:T(1024)S(1)}, f32[1024]{0:T(1024)}, u32[]{:S(2)}) copy-start(f32[1024]{0:T(1024)} %param.19) | copy-start | bytes 12292
  7.4 10.4 %collective-permute-start = (bf16[160,1152]{1,0:T(8,128)(2,1)S(1)}, bf16[160,1152]{1,0:T(8,128)(2,1)S(1)}, u32[]{:S(2)}, u32[]{:S(2)}) collective-permute-start(bf16[160,1152]{1,0:T(8,128)(2,1)S(1)} %get-tuple-element.22), channel_id=1, source_target_pairs={{0,1},{1,0},{2,3},{3,2},{4,5},{5,4},{6,7},{7,6},{8,9},{9,8},{10,11... | collective-permute-start | bytes 1105928 | tf_op jit(solution)/shard_map/ppermute | solution.py:584
  8.9 11.9 %collective-permute-start.1 = (bf16[160,1152]{1,0:T(8,128)(2,1)S(1)}, bf16[160,1152]{1,0:T(8,128)(2,1)S(1)}, u32[]{:S(2)}, u32[]{:S(2)}) collective-permute-start(bf16[160,1152]{1,0:T(8,128)(2,1)S(1)} %get-tuple-element.23.after_ref), channel_id=1, source_target_pairs={{1,3},{2,0},{3,5},{4,2},{5,7},{6,4},{7,9},{8,6},{9,11},{10,8},{11,... | collective-permute-start | bytes 1105928 | tf_op jit(solution)/shard_map/ppermute | solution.py:590
  23.1 19.8 %all-to-all-start = ((bf16[8,160,384]{2,1,0:T(8,128)(2,1)}), bf16[8,160,384]{2,1,0:T(8,128)(2,1)S(1)}, u32[]{:S(2)}, u32[]{:S(2)}) async-start(bf16[8,160,384]{2,1,0:T(8,128)(2,1)} %get-tuple-element.25), calls=%async_computation | async-start | bytes 1966080 | tf_op jit(solution)/shard_map/all_to_all | solution.py:603
  42.9 22.9 %all-to-all-start.1 = ((bf16[8,272,128]{2,1,0:T(8,128)(2,1)}), bf16[8,272,128]{2,1,0:T(8,128)(2,1)S(1)}, u32[]{:S(2)}, u32[]{:S(2)}) async-start(bf16[8,272,128]{2,1,0:T(8,128)(2,1)} %get-tuple-element.37), calls=%async_computation.1 | async-start | bytes 1114112 | tf_op jit(solution)/shard_map/all_to_all | solution.py:603
  46.6 11.1 %collective-permute-start.3 = (bf16[4,160,256]{2,1,0:T(8,128)(2,1)S(1)}, bf16[4,160,256]{2,1,0:T(8,128)(2,1)S(1)}, u32[]{:S(2)}, u32[]{:S(2)}) collective-permute-start(bf16[4,160,256]{2,1,0:T(8,128)(2,1)S(1)} %get-tuple-element.40), channel_id=1, source_target_pairs={{8,0},{16,8},{24,16},{32,24},{40,32},{48,40},{56,48},{64,56},{72,6... | collective-permute-start | bytes 983048 | tf_op jit(solution)/shard_map/ppermute | solution.py:595
  49.0 10.9 %collective-permute-start.2 = (bf16[4,160,256]{2,1,0:T(8,128)(2,1)S(1)}, bf16[4,160,256]{2,1,0:T(8,128)(2,1)S(1)}, u32[]{:S(2)}, u32[]{:S(2)}) collective-permute-start(bf16[4,160,256]{2,1,0:T(8,128)(2,1)S(1)} %get-tuple-element.41), channel_id=1, source_target_pairs={{0,8},{8,16},{16,24},{24,32},{32,40},{40,48},{48,56},{56,64},{64,7... | collective-permute-start | bytes 983048 | tf_op jit(solution)/shard_map/ppermute | solution.py:595
  57.7 2.2 %copy-start.4 = (bf16[4,160,256]{2,1,0:T(8,128)(2,1)}, bf16[4,160,256]{2,1,0:T(8,128)(2,1)S(1)}, u32[]{:S(2)}) copy-start(bf16[4,160,256]{2,1,0:T(8,128)(2,1)S(1)} %collective-permute-done.3.high_hbm) | copy-start | bytes 983044
  59.9 0.7 copy-start.5
  65.8 49.1 %copy-start = (bf16[1024,1024]{1,0:T(8,128)(2,1)S(1)}, bf16[1024,1024]{1,0:T(8,128)(2,1)}, u32[]{:S(2)}) copy-start(bf16[1024,1024]{1,0:T(8,128)(2,1)} %w_out_ref.1) | copy-start | bytes 6291460
  65.8 56.5 %copy-start.1 = (bf16[110,2048]{1,0:T(8,128)(2,1)S(1)}, bf16[110,2048]{1,0:T(8,128)(2,1)}, u32[]{:S(2)}) copy-start(bf16[110,2048]{1,0:T(8,128)(2,1)} %grid_ref.1) | copy-start | bytes 1351684
  65.8 56.5 %copy-start.2 = (s32[2048]{0:T(1024)S(1)}, s32[2048]{0:T(1024)}, u32[]{:S(2)}) copy-start(s32[2048]{0:T(1024)} %param.13) | copy-start | bytes 24580
  66.3 3.4 %collective-permute-start.4 = (f32[224,128]{1,0:T(8,128)S(1)}, f32[224,128]{1,0:T(8,128)S(1)}, u32[]{:S(2)}, u32[]{:S(2)}) collective-permute-start(f32[224,128]{1,0:T(8,128)S(1)} %grads.1), channel_id=1, source_target_pairs={{0,8},{8,0},{16,24},{24,16},{32,40},{40,32},{48,56},{56,48},{64,72... | collective-permute-start | bytes 344072 | tf_op jit(solution)/shard_map/ppermute | solution.py:599
  69.7 5.8 %collective-permute-start.5 = (bf16[224,128]{1,0:T(8,128)(2,1)S(1)}, bf16[224,128]{1,0:T(8,128)(2,1)S(1)}, u32[]{:S(2)}, u32[]{:S(2)}) collective-permute-start(bf16[224,128]{1,0:T(8,128)(2,1)S(1)} %add_convert_fusion.3), channel_id=1, source_target_pairs={{0,16},{8,24},{16,0},{24,8},{32,48},{40,56},{48,32},{56,40},{64,80... | collective-permute-start | bytes 172040 | tf_op jit(solution)/shard_map/ppermute | solution.py:599
  75.5 4.3 %collective-permute-start.6 = (bf16[224,128]{1,0:T(8,128)(2,1)S(1)}, bf16[224,128]{1,0:T(8,128)(2,1)S(1)}, u32[]{:S(2)}, u32[]{:S(2)}) collective-permute-start(bf16[224,128]{1,0:T(8,128)(2,1)S(1)} %add_convert_fusion.2), channel_id=1, source_target_pairs={{0,32},{8,40},{16,48},{24,56},{32,0},{40,8},{48,16},{56,24},{64,96... | collective-permute-start | bytes 172040 | tf_op jit(solution)/shard_map/ppermute | solution.py:599
  79.7 7.6 %collective-permute-start.7 = (bf16[224,128]{1,0:T(8,128)(2,1)S(1)}, bf16[224,128]{1,0:T(8,128)(2,1)S(1)}, u32[]{:S(2)}, u32[]{:S(2)}) collective-permute-start(bf16[224,128]{1,0:T(8,128)(2,1)S(1)} %add_convert_fusion.1), channel_id=1, source_target_pairs={{0,64},{8,72},{16,80},{24,88},{32,96},{40,104},{48,112},{56,120},{... | collective-permute-start | bytes 172040 | tf_op jit(solution)/shard_map/ppermute | solution.py:599
  87.4 8.2 %collective-permute-start.8 = (bf16[224,128]{1,0:T(8,128)(2,1)S(1)}, bf16[224,128]{1,0:T(8,128)(2,1)S(1)}, u32[]{:S(2)}, u32[]{:S(2)}) collective-permute-start(bf16[224,128]{1,0:T(8,128)(2,1)S(1)} %add_convert_fusion.grad_ref), channel_id=1, source_target_pairs={{0,128},{8,136},{16,144},{24,152},{32,160},{40,168},{48,176},{56,1... | collective-permute-start | bytes 172040 | tf_op jit(solution)/shard_map/ppermute | solution.py:599
  111.8 4.5 %collective-permute-start.10 = (bf16[160,128]{1,0:T(8,128)(2,1)S(1)}, bf16[160,128]{1,0:T(8,128)(2,1)S(1)}, u32[]{:S(2)}, u32[]{:S(2)}) collective-permute-start(bf16[160,128]{1,0:T(8,128)(2,1)S(1)} %make_table.1.own_ref), channel_id=1, source_target_pairs={{0,1},{1,0},{2,3},{3,2},{4,5},{5,4},{6,7},{7,6},{8,9},{9,8},{10,11... | collective-permute-start | bytes 122888 | tf_op jit(solution)/shard_map/ppermute | solution.py:584
  112.4 9.8 %collective-permute-start.9 = (bf16[160,128]{1,0:T(8,128)(2,1)S(1)}, bf16[160,128]{1,0:T(8,128)(2,1)S(1)}, u32[]{:S(2)}, u32[]{:S(2)}) collective-permute-start(bf16[160,128]{1,0:T(8,128)(2,1)S(1)} %make_table.1.own_ref), channel_id=1, source_target_pairs={{0,2},{2,4},{3,1},{4,6},{5,3},{6,8},{7,5},{8,10},{9,7},{10,12},{11... | collective-permute-start | bytes 122888 | tf_op jit(solution)/shard_map/ppermute | solution.py:590

commit v4 on v3

--- a/solution.py
+++ b/solution.py
@@ -14,6 +14,7 @@
 QB = 256
 KC = 128
 ROWS = 112
+EXTRA = 16
 BF = jnp.bfloat16
 F32 = jnp.float32
 LOG2E = 1.4426950408889634
@@ -91,7 +92,7 @@
         message = (half + half * jnp.tanh(half)).astype(BF)
         spread = dot(pick_ref[...], message, 1, 0)
         far_ref[:, at : at + width] = spread[:nodes].astype(BF)
-        mid_ref[:, at : at + width] = spread[nodes : 2 * nodes].astype(BF)
+        mid_ref[:nodes, at : at + width] = spread[nodes : 2 * nodes].astype(BF)
         own_ref[:, at : at + width] = spread[2 * nodes :]
     copies[4].wait()
     copies[5].wait()
@@ -100,7 +101,8 @@
     pick(dec_ref[...])
     spread = dot(pick_ref[...], cot_pad[...], 1, 1)
     far_ref[:, model:] = spread[:nodes].astype(BF)
-    mid_ref[:, model:] = spread[nodes : 2 * nodes].astype(BF)
+    mid_ref[nodes:, :] = jnp.zeros((EXTRA, mid_ref.shape[1]), BF)
+    mid_ref[:nodes, model:] = spread[nodes : 2 * nodes].astype(BF)
     own_ref[:, model:] = spread[2 * nodes :]
 
 
@@ -113,7 +115,7 @@
         encode_kernel,
         in_specs=[HBM] * 6,
         out_specs=(VMEM,) * 3,
-        out_shape=(shape((NODE_DEV, wide), BF), shape((NODE_DEV, wide), BF), shape((NODE_DEV, wide), F32)),
+        out_shape=(shape((NODE_DEV, wide), BF), shape((NODE_DEV + EXTRA, wide), BF), shape((NODE_DEV, wide), F32)),
         scratch_shapes=[pltpu.VMEM(a.shape, a.dtype) for a in operands]
         + [
             pltpu.VMEM((points, LANES), BF),
@@ -169,7 +171,7 @@
 
 def project_kernel(own_ref, mid_ref, far_ref, gain_ref, w_ref, packed_hbm, enc_ref, s_ref, packed, sem):
     model = gain_ref.shape[1]
-    total = own_ref[...] + mid_ref[...].astype(F32) + far_ref[...].astype(F32)
+    total = own_ref[...] + mid_ref[:NODE_DEV].astype(F32) + far_ref[...].astype(F32)
     enc = total[:, :model]
     s_ref[...] = total[:, model:].astype(BF)
     enc_ref[...] = enc
@@ -350,8 +352,8 @@
     )(qkv, *pinned(win))
 
 
-def far_kernel(reach, q_hbm, acc_hbm, top_hbm, win_hbm, mix_hbm, low_hbm, high_hbm, node_hbm, out_ref,
-               q_ref, acc_ref, top_ref, win_ref, mix_ref, low_ref, high_ref,
+def far_kernel(reach, q_hbm, acc_hbm, top_hbm, win_hbm, mix_hbm, chip_hbm, off_hbm, node_hbm, out_ref,
+               q_ref, acc_ref, top_ref, win_ref, mix_ref, chip_ref, off_ref,
                k_ref, v_ref, vt_ref, score_ref, prob_ref, node_ref, sem):
     band_rows = q_ref.shape[1]
     groups = band_rows // NODE_DEV
@@ -361,15 +363,16 @@
         [
             pltpu.make_async_copy(source, target, sem.at[at])
             for at, (source, target) in enumerate(
-                [(low_hbm, low_ref), (high_hbm, high_ref), (q_hbm, q_ref), (acc_hbm, acc_ref), (top_hbm, top_ref), (win_hbm, win_ref), (mix_hbm, mix_ref)]
+                [(chip_hbm, chip_ref), (off_hbm, off_ref), (q_hbm, q_ref), (acc_hbm, acc_ref), (top_hbm, top_ref), (win_hbm, win_ref), (mix_hbm, mix_ref)]
             )
         ]
     )
+    core = lax.rem(lax.axis_index("band"), 2)
     copies[0].wait()
     copies[1].wait()
-    for side_at, half in enumerate((low_ref, high_ref)):
+    for base, half in (((1 - core) * reach, chip_ref), (core * reach, off_ref)):
         for group in range(groups // 2):
-            rows = pl.ds(side_at * reach + (group ^ 1) * NODE_DEV, NODE_DEV)
+            rows = pl.ds(pl.multiple_of(base + (group ^ 1) * NODE_DEV, NODE_DEV), NODE_DEV)
             k_ref[rows, :] = half[group, :, :LANES]
             v_ref[rows, :] = half[group, :, LANES:].astype(F32)
     vt = v_ref[...].T.astype(BF)
@@ -424,17 +427,17 @@
         copy.wait()
 
 
-def far(queries, acc, top, low, high, win, mix):
+def far(queries, acc, top, on_chip, off_chip, win, mix):
     band_rows = queries.shape[1]
     groups = band_rows // NODE_DEV
-    reach = low.shape[0] * NODE_DEV
-    held = (queries, acc, top, win, mix, low, high)
+    reach = on_chip.shape[0] * NODE_DEV
+    held = (queries, acc, top, win, mix, on_chip, off_chip)
     return pl.pallas_call(
         functools.partial(far_kernel, reach),
         in_specs=[HBM] * 7,
         out_specs=(HBM, VMEM),
         out_shape=(
-            in_hbm(shape((groups, NODE_DEV + 2 * ROWS, LANES), BF)),
+            in_hbm(shape((groups, NODE_DEV + ROWS, LANES), BF)),
             shape((LANES, band_rows), BF),
         ),
         scratch_shapes=[pltpu.VMEM(a.shape, a.dtype) for a in held]
@@ -453,7 +456,7 @@
     )(*pinned(*held))
 
 
-def grads_kernel(out_ref, extra_ref, grad_ref):
+def grads_kernel(out_ref, extra_ref, keep_ref, give_ref):
     groups = extra_ref.shape[0]
     grad = jnp.zeros((LANES, LANES), F32)
     total = jnp.zeros((ROWS, LANES), F32)
@@ -461,16 +464,18 @@
         at = (group ^ 1) * NODE_DEV
         grad += dot(extra_ref[group, :NODE_DEV, :], out_ref[:, at : at + NODE_DEV], 0, 1)
         total += extra_ref[group, NODE_DEV:, :].astype(F32)
-    grad_ref[:ROWS, :] = grad[:ROWS]
-    grad_ref[ROWS:, :] = total
+    first = lax.rem(lax.axis_index("band"), 2) == 0
+    keep_ref[...] = jnp.where(first, grad[:ROWS], total)
+    give_ref[...] = jnp.where(first, total, grad[:ROWS])
 
 
 def grads(out, extra):
+    half = shape((ROWS, LANES), F32)
     return pl.pallas_call(
         grads_kernel,
         in_specs=[VMEM] * 2,
-        out_specs=VMEM,
-        out_shape=shape((2 * ROWS, LANES), F32),
+        out_specs=(VMEM,) * 2,
+        out_shape=(half, half),
         compiler_params=params(),
         name="grads",
     )(out, extra)
@@ -494,7 +499,7 @@
     )(parts, node)
 
 
-def decode_kernel(far_ref, mid_ref, own_ref, dec_ref, grid_ref, pred_ref):
+def decode_kernel(mid_ref, far_ref, own_ref, dec_ref, grid_ref, pred_ref):
     channels, points = grid_ref.shape
     nodes = NODE_DEV
     rows = 4 * LANES
@@ -528,7 +533,7 @@
         out_shape=shape(grid_in.shape, BF),
         compiler_params=params(),
         name="decode",
-    )(far_rows, mid_rows, own_rows, dec_row, grid_in)
+    )(mid_rows, far_rows, own_rows, dec_row, grid_in)
 
 
 def spread_kernel(grad_ref, more_ref, parts_hbm, filled_hbm, sum_ref, sem):
@@ -554,26 +559,49 @@
     )(grad, more, *pinned(parts))
 
 
-def gradient_kernel(parts_ref, w_out_ref, grad_ref):
-    channels, model = grad_ref.shape
-    mixed = jnp.zeros((ROWS, model), F32)
-    for group in range(parts_ref.shape[0]):
-        mixed += dot(parts_ref[group, NODE_DEV : NODE_DEV + ROWS, :], w_out_ref[group * LANES : (group + 1) * LANES, :], 1, 0)
-    for group in range(parts_ref.shape[0]):
-        cols = slice(group * LANES, (group + 1) * LANES)
-        whole = mixed[:, cols] + parts_ref[group, NODE_DEV + ROWS :, :].astype(F32)
-        grad_ref[:, cols] = whole[:channels]
-
-
-def gradient(parts, w_out, channels):
-    return pl.pallas_call(
-        gradient_kernel,
+def half_kernel(parts_ref, w_out_ref, half_ref):
+    first = lax.rem(lax.axis_index("band"), 2) == 0
+    groups = parts_ref.shape[0]
+
+    @pl.when(first)
+    def _():
+        mixed = jnp.zeros(half_ref.shape, F32)
+        for group in range(groups):
+            rows = w_out_ref[group * LANES : (group + 1) * LANES, :]
+            mixed += dot(parts_ref[group, NODE_DEV:, :], rows, 1, 0)
+        half_ref[...] = mixed
+
+    @pl.when(jnp.logical_not(first))
+    def _():
+        for group in range(groups):
+            half_ref[:, group * LANES : (group + 1) * LANES] = parts_ref[group, NODE_DEV:, :].astype(F32)
+
+
+def gradient_half(parts, w_out):
+    return pl.pallas_call(
+        half_kernel,
         in_specs=[VMEM] * 2,
         out_specs=VMEM,
-        out_shape=shape((channels, w_out.shape[0]), F32),
-        compiler_params=params(),
-        name="gradient",
+        out_shape=shape((ROWS, w_out.shape[1]), F32),
+        compiler_params=params(),
+        name="gradient_half",
     )(parts, w_out)
+
+
+def add_kernel(mine_ref, other_ref, out_ref):
+    channels = out_ref.shape[0]
+    out_ref[...] = mine_ref[:channels] + other_ref[:channels]
+
+
+def add(mine, other, channels):
+    return pl.pallas_call(
+        add_kernel,
+        in_specs=[VMEM] * 2,
+        out_specs=VMEM,
+        out_shape=shape((channels, mine.shape[1]), F32),
+        compiler_params=params(),
+        name="add",
+    )(mine, other)
 
 
 def total_devices():
@@ -590,13 +618,20 @@
     return lax.ppermute(block, BOTH, [(i, j) for i, j in pairs if 0 <= j < count])
 
 
-def along_band(block, shift):
+def next_chip(block):
     count = lax.axis_size("band")
-    return lax.ppermute(block, "band", [(i, i + shift) for i in range(count) if 0 <= i + shift < count])
+    pairs = [(i, i - 1 + 2 * (i % 2)) for i in range(count)]
+    return lax.ppermute(block, "band", [(i, j) for i, j in pairs if 0 <= j < count])
 
 
 def flipped(block, axis, bit):
     return lax.ppermute(block, axis, [(i, i ^ (1 << bit)) for i in range(lax.axis_size(axis))])
+
+
+def across(block):
+    planes = lax.axis_size("band") // 4
+    other = [(z + 6) % planes if z % 4 < 2 else (z + 2) % planes for z in range(planes)]
+    return lax.ppermute(block, "band", [(i, other[i // 4] * 4 + i % 4) for i in range(planes * 4)])
 
 
 def swap(block):
@@ -619,20 +654,23 @@
     qkv, send, node = lax.optimization_barrier((qkv, send, node))
     half = groups // 2
     reach = half * NODE_DEV
-    from_low = along_band(qkv[half:, :, LANES:], 1)
-    from_high = along_band(qkv[:half, :, LANES:], -1)
+    core = lax.rem(lax.axis_index("band"), 2)
+    kv = qkv[:, :, LANES:]
+    on_chip = flipped(lax.dynamic_slice_in_dim(kv, (1 - core) * half, half, 0), "band", 0)
+    off_chip = next_chip(lax.dynamic_slice_in_dim(kv, core * half, half, 0))
     extra = swap(send)
     acc, top, queries = near(qkv, win_offsets, reach)
-    parts, attended = far(queries, acc, top, from_low, from_high, win_offsets, mix)
-    grad = grads(attended, extra)
-    grad = (grad + flipped(grad, "band", 0)).astype(BF)
+    parts, attended = far(queries, acc, top, on_chip, off_chip, win_offsets, mix)
+    grad, give = grads(attended, extra)
+    grad = (grad + flipped(give, "band", 0)).astype(BF)
     for bit in (1, 2, 3):
         grad = (grad.astype(F32) + flipped(grad, "band", bit).astype(F32)).astype(BF)
-    parts = swap(spread(grad, flipped(grad, "band", 4), parts))
+    parts = swap(spread(grad, across(grad), parts))
     table = make_table(parts, node)
+    half_grad = gradient_half(parts, w_out)
     prediction = decode(two_over(table, 1), to_partner(table), table, dec_row, grid_in)
-    grad_dec = gradient(parts, w_out, channels).T
-    return (prediction, grad_dec)
+    grad_dec = add(half_grad, flipped(half_grad, "band", 0), channels)
+    return (prediction, grad_dec.T)
 
 
 def solution(mesh):

time: 125 us -> 117 us (0.936); the launches traced: 124 us -> 117 us
  waiting for transfers between devices: 38.8 us -> 34 us
  blocking collectives: 15.3 us -> 13.9 us
    ppermute x5 -> x6, starting transfers between devices: 15.6 us -> 9.99 us  [flipped(): lax.ppermute(block, axis, [(i, i ^ 1 << bit) for i in range(lax.axis_size...]
    ppermute x2, starting transfers between devices: 4.79 us -> 9.75 us  [the longest x1 5.55 us: across(): lax.ppermute(block, 'band', [(i, other[i // 4] * 4 + i % 4) for i in rang...]
    ppermute x5 -> x6, waiting for transfers between devices: 13.5 us -> 9.02 us  [flipped(): lax.ppermute(block, axis, [(i, i ^ 1 << bit) for i in range(lax.axis_size...]
    all_to_all x1, blocking collectives: 15.3 us -> 13.9 us  [swap(): lax.all_to_all(block, 'head', split_axis=0, concat_axis=0, tiled=True)]
  transfers between devices with their start and end apart: 13 -> 14, of which waited for: 9 -> 9; matrix products, arithmetic and copies ran while one was open for 0% -> 0% of each run, Pallas kernels for 14% -> 15%
where the time goes in v4:
time: 117 us
  starting transfers between devices  38.4 us (33%)
  waiting for transfers between devices  34 us (29%)
  Pallas kernels  28.9 us (25%)
  blocking collectives  13.9 us (12%)
    all_to_all x1, blocking collectives, swap(): lax.all_to_all(block, 'head', split_axis=0, concat_axis=0, tiled=True)  13.9 us
    all_to_all x2, waiting for transfers between devices, swap(): lax.all_to_all(block, 'head', split_axis=0, concat_axis=0, tiled=True)  13.2 us
    ppermute x6, starting transfers between devices, flipped(): lax.ppermute(block, axis, [(i, i ^ 1 << bit) for i in range(lax.axis_size...  9.99 us
    ppermute x2, waiting for transfers between devices, two_over(): lax.ppermute(block, BOTH, [(i, j) for i, j in pairs if 0 <= j < count])  9.17 us
    ppermute x6, waiting for transfers between devices, flipped(): lax.ppermute(block, axis, [(i, i ^ 1 << bit) for i in range(lax.axis_size...  9.02 us
    ppermute x2, starting transfers between devices, two_over(): lax.ppermute(block, BOTH, [(i, j) for i, j in pairs if 0 <= j < count])  8.25 us
    all_to_all x2, starting transfers between devices, swap(): lax.all_to_all(block, 'head', split_axis=0, concat_axis=0, tiled=True)  7.52 us
    pallas_call x1, Pallas kernels, encode(): pl.pallas_call(encode_kernel, in_specs=[HBM] * 6, out_specs=(VMEM,) * 3,...  6.71 us
  transfers between devices with their start and end apart: 14, of which 9 were waited for; matrix products, arithmetic and copies ran while one was open for 0% of the time, Pallas kernels for 15%

profile of v4, /device:TPU:32, one launch (start us, length us, event | category | flops | bytes accessed | tf_op | source)
XLA Modules:
  0.0 117.0 jit_solution(8594747662301252680)
XLA Ops:
  0.6 6.7 %encode.1 = (bf16[160,1152]{1,0:T(8,128)(2,1)S(1)}, bf16[176,1152]{1,0:T(8,128)(2,1)S(1)}, f32[160,1152]{1,0:T(8,128)S(1)}) custom-call(bf16[110,2048]{1,0:T(8,128)(2,1)} %grid_ref.1, s32[1,2048]{1,0:T(1,128)} %bitcast.11, bf16[110,1024]{1,0:T(8,128)(2,1)} %w_hbm.2, f32[1,1024]{1,0:T(1,128)} %bitcast.12, bf16[110,2048]{1,0:T(8,128)(2,1)} %cot_hbm.1, ...), custom_call_target="tpu_custom_call" | custom-call | tf_op jit(solution)/shard_map/encode/pallas_call | solution.py:114
  7.4 1.6 %collective-permute-start = (bf16[176,1152]{1,0:T(8,128)(2,1)S(1)}, bf16[176,1152]{1,0:T(8,128)(2,1)S(1)}, u32[]{:S(2)}, u32[]{:S(2)}) collective-permute-start(bf16[176,1152]{1,0:T(8,128)(2,1)S(1)} %get-tuple-element.24), channel_id=1, source_target_pairs={{0,1},{1,0},{2,3},{3,2},{4,5},{5,4},{6,7},{7,6},{8,9},{9,8},{10,11... | collective-permute-start | bytes 1216520 | tf_op jit(solution)/shard_map/ppermute | solution.py:612
  8.9 5.8 %collective-permute-start.1 = (bf16[160,1152]{1,0:T(8,128)(2,1)S(1)}, bf16[160,1152]{1,0:T(8,128)(2,1)S(1)}, u32[]{:S(2)}, u32[]{:S(2)}) collective-permute-start(bf16[160,1152]{1,0:T(8,128)(2,1)S(1)} %get-tuple-element.25.after_ref), channel_id=1, source_target_pairs={{1,3},{2,0},{3,5},{4,2},{5,7},{6,4},{7,9},{8,6},{9,11},{10,8},{11,... | collective-permute-start | bytes 1105928 | tf_op jit(solution)/shard_map/ppermute | solution.py:618
  14.7 3.1 %load.1 = (bf16[1024,3072]{1,0:T(8,128)(2,1)S(1)}, bf16[128,1024]{1,0:T(8,128)(2,1)S(1)}, bf16[128,128]{1,0:T(8,128)(2,1)}) custom-call(bf16[1024,3072]{1,0:T(8,128)(2,1)} %w_hbm.3, bf16[1024,1024]{1,0:T(8,128)(2,1)} %w_out_ref.1, bf16[110,1024]{1,0:T(8,128)(2,1)} %bitcast.10, bf16[160,1152]{1,0:T(8,128)(2,1)S(1)} %get-tuple-element.25.after_ref), custom_call_target="tpu_custom_call" | custom-call | flops 33554432 | bytes 6291456 | tf_op jit(solution)/shard_map/load/pallas_call | solution.py:155
  17.8 3.1 %collective-permute-done.1.far_ref = bf16[160,1152]{1,0:T(8,128)(2,1)S(1)} collective-permute-done((bf16[160,1152]{1,0:T(8,128)(2,1)S(1)}, bf16[160,1152]{1,0:T(8,128)(2,1)S(1)}, u32[]{:S(2)}, u32[]{:S(2)}) %collective-permute-start.1) | collective-permute-done | bytes 368672 | tf_op jit(solution)/shard_map/ppermute | solution.py:618
  20.9 0.7 collective-permute-done.mid_ref
  21.6 2.2 %project.1 = (bf16[8,160,384]{2,1,0:T(8,128)(2,1)}, f32[160,1024]{1,0:T(8,128)S(1)}, bf16[160,128]{1,0:T(8,128)(2,1)S(1)}) custom-call(f32[160,1152]{1,0:T(8,128)S(1)} %get-tuple-element.23.own_ref, bf16[176,1152]{1,0:T(8,128)(2,1)S(1)} %collective-permute-done.mid_ref, bf16[160,1152]{1,0:T(8,128)(2,1)S(1)} %collective-permute-done.1.far_ref, ...), custom_call_target="tpu_custom_call" | custom-call | tf_op jit(solution)/shard_map/project/pallas_call | solution.py:201
  23.8 3.8 %all-to-all-start = ((bf16[8,160,384]{2,1,0:T(8,128)(2,1)}), bf16[8,160,384]{2,1,0:T(8,128)(2,1)S(1)}, u32[]{:S(2)}, u32[]{:S(2)}) async-start(bf16[8,160,384]{2,1,0:T(8,128)(2,1)} %get-tuple-element.27), calls=%async_computation | async-start | bytes 1966080 | tf_op jit(solution)/shard_map/all_to_all | solution.py:638
  27.6 1.2 %side.1 = (bf16[8,272,128]{2,1,0:T(8,128)(2,1)}, f32[160,128]{1,0:T(8,128)S(1)}) custom-call(f32[160,1024]{1,0:T(8,128)S(1)} %get-tuple-element.28.enc_ref, bf16[160,128]{1,0:T(8,128)(2,1)S(1)} %get-tuple-element.29.s_ref, bf16[128,1024]{1,0:T(8,128)(2,1)S(1)} %get-tuple-element.30.dec_ref), custom_call_target="tpu_custom_call" | custom-call | tf_op jit(solution)/shard_map/side/pallas_call | solution.py:238
  28.8 13.2 %all-to-all-done.qkv_ref = bf16[8,160,384]{2,1,0:T(8,128)(2,1)S(1)} async-done(((bf16[8,160,384]{2,1,0:T(8,128)(2,1)}), bf16[8,160,384]{2,1,0:T(8,128)(2,1)S(1)}, u32[]{:S(2)}, u32[]{:S(2)}) %all-to-all-start) | async-done | bytes 983072 | tf_op jit(solution)/shard_map/all_to_all | solution.py:638
  42.2 1.8 %collective-permute-start.2 = (bf16[4,160,256]{2,1,0:T(8,128)(2,1)S(1)}, bf16[4,160,256]{2,1,0:T(8,128)(2,1)S(1)}, u32[]{:S(2)}, u32[]{:S(2)}) collective-permute-start(bf16[4,160,256]{2,1,0:T(8,128)(2,1)S(1)} %get-tuple-element.45), channel_id=1, source_target_pairs={{0,8},{8,0},{16,24},{24,16},{32,40},{40,32},{48,56},{56,48},{64,72... | collective-permute-start | bytes 983048 | tf_op jit(solution)/shard_map/ppermute | solution.py:628
  44.0 4.2 %collective-permute-start.3 = (bf16[4,160,256]{2,1,0:T(8,128)(2,1)S(1)}, bf16[4,160,256]{2,1,0:T(8,128)(2,1)S(1)}, u32[]{:S(2)}, u32[]{:S(2)}) collective-permute-start(bf16[4,160,256]{2,1,0:T(8,128)(2,1)S(1)} %get-tuple-element.44), channel_id=1, source_target_pairs={{8,16},{16,8},{24,32},{32,24},{40,48},{48,40},{56,64},{64,56},{72,... | collective-permute-start | bytes 983048 | tf_op jit(solution)/shard_map/ppermute | solution.py:624
  48.2 3.7 %all-to-all-start.1 = ((bf16[8,272,128]{2,1,0:T(8,128)(2,1)}), bf16[8,272,128]{2,1,0:T(8,128)(2,1)S(1)}, u32[]{:S(2)}, u32[]{:S(2)}) async-start(bf16[8,272,128]{2,1,0:T(8,128)(2,1)} %get-tuple-element.39), calls=%async_computation.1 | async-start | bytes 1114112 | tf_op jit(solution)/shard_map/all_to_all | solution.py:638
  52.0 6.3 %near.1 = (f32[5,2,80,256]{3,2,1,0:T(8,128)}, f32[5,1,512]{2,1,0:T(1,128)}, bf16[2,1280,128]{2,1,0:T(8,128)(2,1)}) custom-call(bf16[8,160,384]{2,1,0:T(8,128)(2,1)S(1)} %all-to-all-done.qkv_ref, s32[2,1280]{1,0:T(2,128)} %win_hbm.3), custom_call_target="tpu_custom_call" | custom-call | flops 6000000000 | bytes 4000000 | tf_op jit(solution)/shard_map/near/pallas_call | solution.py:334
  58.3 0.7 copy-done.4
  59.1 5.2 %far.1 = (bf16[8,272,128]{2,1,0:T(8,128)(2,1)}, bf16[128,1280]{1,0:T(8,128)(2,1)S(1)}) custom-call(bf16[2,1280,128]{2,1,0:T(8,128)(2,1)} %get-tuple-element.34.q_hbm, f32[5,2,80,256]{3,2,1,0:T(8,128)} %get-tuple-element.35.acc_hbm, f32[5,1,512]{2,1,0:T(1,128)} %get-tuple-element.36.top_hbm, s32[2,1280]{1,0:T(2,128)} %win_hbm.3, ...), custom_call_target="tpu_custom_call" | custom-call | flops 6000000000 | bytes 2000000 | tf_op jit(solution)/shard_map/far/pallas_call | solution.py:435
  64.8 1.4 %collective-permute-start.4 = (f32[112,128]{1,0:T(8,128)S(1)}, f32[112,128]{1,0:T(8,128)S(1)}, u32[]{:S(2)}, u32[]{:S(2)}) collective-permute-start(f32[112,128]{1,0:T(8,128)S(1)} %get-tuple-element.41), channel_id=1, source_target_pairs={{0,8},{8,0},{16,24},{24,16},{32,40},{40,32},{48,56},{56,48},{64,72... | collective-permute-start | bytes 172040 | tf_op jit(solution)/shard_map/ppermute | solution.py:628
  66.1 0.9 collective-permute-done.4
  67.0 2.7 %collective-permute-start.5 = (bf16[112,128]{1,0:T(8,128)(2,1)S(1)}, bf16[112,128]{1,0:T(8,128)(2,1)S(1)}, u32[]{:S(2)}, u32[]{:S(2)}) collective-permute-start(bf16[112,128]{1,0:T(8,128)(2,1)S(1)} %add_convert_fusion.3), channel_id=1, source_target_pairs={{0,16},{8,24},{16,0},{24,8},{32,48},{40,56},{48,32},{56,40},{64,80... | collective-permute-start | bytes 86024 | tf_op jit(solution)/shard_map/ppermute | solution.py:628
  69.7 2.8 %collective-permute-done.5 = bf16[112,128]{1,0:T(8,128)(2,1)S(1)} collective-permute-done((bf16[112,128]{1,0:T(8,128)(2,1)S(1)}, bf16[112,128]{1,0:T(8,128)(2,1)S(1)}, u32[]{:S(2)}, u32[]{:S(2)}) %collective-permute-start.5) | collective-permute-done | bytes 28704 | tf_op jit(solution)/shard_map/ppermute | solution.py:628
  73.0 3.5 %collective-permute-done.6 = bf16[112,128]{1,0:T(8,128)(2,1)S(1)} collective-permute-done((bf16[112,128]{1,0:T(8,128)(2,1)S(1)}, bf16[112,128]{1,0:T(8,128)(2,1)S(1)}, u32[]{:S(2)}, u32[]{:S(2)}) %collective-permute-start.6) | collective-permute-done | bytes 28704 | tf_op jit(solution)/shard_map/ppermute | solution.py:628
  76.5 3.6 %collective-permute-start.7 = (bf16[112,128]{1,0:T(8,128)(2,1)S(1)}, bf16[112,128]{1,0:T(8,128)(2,1)S(1)}, u32[]{:S(2)}, u32[]{:S(2)}) collective-permute-start(bf16[112,128]{1,0:T(8,128)(2,1)S(1)} %add_convert_fusion.1), channel_id=1, source_target_pairs={{0,64},{8,72},{16,80},{24,88},{32,96},{40,104},{48,112},{56,120},{... | collective-permute-start | bytes 86024 | tf_op jit(solution)/shard_map/ppermute | solution.py:628
  80.1 1.9 %collective-permute-done.7 = bf16[112,128]{1,0:T(8,128)(2,1)S(1)} collective-permute-done((bf16[112,128]{1,0:T(8,128)(2,1)S(1)}, bf16[112,128]{1,0:T(8,128)(2,1)S(1)}, u32[]{:S(2)}, u32[]{:S(2)}) %collective-permute-start.7) | collective-permute-done | bytes 28704 | tf_op jit(solution)/shard_map/ppermute | solution.py:628
  81.9 5.5 %collective-permute-start.8 = (bf16[112,128]{1,0:T(8,128)(2,1)S(1)}, bf16[112,128]{1,0:T(8,128)(2,1)S(1)}, u32[]{:S(2)}, u32[]{:S(2)}) collective-permute-start(bf16[112,128]{1,0:T(8,128)(2,1)S(1)} %add_convert_fusion.grad_ref), channel_id=1, source_target_pairs={{0,192},{8,200},{16,208},{24,216},{32,224},{40,232},{48,240},{56,2... | collective-permute-start | bytes 86024 | tf_op jit(solution)/shard_map/ppermute | solution.py:634
  87.5 1.9 %collective-permute-done.8.more_ref = bf16[112,128]{1,0:T(8,128)(2,1)S(1)} collective-permute-done((bf16[112,128]{1,0:T(8,128)(2,1)S(1)}, bf16[112,128]{1,0:T(8,128)(2,1)S(1)}, u32[]{:S(2)}, u32[]{:S(2)}) %collective-permute-start.8) | collective-permute-done | bytes 28704 | tf_op jit(solution)/shard_map/ppermute | solution.py:634
  89.3 0.8 spread.1
  90.1 13.9 %all_to_all.15.parts_ref = bf16[8,272,128]{2,1,0:T(8,128)(2,1)S(1)} all-to-all(bf16[8,272,128]{2,1,0:T(8,128)(2,1)} %spread.1), channel_id=1, replica_groups=mesh['band'=32,'head'=8] {'head'}, dimensions={0} | all-to-all | bytes 1114112 | tf_op jit(solution)/shard_map/all_to_all | solution.py:638
  104.8 2.5 %collective-permute-start.10 = (bf16[160,128]{1,0:T(8,128)(2,1)S(1)}, bf16[160,128]{1,0:T(8,128)(2,1)S(1)}, u32[]{:S(2)}, u32[]{:S(2)}) collective-permute-start(bf16[160,128]{1,0:T(8,128)(2,1)S(1)} %make_table.1.own_ref), channel_id=1, source_target_pairs={{0,2},{2,4},{3,1},{4,6},{5,3},{6,8},{7,5},{8,10},{9,7},{10,12},{11... | collective-permute-start | bytes 122888 | tf_op jit(solution)/shard_map/ppermute | solution.py:618
  107.3 1.4 %collective-permute-start.9 = (bf16[160,128]{1,0:T(8,128)(2,1)S(1)}, bf16[160,128]{1,0:T(8,128)(2,1)S(1)}, u32[]{:S(2)}, u32[]{:S(2)}) collective-permute-start(bf16[160,128]{1,0:T(8,128)(2,1)S(1)} %make_table.1.own_ref), channel_id=1, source_target_pairs={{0,1},{1,0},{2,3},{3,2},{4,5},{5,4},{6,7},{7,6},{8,9},{9,8},{10,11... | collective-permute-start | bytes 122888 | tf_op jit(solution)/shard_map/ppermute | solution.py:612
  108.6 6.1 %collective-permute-done.10.far_ref = bf16[160,128]{1,0:T(8,128)(2,1)S(1)} collective-permute-done((bf16[160,128]{1,0:T(8,128)(2,1)S(1)}, bf16[160,128]{1,0:T(8,128)(2,1)S(1)}, u32[]{:S(2)}, u32[]{:S(2)}) %collective-permute-start.10) | collective-permute-done | bytes 40992 | tf_op jit(solution)/shard_map/ppermute | solution.py:618
  114.7 1.4 %decode.1 = bf16[110,2048]{1,0:T(8,128)(2,1)} custom-call(bf16[160,128]{1,0:T(8,128)(2,1)S(1)} %collective-permute-done.9.mid_ref, bf16[160,128]{1,0:T(8,128)(2,1)S(1)} %collective-permute-done.10.far_ref, bf16[160,128]{1,0:T(8,128)(2,1)S(1)} %make_table.1.own_ref, s32[1,2048]{1,0:T(1,128)S(1)} %bitcast.7, bf16[110,2048]{1,0:T(8,128)(2,1)S(1)} %copy-done.1), custom_call_target="tpu_custom_call" | custom-call | tf_op jit(solution)/shard_map/decode/pallas_call | solution.py:529
  116.2 0.8 add.29
  (27 shorter events, 2.0 us)
Async XLA Ops:
  0.6 20.9 %copy-start.3 = (f32[1024]{0:T(1024)S(1)}, f32[1024]{0:T(1024)}, u32[]{:S(2)}) copy-start(f32[1024]{0:T(1024)} %param.19) | copy-start | bytes 12292
  7.4 14.2 %collective-permute-start = (bf16[176,1152]{1,0:T(8,128)(2,1)S(1)}, bf16[176,1152]{1,0:T(8,128)(2,1)S(1)}, u32[]{:S(2)}, u32[]{:S(2)}) collective-permute-start(bf16[176,1152]{1,0:T(8,128)(2,1)S(1)} %get-tuple-element.24), channel_id=1, source_target_pairs={{0,1},{1,0},{2,3},{3,2},{4,5},{5,4},{6,7},{7,6},{8,9},{9,8},{10,11... | collective-permute-start | bytes 1216520 | tf_op jit(solution)/shard_map/ppermute | solution.py:612
  8.9 11.9 %collective-permute-start.1 = (bf16[160,1152]{1,0:T(8,128)(2,1)S(1)}, bf16[160,1152]{1,0:T(8,128)(2,1)S(1)}, u32[]{:S(2)}, u32[]{:S(2)}) collective-permute-start(bf16[160,1152]{1,0:T(8,128)(2,1)S(1)} %get-tuple-element.25.after_ref), channel_id=1, source_target_pairs={{1,3},{2,0},{3,5},{4,2},{5,7},{6,4},{7,9},{8,6},{9,11},{10,8},{11,... | collective-permute-start | bytes 1105928 | tf_op jit(solution)/shard_map/ppermute | solution.py:618
  23.8 18.3 %all-to-all-start = ((bf16[8,160,384]{2,1,0:T(8,128)(2,1)}), bf16[8,160,384]{2,1,0:T(8,128)(2,1)S(1)}, u32[]{:S(2)}, u32[]{:S(2)}) async-start(bf16[8,160,384]{2,1,0:T(8,128)(2,1)} %get-tuple-element.27), calls=%async_computation | async-start | bytes 1966080 | tf_op jit(solution)/shard_map/all_to_all | solution.py:638
  42.2 16.0 %collective-permute-start.2 = (bf16[4,160,256]{2,1,0:T(8,128)(2,1)S(1)}, bf16[4,160,256]{2,1,0:T(8,128)(2,1)S(1)}, u32[]{:S(2)}, u32[]{:S(2)}) collective-permute-start(bf16[4,160,256]{2,1,0:T(8,128)(2,1)S(1)} %get-tuple-element.45), channel_id=1, source_target_pairs={{0,8},{8,0},{16,24},{24,16},{32,40},{40,32},{48,56},{56,48},{64,72... | collective-permute-start | bytes 983048 | tf_op jit(solution)/shard_map/ppermute | solution.py:628
  44.0 14.2 %collective-permute-start.3 = (bf16[4,160,256]{2,1,0:T(8,128)(2,1)S(1)}, bf16[4,160,256]{2,1,0:T(8,128)(2,1)S(1)}, u32[]{:S(2)}, u32[]{:S(2)}) collective-permute-start(bf16[4,160,256]{2,1,0:T(8,128)(2,1)S(1)} %get-tuple-element.44), channel_id=1, source_target_pairs={{8,16},{16,8},{24,32},{32,24},{40,48},{48,40},{56,64},{64,56},{72,... | collective-permute-start | bytes 983048 | tf_op jit(solution)/shard_map/ppermute | solution.py:624
  48.2 16.1 %all-to-all-start.1 = ((bf16[8,272,128]{2,1,0:T(8,128)(2,1)}), bf16[8,272,128]{2,1,0:T(8,128)(2,1)S(1)}, u32[]{:S(2)}, u32[]{:S(2)}) async-start(bf16[8,272,128]{2,1,0:T(8,128)(2,1)} %get-tuple-element.39), calls=%async_computation.1 | async-start | bytes 1114112 | tf_op jit(solution)/shard_map/all_to_all | solution.py:638
  58.2 0.7 copy-start.4
  58.2 0.8 copy-start.5
  59.1 44.9 %copy-start = (bf16[1024,1024]{1,0:T(8,128)(2,1)S(1)}, bf16[1024,1024]{1,0:T(8,128)(2,1)}, u32[]{:S(2)}) copy-start(bf16[1024,1024]{1,0:T(8,128)(2,1)} %w_out_ref.1) | copy-start | bytes 6291460
  64.3 50.5 %copy-start.1 = (bf16[110,2048]{1,0:T(8,128)(2,1)S(1)}, bf16[110,2048]{1,0:T(8,128)(2,1)}, u32[]{:S(2)}) copy-start(bf16[110,2048]{1,0:T(8,128)(2,1)} %grid_ref.1) | copy-start | bytes 1351684
  64.3 50.5 %copy-start.2 = (s32[2048]{0:T(1024)S(1)}, s32[2048]{0:T(1024)}, u32[]{:S(2)}) copy-start(s32[2048]{0:T(1024)} %param.13) | copy-start | bytes 24580
  64.8 2.3 %collective-permute-start.4 = (f32[112,128]{1,0:T(8,128)S(1)}, f32[112,128]{1,0:T(8,128)S(1)}, u32[]{:S(2)}, u32[]{:S(2)}) collective-permute-start(f32[112,128]{1,0:T(8,128)S(1)} %get-tuple-element.41), channel_id=1, source_target_pairs={{0,8},{8,0},{16,24},{24,16},{32,40},{40,32},{48,56},{56,48},{64,72... | collective-permute-start | bytes 172040 | tf_op jit(solution)/shard_map/ppermute | solution.py:628
  67.0 5.5 %collective-permute-start.5 = (bf16[112,128]{1,0:T(8,128)(2,1)S(1)}, bf16[112,128]{1,0:T(8,128)(2,1)S(1)}, u32[]{:S(2)}, u32[]{:S(2)}) collective-permute-start(bf16[112,128]{1,0:T(8,128)(2,1)S(1)} %add_convert_fusion.3), channel_id=1, source_target_pairs={{0,16},{8,24},{16,0},{24,8},{32,48},{40,56},{48,32},{56,40},{64,80... | collective-permute-start | bytes 86024 | tf_op jit(solution)/shard_map/ppermute | solution.py:628
  72.5 4.0 %collective-permute-start.6 = (bf16[112,128]{1,0:T(8,128)(2,1)S(1)}, bf16[112,128]{1,0:T(8,128)(2,1)S(1)}, u32[]{:S(2)}, u32[]{:S(2)}) collective-permute-start(bf16[112,128]{1,0:T(8,128)(2,1)S(1)} %add_convert_fusion.2), channel_id=1, source_target_pairs={{0,32},{8,40},{16,48},{24,56},{32,0},{40,8},{48,16},{56,24},{64,96... | collective-permute-start | bytes 86024 | tf_op jit(solution)/shard_map/ppermute | solution.py:628
  76.5 5.4 %collective-permute-start.7 = (bf16[112,128]{1,0:T(8,128)(2,1)S(1)}, bf16[112,128]{1,0:T(8,128)(2,1)S(1)}, u32[]{:S(2)}, u32[]{:S(2)}) collective-permute-start(bf16[112,128]{1,0:T(8,128)(2,1)S(1)} %add_convert_fusion.1), channel_id=1, source_target_pairs={{0,64},{8,72},{16,80},{24,88},{32,96},{40,104},{48,112},{56,120},{... | collective-permute-start | bytes 86024 | tf_op jit(solution)/shard_map/ppermute | solution.py:628
  81.9 7.4 %collective-permute-start.8 = (bf16[112,128]{1,0:T(8,128)(2,1)S(1)}, bf16[112,128]{1,0:T(8,128)(2,1)S(1)}, u32[]{:S(2)}, u32[]{:S(2)}) collective-permute-start(bf16[112,128]{1,0:T(8,128)(2,1)S(1)} %add_convert_fusion.grad_ref), channel_id=1, source_target_pairs={{0,192},{8,200},{16,208},{24,216},{32,224},{40,232},{48,240},{56,2... | collective-permute-start | bytes 86024 | tf_op jit(solution)/shard_map/ppermute | solution.py:634
  104.6 11.5 %collective-permute-start.11 = (f32[112,1024]{1,0:T(8,128)S(1)}, f32[112,1024]{1,0:T(8,128)S(1)}, u32[]{:S(2)}, u32[]{:S(2)}) collective-permute-start(f32[112,1024]{1,0:T(8,128)S(1)} %gradient_half.1.mine_ref), channel_id=1, source_target_pairs={{0,8},{8,0},{16,24},{24,16},{32,40},{40,32},{48,56},{56,48},{64,72... | collective-permute-start | bytes 1376264 | tf_op jit(solution)/shard_map/ppermute | solution.py:628
  104.8 9.9 %collective-permute-start.10 = (bf16[160,128]{1,0:T(8,128)(2,1)S(1)}, bf16[160,128]{1,0:T(8,128)(2,1)S(1)}, u32[]{:S(2)}, u32[]{:S(2)}) collective-permute-start(bf16[160,128]{1,0:T(8,128)(2,1)S(1)} %make_table.1.own_ref), channel_id=1, source_target_pairs={{0,2},{2,4},{3,1},{4,6},{5,3},{6,8},{7,5},{8,10},{9,7},{10,12},{11... | collective-permute-start | bytes 122888 | tf_op jit(solution)/shard_map/ppermute | solution.py:618
  107.3 7.5 %collective-permute-start.9 = (bf16[160,128]{1,0:T(8,128)(2,1)S(1)}, bf16[160,128]{1,0:T(8,128)(2,1)S(1)}, u32[]{:S(2)}, u32[]{:S(2)}) collective-permute-start(bf16[160,128]{1,0:T(8,128)(2,1)S(1)} %make_table.1.own_ref), channel_id=1, source_target_pairs={{0,1},{1,0},{2,3},{3,2},{4,5},{5,4},{6,7},{7,6},{8,9},{9,8},{10,11... | collective-permute-start | bytes 122888 | tf_op jit(solution)/shard_map/ppermute | solution.py:612

commit v5 on v4

--- a/solution.py
+++ b/solution.py
@@ -55,125 +55,137 @@
     return (index - side) * NODE_DEV, index * NODE_DEV, (index + side) * NODE_DEV
 
 
-def encode_kernel(grid_hbm, enc_hbm, w_hbm, b_hbm, cot_hbm, dec_hbm, far_ref, mid_ref, own_ref,
-                  grid_ref, enc_ref, w_ref, b_ref, cot_ref, dec_ref, rows_ref, w_pad, cot_pad, pick_ref, sem):
-    channels, points = grid_ref.shape
+def fill_pick(pick_ref, target):
+    nodes, points = NODE_DEV, pick_ref.shape[1]
+    node_id = lax.broadcasted_iota(jnp.int32, (nodes, points), 0)
+    for at, base in enumerate(chunk_bases()):
+        pick_ref[at * nodes : (at + 1) * nodes, :] = jnp.where(node_id == target - base, 1.0, 0.0).astype(BF)
+
+
+def encode_kernel(grid_hbm, enc_hbm, w_hbm, b_hbm, far_ref, mid_ref, own_ref,
+                  grid_ref, enc_ref, w_ref, b_ref, w_half, pick_ref, sem):
     model = w_ref.shape[1]
     nodes = NODE_DEV
     copies = started(
         [
             pltpu.make_async_copy(source, target, sem.at[at])
             for at, (source, target) in enumerate(
-                [(grid_hbm, grid_ref), (enc_hbm, enc_ref), (w_hbm, w_ref), (b_hbm, b_ref), (cot_hbm, cot_ref), (dec_hbm, dec_ref)]
+                [(grid_hbm, grid_ref), (enc_hbm, enc_ref), (w_hbm, w_ref), (b_hbm, b_ref)]
             )
         ]
     )
-    bases = chunk_bases()
-    node_id = lax.broadcasted_iota(jnp.int32, (nodes, points), 0)
-
-    def pick(target):
-        for at, base in enumerate(bases):
-            pick_ref[at * nodes : (at + 1) * nodes, :] = jnp.where(node_id == target - base, 1.0, 0.0).astype(BF)
-
     copies[1].wait()
-    pick(enc_ref[...])
+    fill_pick(pick_ref, enc_ref[...])
+    copies[2].wait()
+    w_half[...] = (w_ref[...].astype(F32) * 0.5).astype(BF)
     copies[0].wait()
-    padded = jnp.concatenate(
-        [grid_ref[...].astype(F32), jnp.zeros((LANES - channels, points), F32)], axis=0
-    )
-    rows_ref[...] = padded.T.astype(BF)
-    copies[2].wait()
     copies[3].wait()
-    w_pad[...] = jnp.zeros_like(w_pad)
-    w_pad[:channels, :] = (w_ref[...].astype(F32) * 0.5).astype(BF)
-    width = 256
+    width = 512
+    mid_ref[nodes:, :] = jnp.zeros((EXTRA, model), BF)
     for at in range(0, model, width):
-        half = dot(rows_ref[...], w_pad[:, at : at + width], 1, 0) + b_ref[:, at : at + width] * 0.5
+        half = dot(grid_ref[...], w_half[:, at : at + width], 0, 0) + b_ref[:, at : at + width] * 0.5
         message = (half + half * jnp.tanh(half)).astype(BF)
         spread = dot(pick_ref[...], message, 1, 0)
         far_ref[:, at : at + width] = spread[:nodes].astype(BF)
         mid_ref[:nodes, at : at + width] = spread[nodes : 2 * nodes].astype(BF)
         own_ref[:, at : at + width] = spread[2 * nodes :]
-    copies[4].wait()
-    copies[5].wait()
+
+
+def encode(grid_in, enc_row, w_in, b_row):
+    points = grid_in.shape[1]
+    model = w_in.shape[1]
+    operands = (grid_in, enc_row, w_in, b_row)
+    return pl.pallas_call(
+        encode_kernel,
+        in_specs=[HBM] * 4,
+        out_specs=(VMEM,) * 3,
+        out_shape=(shape((NODE_DEV, model), BF), shape((NODE_DEV + EXTRA, model), BF), shape((NODE_DEV, model), F32)),
+        scratch_shapes=[pltpu.VMEM(a.shape, a.dtype) for a in operands]
+        + [
+            pltpu.VMEM(w_in.shape, BF),
+            pltpu.VMEM((3 * NODE_DEV, points), BF),
+            pltpu.SemaphoreType.DMA((4,)),
+        ],
+        compiler_params=params(),
+        name="encode",
+    )(*pinned(*operands))
+
+
+def prepare_kernel(w_hbm, out_hbm, dec_hbm, cot_hbm, target_hbm, after_ref,
+                   w_ref, pad_ref, mix_hbm, far_ref, mid_ref, own_ref,
+                   mix_ref, out_rows, dec_rows, cot_ref, target_ref, cot_pad, pick_ref, sem):
+    channels = dec_rows.shape[0]
+    nodes = NODE_DEV
+    at = pl.multiple_of(lax.axis_index("head") * LANES, LANES)
+    copies = started(
+        [
+            pltpu.make_async_copy(source, target, sem.at[number])
+            for number, (source, target) in enumerate(
+                [
+                    (target_hbm, target_ref),
+                    (cot_hbm, cot_ref),
+                    (dec_hbm, dec_rows),
+                    (out_hbm.at[pl.ds(at, LANES), :], out_rows),
+                    (w_hbm, w_ref),
+                ]
+            )
+        ]
+    )
+    copies[0].wait()
+    fill_pick(pick_ref, target_ref[...])
+    copies[1].wait()
     cot_pad[...] = jnp.zeros_like(cot_pad)
     cot_pad[:channels, :] = cot_ref[...]
-    pick(dec_ref[...])
     spread = dot(pick_ref[...], cot_pad[...], 1, 1)
-    far_ref[:, model:] = spread[:nodes].astype(BF)
-    mid_ref[nodes:, :] = jnp.zeros((EXTRA, mid_ref.shape[1]), BF)
-    mid_ref[:nodes, model:] = spread[nodes : 2 * nodes].astype(BF)
-    own_ref[:, model:] = spread[2 * nodes :]
-
-
-def encode(grid_in, enc_row, w_in, b_row, cotangent, dec_row):
-    channels, points = grid_in.shape
-    model = w_in.shape[1]
-    wide = model + LANES
-    operands = (grid_in, enc_row, w_in, b_row, cotangent, dec_row)
-    return pl.pallas_call(
-        encode_kernel,
-        in_specs=[HBM] * 6,
-        out_specs=(VMEM,) * 3,
-        out_shape=(shape((NODE_DEV, wide), BF), shape((NODE_DEV + EXTRA, wide), BF), shape((NODE_DEV, wide), F32)),
-        scratch_shapes=[pltpu.VMEM(a.shape, a.dtype) for a in operands]
-        + [
-            pltpu.VMEM((points, LANES), BF),
+    far_ref[...] = spread[:nodes].astype(BF)
+    mid_ref[...] = spread[nodes : 2 * nodes].astype(BF)
+    own_ref[...] = spread[2 * nodes :]
+    copies[2].wait()
+    pad_ref[...] = jnp.zeros_like(pad_ref)
+    pad_ref[:channels, :] = dec_rows[...]
+    copies[3].wait()
+    mix_ref[...] = dot(out_rows[...], pad_ref[...], 1, 1).astype(BF)
+    copy = pltpu.make_async_copy(mix_ref, mix_hbm, sem.at[len(copies)])
+    copy.start()
+    copy.wait()
+    copies[4].wait()
+
+
+def prepare(w_qkv, w_out, dec_cols, cotangent, dec_row, after):
+    model = w_qkv.shape[0]
+    points = cotangent.shape[1]
+    part = (NODE_DEV, LANES)
+    return pl.pallas_call(
+        prepare_kernel,
+        in_specs=[HBM] * 5 + [pl.BlockSpec(memory_space=pl.ANY)],
+        out_specs=(VMEM, VMEM, HBM, VMEM, VMEM, VMEM),
+        out_shape=(
+            shape(w_qkv.shape, BF),
+            shape((LANES, model), BF),
+            in_hbm(shape((LANES, LANES), BF)),
+            shape(part, BF),
+            shape(part, BF),
+            shape(part, F32),
+        ),
+        scratch_shapes=[
+            pltpu.VMEM((LANES, LANES), BF),
             pltpu.VMEM((LANES, model), BF),
+            pltpu.VMEM(dec_cols.shape, BF),
+            pltpu.VMEM(cotangent.shape, BF),
+            pltpu.VMEM(dec_row.shape, jnp.int32),
             pltpu.VMEM((LANES, points), BF),
             pltpu.VMEM((3 * NODE_DEV, points), BF),
             pltpu.SemaphoreType.DMA((6,)),
         ],
         compiler_params=params(),
-        name="encode",
-    )(*pinned(*operands))
-
-
-def load_kernel(w_hbm, out_hbm, dec_hbm, after_ref, w_ref, dec_ref, mix_hbm, mix_ref, out_rows, dec_rows, sem):
-    channels = dec_rows.shape[0]
-    at = pl.multiple_of(lax.axis_index("head") * LANES, LANES)
-    copies = started(
-        [
-            pltpu.make_async_copy(out_hbm.at[pl.ds(at, LANES), :], out_rows, sem.at[0]),
-            pltpu.make_async_copy(dec_hbm, dec_rows, sem.at[1]),
-            pltpu.make_async_copy(w_hbm, w_ref, sem.at[2]),
-        ]
-    )
-    copies[0].wait()
-    copies[1].wait()
-    dec_ref[...] = jnp.zeros_like(dec_ref)
-    dec_ref[:channels, :] = dec_rows[...]
-    mix_ref[...] = dot(out_rows[...], dec_ref[...], 1, 1).astype(BF)
-    copy = pltpu.make_async_copy(mix_ref, mix_hbm, sem.at[3])
-    copy.start()
-    copy.wait()
-    copies[2].wait()
-
-
-def load(w_qkv, w_out, dec_cols, after):
-    model = w_qkv.shape[0]
-    return pl.pallas_call(
-        load_kernel,
-        in_specs=[HBM] * 3 + [pl.BlockSpec(memory_space=pl.ANY)],
-        out_specs=(VMEM, VMEM, HBM),
-        out_shape=(shape(w_qkv.shape, BF), shape((LANES, model), BF), in_hbm(shape((LANES, LANES), BF))),
-        scratch_shapes=[
-            pltpu.VMEM((LANES, LANES), BF),
-            pltpu.VMEM((LANES, model), BF),
-            pltpu.VMEM(dec_cols.shape, BF),
-            pltpu.SemaphoreType.DMA((4,)),
-        ],
-        compiler_params=params(),
-        cost_estimate=pl.CostEstimate(flops=2 * model * LANES * LANES, bytes_accessed=2 * w_qkv.size, transcendentals=0),
-        name="load",
-    )(*pinned(w_qkv, w_out, dec_cols), after)
-
-
-def project_kernel(own_ref, mid_ref, far_ref, gain_ref, w_ref, packed_hbm, enc_ref, s_ref, packed, sem):
+        cost_estimate=pl.CostEstimate(flops=500_000_000, bytes_accessed=2 * w_qkv.size, transcendentals=0),
+        name="prepare",
+    )(*pinned(w_qkv, w_out, dec_cols, cotangent, dec_row), after)
+
+
+def project_kernel(own_ref, mid_ref, far_ref, gain_ref, w_ref, packed_hbm, enc_ref, packed, sem):
     model = gain_ref.shape[1]
-    total = own_ref[...] + mid_ref[:NODE_DEV].astype(F32) + far_ref[...].astype(F32)
-    enc = total[:, :model]
-    s_ref[...] = total[:, model:].astype(BF)
+    enc = own_ref[...] + mid_ref[:NODE_DEV].astype(F32) + far_ref[...].astype(F32)
     enc_ref[...] = enc
     centred = enc - jnp.mean(enc, axis=1, keepdims=True)
     spread_sq = jnp.mean(centred * centred, axis=1, keepdims=True)
@@ -201,11 +213,10 @@
     return pl.pallas_call(
         project_kernel,
         in_specs=[VMEM] * 5,
-        out_specs=(HBM, VMEM, VMEM),
+        out_specs=(HBM, VMEM),
         out_shape=(
             in_hbm(shape((groups, NODE_DEV, 3 * LANES), BF)),
             shape((NODE_DEV, model), F32),
-            shape((NODE_DEV, LANES), BF),
         ),
         scratch_shapes=[
             pltpu.VMEM((groups, NODE_DEV, 3 * LANES), BF),
@@ -216,10 +227,10 @@
     )(own, mid, far, gain_row, w_qkv)
 
 
-def side_kernel(enc_ref, s_ref, dec_ref, send_hbm, node_ref, send, sem):
+def side_kernel(enc_ref, own_ref, mid_ref, far_ref, dec_ref, send_hbm, node_ref, send, sem):
     groups = send.shape[0]
     enc = enc_ref[...]
-    summed = s_ref[...]
+    summed = (own_ref[...] + mid_ref[...].astype(F32) + far_ref[...].astype(F32)).astype(BF)
     high = enc.astype(BF)
     low = (enc - high.astype(F32)).astype(BF)
     node_ref[...] = dot(high, dec_ref[...], 1, 1)
@@ -232,18 +243,18 @@
     copy.wait()
 
 
-def side(enc, summed, dec_pad):
+def side(enc, own, mid, far, dec_pad):
     groups = enc.shape[1] // LANES
     send_shape = (groups, NODE_DEV + ROWS, LANES)
     return pl.pallas_call(
         side_kernel,
-        in_specs=[VMEM] * 3,
+        in_specs=[VMEM] * 5,
         out_specs=(HBM, VMEM),
         out_shape=(in_hbm(shape(send_shape, BF)), shape((NODE_DEV, LANES), F32)),
         scratch_shapes=[pltpu.VMEM(send_shape, BF), pltpu.SemaphoreType.DMA],
         compiler_params=params(),
         name="side",
-    )(enc, summed, dec_pad)
+    )(enc, own, mid, far, dec_pad)
 
 
 def limits(win, reach, start, first_node, node_total):
@@ -644,13 +655,18 @@
     channels = grid_in.shape[0]
     groups = lax.axis_size("head")
     dec_row = dec_node[None]
-    far_part, mid_part, own = encode(grid_in, enc_node[None], w_in, b_in[None], cotangent, dec_row)
-    weights, dec_pad, mix = load(w_qkv, w_out, w_dec.T, far_part)
+    far_part, mid_part, own = encode(grid_in, enc_node[None], w_in, b_in[None])
+    weights, dec_pad, mix, far_sum, mid_sum, own_sum = prepare(
+        w_qkv, w_out, w_dec.T, cotangent, dec_row, far_part
+    )
     mid_in = to_partner(mid_part)
     far_in = two_over(far_part, -1)
-    packed, enc, summed = project(own, mid_in, far_in, norm_gain[None], weights)
+    mid_sum = to_partner(mid_sum)
+    far_sum = two_over(far_sum, -1)
+    packed, enc = project(own, mid_in, far_in, norm_gain[None], weights)
+    packed, mid_sum, far_sum = lax.optimization_barrier((packed, mid_sum, far_sum))
     qkv = swap(packed)
-    send, node = side(enc, summed, dec_pad)
+    send, node = side(enc, own_sum, mid_sum, far_sum, dec_pad)
     qkv, send, node = lax.optimization_barrier((qkv, send, node))
     half = groups // 2
     reach = half * NODE_DEV
@@ -668,8 +684,9 @@
     parts = swap(spread(grad, across(grad), parts))
     table = make_table(parts, node)
     half_grad = gradient_half(parts, w_out)
-    prediction = decode(two_over(table, 1), to_partner(table), table, dec_row, grid_in)
     grad_dec = add(half_grad, flipped(half_grad, "band", 0), channels)
+    grad_dec, mid_rows = lax.optimization_barrier((grad_dec, to_partner(table)))
+    prediction = decode(two_over(table, 1), mid_rows, table, dec_row, grid_in)
     return (prediction, grad_dec.T)
 
 

time: 117 us -> 117 us (level)
  starting transfers between devices: 38.4 us -> 41.7 us
  waiting for transfers between devices: 34 us -> 31.6 us
  Pallas kernels: 28.9 us -> 27.2 us
    ppermute x2 -> x3, starting transfers between devices: 8.25 us -> 13.4 us  [two_over(): lax.ppermute(block, BOTH, [(i, j) for i, j in pairs if 0 <= j < count])]
    ppermute x2 -> x3, waiting for transfers between devices: 9.17 us -> 6.48 us  [two_over(): lax.ppermute(block, BOTH, [(i, j) for i, j in pairs if 0 <= j < count])]
    ppermute x6, starting transfers between devices: 9.99 us -> 7.33 us  [flipped(): lax.ppermute(block, axis, [(i, i ^ 1 << bit) for i in range(lax.axis_size...]
    all_to_all x2, starting transfers between devices: 7.52 us -> 9.49 us  [swap(): lax.all_to_all(block, 'head', split_axis=0, concat_axis=0, tiled=True)]
    pallas_call x4, Pallas kernels: 13.2 us -> 11.5 us  [the longest x1 4.94 us: encode(): pl.pallas_call(encode_kernel, in_specs=[HBM] * 4, out_specs=(VMEM,) * 3,...]
    ppermute x6, waiting for transfers between devices: 9.02 us -> 10.6 us  [flipped(): lax.ppermute(block, axis, [(i, i ^ 1 << bit) for i in range(lax.axis_size...]
    ppermute x2 -> x3, starting transfers between devices: 2.93 us -> 2.41 us  [to_partner(): lax.ppermute(block, BOTH, [(i, i ^ 1) for i in range(total_devices())])]
  transfers between devices with their start and end apart: 14 -> 16, of which waited for: 9 -> 7; matrix products, arithmetic and copies ran while one was open for 0% -> 0% of each run, Pallas kernels for 15% -> 16%
where the time goes in v5:
time: 117 us; the launch traced here: 116 us
  starting transfers between devices  41.7 us (36%)
  waiting for transfers between devices  31.6 us (27%)
  Pallas kernels  27.2 us (23%)
  blocking collectives  14 us (12%)
    all_to_all x1, blocking collectives, swap(): lax.all_to_all(block, 'head', split_axis=0, concat_axis=0, tiled=True)  14 us
    ppermute x3, starting transfers between devices, two_over(): lax.ppermute(block, BOTH, [(i, j) for i, j in pairs if 0 <= j < count])  13.4 us
    all_to_all x2, waiting for transfers between devices, swap(): lax.all_to_all(block, 'head', split_axis=0, concat_axis=0, tiled=True)  12.6 us
    ppermute x6, waiting for transfers between devices, flipped(): lax.ppermute(block, axis, [(i, i ^ 1 << bit) for i in range(lax.axis_size...  10.6 us
    all_to_all x2, starting transfers between devices, swap(): lax.all_to_all(block, 'head', split_axis=0, concat_axis=0, tiled=True)  9.49 us
    ppermute x6, starting transfers between devices, flipped(): lax.ppermute(block, axis, [(i, i ^ 1 << bit) for i in range(lax.axis_size...  7.33 us
    ppermute x3, waiting for transfers between devices, two_over(): lax.ppermute(block, BOTH, [(i, j) for i, j in pairs if 0 <= j < count])  6.48 us
    pallas_call x1, Pallas kernels, near(): pl.pallas_call(functools.partial(near_kernel, reach), in_specs=[VMEM, HBM...  6.27 us
  transfers between devices with their start and end apart: 16, of which 7 were waited for; matrix products, arithmetic and copies ran while one was open for 0% of the time, Pallas kernels for 16%

profile of v5, /device:TPU:32, one launch (start us, length us, event | category | flops | bytes accessed | tf_op | source)
XLA Modules:
  0.0 116.4 jit_solution(9925070323467219659)
XLA Ops:
  0.6 4.9 %encode.1 = (bf16[160,1024]{1,0:T(8,128)(2,1)S(1)}, bf16[176,1024]{1,0:T(8,128)(2,1)S(1)}, f32[160,1024]{1,0:T(8,128)S(1)}) custom-call(bf16[110,2048]{1,0:T(8,128)(2,1)} %grid_ref.1, s32[1,2048]{1,0:T(1,128)} %bitcast.11, bf16[110,1024]{1,0:T(8,128)(2,1)} %w_hbm.2, f32[1,1024]{1,0:T(1,128)} %bitcast.12), custom_call_target="tpu_custom_call" | custom-call | tf_op jit(solution)/shard_map/encode/pallas_call | solution.py:98
  5.6 1.6 %collective-permute-start = (bf16[176,1024]{1,0:T(8,128)(2,1)S(1)}, bf16[176,1024]{1,0:T(8,128)(2,1)S(1)}, u32[]{:S(2)}, u32[]{:S(2)}) collective-permute-start(bf16[176,1024]{1,0:T(8,128)(2,1)S(1)} %get-tuple-element.31), channel_id=1, source_target_pairs={{0,1},{1,0},{2,3},{3,2},{4,5},{5,4},{6,7},{7,6},{8,9},{9,8},{10,11... | collective-permute-start | bytes 1081352 | tf_op jit(solution)/shard_map/ppermute | solution.py:623
  7.2 5.8 %collective-permute-start.1 = (bf16[160,1024]{1,0:T(8,128)(2,1)S(1)}, bf16[160,1024]{1,0:T(8,128)(2,1)S(1)}, u32[]{:S(2)}, u32[]{:S(2)}) collective-permute-start(bf16[160,1024]{1,0:T(8,128)(2,1)S(1)} %get-tuple-element.32.after_ref), channel_id=1, source_target_pairs={{1,3},{2,0},{3,5},{4,2},{5,7},{6,4},{7,9},{8,6},{9,11},{10,8},{11,... | collective-permute-start | bytes 983048 | tf_op jit(solution)/shard_map/ppermute | solution.py:629
  13.0 3.2 %prepare.1 = (bf16[1024,3072]{1,0:T(8,128)(2,1)S(1)}, bf16[128,1024]{1,0:T(8,128)(2,1)S(1)}, bf16[128,128]{1,0:T(8,128)(2,1)}, bf16[160,128]{1,0:T(8,128)(2,1)S(...) custom-call(bf16[1024,3072]{1,0:T(8,128)(2,1)} %w_hbm.3, bf16[1024,1024]{1,0:T(8,128)(2,1)} %w_out_ref.1, ...), custom_call_target="tpu_custom_call" | custom-call | flops 500000000 | bytes 6291456 | tf_op jit(solution)/shard_map/prepare/pallas_call | solution.py:158
  16.3 5.1 %collective-permute-start.3 = (bf16[160,128]{1,0:T(8,128)(2,1)S(1)}, bf16[160,128]{1,0:T(8,128)(2,1)S(1)}, u32[]{:S(2)}, u32[]{:S(2)}) collective-permute-start(bf16[160,128]{1,0:T(8,128)(2,1)S(1)} %get-tuple-element.36), channel_id=1, source_target_pairs={{1,3},{2,0},{3,5},{4,2},{5,7},{6,4},{7,9},{8,6},{9,11},{10,8},{11,... | collective-permute-start | bytes 122888 | tf_op jit(solution)/shard_map/ppermute | solution.py:629
  21.4 2.2 %project.1 = (bf16[8,160,384]{2,1,0:T(8,128)(2,1)}, f32[160,1024]{1,0:T(8,128)S(1)}) custom-call(f32[160,1024]{1,0:T(8,128)S(1)} %get-tuple-element.30.own_ref, bf16[176,1024]{1,0:T(8,128)(2,1)S(1)} %collective-permute-done.mid_ref, bf16[160,1024]{1,0:T(8,128)(2,1)S(1)} %collective-permute-done.1.far_ref, f32[1,1024]{1,0:T(1,128)S(1)} %bitcast.8, ...), custom_call_target="tpu_custom_call" | custom-call | tf_op jit(solution)/shard_map/project/pallas_call | solution.py:213
  23.6 5.8 %all-to-all-start = ((bf16[8,160,384]{2,1,0:T(8,128)(2,1)}), bf16[8,160,384]{2,1,0:T(8,128)(2,1)S(1)}, u32[]{:S(2)}, u32[]{:S(2)}) async-start(bf16[8,160,384]{2,1,0:T(8,128)(2,1)} %get-tuple-element.37), calls=%async_computation | async-start | bytes 1966080 | tf_op jit(solution)/shard_map/all_to_all | solution.py:649
  29.4 1.2 %side.1 = (bf16[8,272,128]{2,1,0:T(8,128)(2,1)}, f32[160,128]{1,0:T(8,128)S(1)}) custom-call(f32[160,1024]{1,0:T(8,128)S(1)} %get-tuple-element.38.enc_ref, f32[160,128]{1,0:T(8,128)S(1)} %get-tuple-element.39.own_ref, bf16[160,128]{1,0:T(8,128)(2,1)S(1)} %collective-permute-done.2.mid_ref, bf16[160,128]{1,0:T(8,128)(2,1)S(1)} %collective-permute-done.3.far_ref, ...), custom_call_target="tpu_custom_call" | custom-call | tf_op jit(solution)/shard_map/side/pallas_call | solution.py:249
  30.6 12.6 %all-to-all-done.qkv_ref = bf16[8,160,384]{2,1,0:T(8,128)(2,1)S(1)} async-done(((bf16[8,160,384]{2,1,0:T(8,128)(2,1)}), bf16[8,160,384]{2,1,0:T(8,128)(2,1)S(1)}, u32[]{:S(2)}, u32[]{:S(2)}) %all-to-all-start) | async-done | bytes 983072 | tf_op jit(solution)/shard_map/all_to_all | solution.py:649
  43.5 3.9 %collective-permute-start.5 = (bf16[4,160,256]{2,1,0:T(8,128)(2,1)S(1)}, bf16[4,160,256]{2,1,0:T(8,128)(2,1)S(1)}, u32[]{:S(2)}, u32[]{:S(2)}) collective-permute-start(bf16[4,160,256]{2,1,0:T(8,128)(2,1)S(1)} %get-tuple-element.58), channel_id=1, source_target_pairs={{8,16},{16,8},{24,32},{32,24},{40,48},{48,40},{56,64},{64,56},{72,... | collective-permute-start | bytes 983048 | tf_op jit(solution)/shard_map/ppermute | solution.py:635
  47.4 3.7 %all-to-all-start.1 = ((bf16[8,272,128]{2,1,0:T(8,128)(2,1)}), bf16[8,272,128]{2,1,0:T(8,128)(2,1)S(1)}, u32[]{:S(2)}, u32[]{:S(2)}) async-start(bf16[8,272,128]{2,1,0:T(8,128)(2,1)} %get-tuple-element.51), calls=%async_computation.1 | async-start | bytes 1114112 | tf_op jit(solution)/shard_map/all_to_all | solution.py:649
  51.1 6.3 %near.1 = (f32[5,2,80,256]{3,2,1,0:T(8,128)}, f32[5,1,512]{2,1,0:T(1,128)}, bf16[2,1280,128]{2,1,0:T(8,128)(2,1)}) custom-call(bf16[8,160,384]{2,1,0:T(8,128)(2,1)S(1)} %all-to-all-done.qkv_ref, s32[2,1280]{1,0:T(2,128)} %win_hbm.3), custom_call_target="tpu_custom_call" | custom-call | flops 6000000000 | bytes 4000000 | tf_op jit(solution)/shard_map/near/pallas_call | solution.py:345
  57.5 0.7 copy-done.4
  58.3 5.2 %far.1 = (bf16[8,272,128]{2,1,0:T(8,128)(2,1)}, bf16[128,1280]{1,0:T(8,128)(2,1)S(1)}) custom-call(bf16[2,1280,128]{2,1,0:T(8,128)(2,1)} %get-tuple-element.46.q_hbm, f32[5,2,80,256]{3,2,1,0:T(8,128)} %get-tuple-element.47.acc_hbm, f32[5,1,512]{2,1,0:T(1,128)} %get-tuple-element.48.top_hbm, s32[2,1280]{1,0:T(2,128)} %win_hbm.3, ...), custom_call_target="tpu_custom_call" | custom-call | flops 6000000000 | bytes 2000000 | tf_op jit(solution)/shard_map/far/pallas_call | solution.py:446
  63.5 0.5 grads.1
  64.0 2.6 %collective-permute-start.6 = (f32[112,128]{1,0:T(8,128)S(1)}, f32[112,128]{1,0:T(8,128)S(1)}, u32[]{:S(2)}, u32[]{:S(2)}) collective-permute-start(f32[112,128]{1,0:T(8,128)S(1)} %get-tuple-element.53), channel_id=1, source_target_pairs={{0,8},{8,0},{16,24},{24,16},{32,40},{40,32},{48,56},{56,48},{64,72... | collective-permute-start | bytes 172040 | tf_op jit(solution)/shard_map/ppermute | solution.py:639
  66.6 0.9 collective-permute-done.6
  67.5 2.4 %collective-permute-start.7 = (bf16[112,128]{1,0:T(8,128)(2,1)S(1)}, bf16[112,128]{1,0:T(8,128)(2,1)S(1)}, u32[]{:S(2)}, u32[]{:S(2)}) collective-permute-start(bf16[112,128]{1,0:T(8,128)(2,1)S(1)} %add_convert_fusion.3), channel_id=1, source_target_pairs={{0,16},{8,24},{16,0},{24,8},{32,48},{40,56},{48,32},{56,40},{64,80... | collective-permute-start | bytes 86024 | tf_op jit(solution)/shard_map/ppermute | solution.py:639
  69.9 3.1 %collective-permute-done.7 = bf16[112,128]{1,0:T(8,128)(2,1)S(1)} collective-permute-done((bf16[112,128]{1,0:T(8,128)(2,1)S(1)}, bf16[112,128]{1,0:T(8,128)(2,1)S(1)}, u32[]{:S(2)}, u32[]{:S(2)}) %collective-permute-start.7) | collective-permute-done | bytes 28704 | tf_op jit(solution)/shard_map/ppermute | solution.py:639
  73.1 3.9 %collective-permute-done.8 = bf16[112,128]{1,0:T(8,128)(2,1)S(1)} collective-permute-done((bf16[112,128]{1,0:T(8,128)(2,1)S(1)}, bf16[112,128]{1,0:T(8,128)(2,1)S(1)}, u32[]{:S(2)}, u32[]{:S(2)}) %collective-permute-start.8) | collective-permute-done | bytes 28704 | tf_op jit(solution)/shard_map/ppermute | solution.py:639
  76.9 2.1 %collective-permute-start.9 = (bf16[112,128]{1,0:T(8,128)(2,1)S(1)}, bf16[112,128]{1,0:T(8,128)(2,1)S(1)}, u32[]{:S(2)}, u32[]{:S(2)}) collective-permute-start(bf16[112,128]{1,0:T(8,128)(2,1)S(1)} %add_convert_fusion.1), channel_id=1, source_target_pairs={{0,64},{8,72},{16,80},{24,88},{32,96},{40,104},{48,112},{56,120},{... | collective-permute-start | bytes 86024 | tf_op jit(solution)/shard_map/ppermute | solution.py:639
  79.0 2.8 %collective-permute-done.9 = bf16[112,128]{1,0:T(8,128)(2,1)S(1)} collective-permute-done((bf16[112,128]{1,0:T(8,128)(2,1)S(1)}, bf16[112,128]{1,0:T(8,128)(2,1)S(1)}, u32[]{:S(2)}, u32[]{:S(2)}) %collective-permute-start.9) | collective-permute-done | bytes 28704 | tf_op jit(solution)/shard_map/ppermute | solution.py:639
  81.8 5.2 %collective-permute-start.10 = (bf16[112,128]{1,0:T(8,128)(2,1)S(1)}, bf16[112,128]{1,0:T(8,128)(2,1)S(1)}, u32[]{:S(2)}, u32[]{:S(2)}) collective-permute-start(bf16[112,128]{1,0:T(8,128)(2,1)S(1)} %add_convert_fusion.grad_ref), channel_id=1, source_target_pairs={{0,192},{8,200},{16,208},{24,216},{32,224},{40,232},{48,240},{56,2... | collective-permute-start | bytes 86024 | tf_op jit(solution)/shard_map/ppermute | solution.py:645
  87.0 1.9 %collective-permute-done.10.more_ref = bf16[112,128]{1,0:T(8,128)(2,1)S(1)} collective-permute-done((bf16[112,128]{1,0:T(8,128)(2,1)S(1)}, bf16[112,128]{1,0:T(8,128)(2,1)S(1)}, u32[]{:S(2)}, u32[]{:S(2)}) %collective-permute-start.10) | collective-permute-done | bytes 28704 | tf_op jit(solution)/shard_map/ppermute | solution.py:645
  88.8 0.8 spread.1
  89.6 14.0 %all_to_all.15.parts_ref = bf16[8,272,128]{2,1,0:T(8,128)(2,1)S(1)} all-to-all(bf16[8,272,128]{2,1,0:T(8,128)(2,1)} %spread.1), channel_id=1, replica_groups=mesh['band'=32,'head'=8] {'head'}, dimensions={0} | all-to-all | bytes 1114112 | tf_op jit(solution)/shard_map/all_to_all | solution.py:649
  103.6 0.6 gradient_half.1.mine_ref
  104.4 0.7 collective-permute-start.12
  105.1 2.5 %collective-permute-start.13 = (bf16[160,128]{1,0:T(8,128)(2,1)S(1)}, bf16[160,128]{1,0:T(8,128)(2,1)S(1)}, u32[]{:S(2)}, u32[]{:S(2)}) collective-permute-start(bf16[160,128]{1,0:T(8,128)(2,1)S(1)} %make_table.1.own_ref), channel_id=1, source_target_pairs={{0,2},{2,4},{3,1},{4,6},{5,3},{6,8},{7,5},{8,10},{9,7},{10,12},{11... | collective-permute-start | bytes 122888 | tf_op jit(solution)/shard_map/ppermute | solution.py:629
  107.6 0.8 add.29
  108.5 6.5 %collective-permute-done.13.far_ref = bf16[160,128]{1,0:T(8,128)(2,1)S(1)} collective-permute-done((bf16[160,128]{1,0:T(8,128)(2,1)S(1)}, bf16[160,128]{1,0:T(8,128)(2,1)S(1)}, u32[]{:S(2)}, u32[]{:S(2)}) %collective-permute-start.13) | collective-permute-done | bytes 40992 | tf_op jit(solution)/shard_map/ppermute | solution.py:629
  114.9 1.4 %decode.1 = bf16[110,2048]{1,0:T(8,128)(2,1)} custom-call(bf16[160,128]{1,0:T(8,128)(2,1)S(1)} %collective-permute-done.12.mid_ref, bf16[160,128]{1,0:T(8,128)(2,1)S(1)} %collective-permute-done.13.far_ref, bf16[160,128]{1,0:T(8,128)(2,1)S(1)} %make_table.1.own_ref, s32[1,2048]{1,0:T(1,128)S(1)} %bitcast.7, bf16[110,2048]{1,0:T(8,128)(2,1)S(1)} %copy-done.1), custom_call_target="tpu_custom_call" | custom-call | tf_op jit(solution)/shard_map/decode/pallas_call | solution.py:540
  (31 shorter events, 0.8 us)
Async XLA Ops:
  0.6 20.8 %copy-start.3 = (f32[1024]{0:T(1024)S(1)}, f32[1024]{0:T(1024)}, u32[]{:S(2)}) copy-start(f32[1024]{0:T(1024)} %param.19) | copy-start | bytes 12292
  5.6 15.8 %collective-permute-start = (bf16[176,1024]{1,0:T(8,128)(2,1)S(1)}, bf16[176,1024]{1,0:T(8,128)(2,1)S(1)}, u32[]{:S(2)}, u32[]{:S(2)}) collective-permute-start(bf16[176,1024]{1,0:T(8,128)(2,1)S(1)} %get-tuple-element.31), channel_id=1, source_target_pairs={{0,1},{1,0},{2,3},{3,2},{4,5},{5,4},{6,7},{7,6},{8,9},{9,8},{10,11... | collective-permute-start | bytes 1081352 | tf_op jit(solution)/shard_map/ppermute | solution.py:623
  7.2 14.2 %collective-permute-start.1 = (bf16[160,1024]{1,0:T(8,128)(2,1)S(1)}, bf16[160,1024]{1,0:T(8,128)(2,1)S(1)}, u32[]{:S(2)}, u32[]{:S(2)}) collective-permute-start(bf16[160,1024]{1,0:T(8,128)(2,1)S(1)} %get-tuple-element.32.after_ref), channel_id=1, source_target_pairs={{1,3},{2,0},{3,5},{4,2},{5,7},{6,4},{7,9},{8,6},{9,11},{10,8},{11,... | collective-permute-start | bytes 983048 | tf_op jit(solution)/shard_map/ppermute | solution.py:629
  16.2 7.4 %collective-permute-start.2 = (bf16[160,128]{1,0:T(8,128)(2,1)S(1)}, bf16[160,128]{1,0:T(8,128)(2,1)S(1)}, u32[]{:S(2)}, u32[]{:S(2)}) collective-permute-start(bf16[160,128]{1,0:T(8,128)(2,1)S(1)} %get-tuple-element.35), channel_id=1, source_target_pairs={{0,1},{1,0},{2,3},{3,2},{4,5},{5,4},{6,7},{7,6},{8,9},{9,8},{10,11... | collective-permute-start | bytes 122888 | tf_op jit(solution)/shard_map/ppermute | solution.py:623
  16.3 7.3 %collective-permute-start.3 = (bf16[160,128]{1,0:T(8,128)(2,1)S(1)}, bf16[160,128]{1,0:T(8,128)(2,1)S(1)}, u32[]{:S(2)}, u32[]{:S(2)}) collective-permute-start(bf16[160,128]{1,0:T(8,128)(2,1)S(1)} %get-tuple-element.36), channel_id=1, source_target_pairs={{1,3},{2,0},{3,5},{4,2},{5,7},{6,4},{7,9},{8,6},{9,11},{10,8},{11,... | collective-permute-start | bytes 122888 | tf_op jit(solution)/shard_map/ppermute | solution.py:629
  23.6 19.6 %all-to-all-start = ((bf16[8,160,384]{2,1,0:T(8,128)(2,1)}), bf16[8,160,384]{2,1,0:T(8,128)(2,1)S(1)}, u32[]{:S(2)}, u32[]{:S(2)}) async-start(bf16[8,160,384]{2,1,0:T(8,128)(2,1)} %get-tuple-element.37), calls=%async_computation | async-start | bytes 1966080 | tf_op jit(solution)/shard_map/all_to_all | solution.py:649
  43.4 14.0 %collective-permute-start.4 = (bf16[4,160,256]{2,1,0:T(8,128)(2,1)S(1)}, bf16[4,160,256]{2,1,0:T(8,128)(2,1)S(1)}, u32[]{:S(2)}, u32[]{:S(2)}) collective-permute-start(bf16[4,160,256]{2,1,0:T(8,128)(2,1)S(1)} %get-tuple-element.59), channel_id=1, source_target_pairs={{0,8},{8,0},{16,24},{24,16},{32,40},{40,32},{48,56},{56,48},{64,72... | collective-permute-start | bytes 983048 | tf_op jit(solution)/shard_map/ppermute | solution.py:639
  43.5 14.0 %collective-permute-start.5 = (bf16[4,160,256]{2,1,0:T(8,128)(2,1)S(1)}, bf16[4,160,256]{2,1,0:T(8,128)(2,1)S(1)}, u32[]{:S(2)}, u32[]{:S(2)}) collective-permute-start(bf16[4,160,256]{2,1,0:T(8,128)(2,1)S(1)} %get-tuple-element.58), channel_id=1, source_target_pairs={{8,16},{16,8},{24,32},{32,24},{40,48},{48,40},{56,64},{64,56},{72,... | collective-permute-start | bytes 983048 | tf_op jit(solution)/shard_map/ppermute | solution.py:635
  47.4 16.1 %all-to-all-start.1 = ((bf16[8,272,128]{2,1,0:T(8,128)(2,1)}), bf16[8,272,128]{2,1,0:T(8,128)(2,1)S(1)}, u32[]{:S(2)}, u32[]{:S(2)}) async-start(bf16[8,272,128]{2,1,0:T(8,128)(2,1)} %get-tuple-element.51), calls=%async_computation.1 | async-start | bytes 1114112 | tf_op jit(solution)/shard_map/all_to_all | solution.py:649
  57.4 0.7 copy-start.4
  57.5 0.8 copy-start.5
  58.3 45.3 %copy-start = (bf16[1024,1024]{1,0:T(8,128)(2,1)S(1)}, bf16[1024,1024]{1,0:T(8,128)(2,1)}, u32[]{:S(2)}) copy-start(bf16[1024,1024]{1,0:T(8,128)(2,1)} %w_out_ref.1) | copy-start | bytes 6291460
  63.5 51.4 %copy-start.1 = (bf16[110,2048]{1,0:T(8,128)(2,1)S(1)}, bf16[110,2048]{1,0:T(8,128)(2,1)}, u32[]{:S(2)}) copy-start(bf16[110,2048]{1,0:T(8,128)(2,1)} %grid_ref.1) | copy-start | bytes 1351684
  63.5 51.4 %copy-start.2 = (s32[2048]{0:T(1024)S(1)}, s32[2048]{0:T(1024)}, u32[]{:S(2)}) copy-start(s32[2048]{0:T(1024)} %param.13) | copy-start | bytes 24580
  64.0 3.5 %collective-permute-start.6 = (f32[112,128]{1,0:T(8,128)S(1)}, f32[112,128]{1,0:T(8,128)S(1)}, u32[]{:S(2)}, u32[]{:S(2)}) collective-permute-start(f32[112,128]{1,0:T(8,128)S(1)} %get-tuple-element.53), channel_id=1, source_target_pairs={{0,8},{8,0},{16,24},{24,16},{32,40},{40,32},{48,56},{56,48},{64,72... | collective-permute-start | bytes 172040 | tf_op jit(solution)/shard_map/ppermute | solution.py:639
  67.5 5.5 %collective-permute-start.7 = (bf16[112,128]{1,0:T(8,128)(2,1)S(1)}, bf16[112,128]{1,0:T(8,128)(2,1)S(1)}, u32[]{:S(2)}, u32[]{:S(2)}) collective-permute-start(bf16[112,128]{1,0:T(8,128)(2,1)S(1)} %add_convert_fusion.3), channel_id=1, source_target_pairs={{0,16},{8,24},{16,0},{24,8},{32,48},{40,56},{48,32},{56,40},{64,80... | collective-permute-start | bytes 86024 | tf_op jit(solution)/shard_map/ppermute | solution.py:639
  73.0 4.0 %collective-permute-start.8 = (bf16[112,128]{1,0:T(8,128)(2,1)S(1)}, bf16[112,128]{1,0:T(8,128)(2,1)S(1)}, u32[]{:S(2)}, u32[]{:S(2)}) collective-permute-start(bf16[112,128]{1,0:T(8,128)(2,1)S(1)} %add_convert_fusion.2), channel_id=1, source_target_pairs={{0,32},{8,40},{16,48},{24,56},{32,0},{40,8},{48,16},{56,24},{64,96... | collective-permute-start | bytes 86024 | tf_op jit(solution)/shard_map/ppermute | solution.py:639
  76.9 4.9 %collective-permute-start.9 = (bf16[112,128]{1,0:T(8,128)(2,1)S(1)}, bf16[112,128]{1,0:T(8,128)(2,1)S(1)}, u32[]{:S(2)}, u32[]{:S(2)}) collective-permute-start(bf16[112,128]{1,0:T(8,128)(2,1)S(1)} %add_convert_fusion.1), channel_id=1, source_target_pairs={{0,64},{8,72},{16,80},{24,88},{32,96},{40,104},{48,112},{56,120},{... | collective-permute-start | bytes 86024 | tf_op jit(solution)/shard_map/ppermute | solution.py:639
  81.8 7.0 %collective-permute-start.10 = (bf16[112,128]{1,0:T(8,128)(2,1)S(1)}, bf16[112,128]{1,0:T(8,128)(2,1)S(1)}, u32[]{:S(2)}, u32[]{:S(2)}) collective-permute-start(bf16[112,128]{1,0:T(8,128)(2,1)S(1)} %add_convert_fusion.grad_ref), channel_id=1, source_target_pairs={{0,192},{8,200},{16,208},{24,216},{32,224},{40,232},{48,240},{56,2... | collective-permute-start | bytes 86024 | tf_op jit(solution)/shard_map/ppermute | solution.py:645
  104.2 3.4 %collective-permute-start.11 = (f32[112,1024]{1,0:T(8,128)S(1)}, f32[112,1024]{1,0:T(8,128)S(1)}, u32[]{:S(2)}, u32[]{:S(2)}) collective-permute-start(f32[112,1024]{1,0:T(8,128)S(1)} %gradient_half.1.mine_ref), channel_id=1, source_target_pairs={{0,8},{8,0},{16,24},{24,16},{32,40},{40,32},{48,56},{56,48},{64,72... | collective-permute-start | bytes 1376264 | tf_op jit(solution)/shard_map/ppermute | solution.py:639
  104.4 4.1 %collective-permute-start.12 = (bf16[160,128]{1,0:T(8,128)(2,1)S(1)}, bf16[160,128]{1,0:T(8,128)(2,1)S(1)}, u32[]{:S(2)}, u32[]{:S(2)}) collective-permute-start(bf16[160,128]{1,0:T(8,128)(2,1)S(1)} %make_table.1.own_ref), channel_id=1, source_target_pairs={{0,1},{1,0},{2,3},{3,2},{4,5},{5,4},{6,7},{7,6},{8,9},{9,8},{10,11... | collective-permute-start | bytes 122888 | tf_op jit(solution)/shard_map/ppermute | solution.py:623
  105.1 9.8 %collective-permute-start.13 = (bf16[160,128]{1,0:T(8,128)(2,1)S(1)}, bf16[160,128]{1,0:T(8,128)(2,1)S(1)}, u32[]{:S(2)}, u32[]{:S(2)}) collective-permute-start(bf16[160,128]{1,0:T(8,128)(2,1)S(1)} %make_table.1.own_ref), channel_id=1, source_target_pairs={{0,2},{2,4},{3,1},{4,6},{5,3},{6,8},{7,5},{8,10},{9,7},{10,12},{11... | collective-permute-start | bytes 122888 | tf_op jit(solution)/shard_map/ppermute | solution.py:629

commit v6 on v5

--- a/solution.py
+++ b/solution.py
@@ -363,8 +363,8 @@
     )(qkv, *pinned(win))
 
 
-def far_kernel(reach, q_hbm, acc_hbm, top_hbm, win_hbm, mix_hbm, chip_hbm, off_hbm, node_hbm, out_ref,
-               q_ref, acc_ref, top_ref, win_ref, mix_ref, chip_ref, off_ref,
+def far_kernel(reach, q_hbm, acc_hbm, top_hbm, win_hbm, mix_hbm, off_hbm, chip_ref, node_hbm, out_ref,
+               q_ref, acc_ref, top_ref, win_ref, mix_ref, off_ref,
                k_ref, v_ref, vt_ref, score_ref, prob_ref, node_ref, sem):
     band_rows = q_ref.shape[1]
     groups = band_rows // NODE_DEV
@@ -374,14 +374,14 @@
         [
             pltpu.make_async_copy(source, target, sem.at[at])
             for at, (source, target) in enumerate(
-                [(chip_hbm, chip_ref), (off_hbm, off_ref), (q_hbm, q_ref), (acc_hbm, acc_ref), (top_hbm, top_ref), (win_hbm, win_ref), (mix_hbm, mix_ref)]
+                [(off_hbm, off_ref), (q_hbm, q_ref), (acc_hbm, acc_ref), (top_hbm, top_ref), (win_hbm, win_ref), (mix_hbm, mix_ref)]
             )
         ]
     )
     core = lax.rem(lax.axis_index("band"), 2)
-    copies[0].wait()
-    copies[1].wait()
     for base, half in (((1 - core) * reach, chip_ref), (core * reach, off_ref)):
+        if half is off_ref:
+            copies[0].wait()
         for group in range(groups // 2):
             rows = pl.ds(pl.multiple_of(base + (group ^ 1) * NODE_DEV, NODE_DEV), NODE_DEV)
             k_ref[rows, :] = half[group, :, :LANES]
@@ -390,7 +390,7 @@
     for head in range(2):
         vt_ref[head, :HDIM, :] = vt[head * HDIM : (head + 1) * HDIM]
         vt_ref[head, HDIM:, :] = jnp.ones((16, 2 * reach), BF)
-    for copy in copies[2:]:
+    for copy in copies[1:]:
         copy.wait()
     for block in range(band_rows // QB):
         start = block * QB
@@ -442,10 +442,10 @@
     band_rows = queries.shape[1]
     groups = band_rows // NODE_DEV
     reach = on_chip.shape[0] * NODE_DEV
-    held = (queries, acc, top, win, mix, on_chip, off_chip)
+    held = (queries, acc, top, win, mix, off_chip)
     return pl.pallas_call(
         functools.partial(far_kernel, reach),
-        in_specs=[HBM] * 7,
+        in_specs=[HBM] * 6 + [VMEM],
         out_specs=(HBM, VMEM),
         out_shape=(
             in_hbm(shape((groups, NODE_DEV + ROWS, LANES), BF)),
@@ -464,7 +464,7 @@
         compiler_params=params(),
         cost_estimate=pl.CostEstimate(flops=6_000_000_000, bytes_accessed=2_000_000, transcendentals=1_000_000),
         name="far",
-    )(*pinned(*held))
+    )(*pinned(*held), on_chip)
 
 
 def grads_kernel(out_ref, extra_ref, keep_ref, give_ref):
@@ -492,19 +492,21 @@
     )(out, extra)
 
 
-def table_kernel(parts_ref, node_ref, table_ref):
+def table_kernel(parts_ref, node_ref, table_ref, padded_ref):
     total = node_ref[...]
     for group in range(parts_ref.shape[0]):
         total += parts_ref[group, :NODE_DEV, :].astype(F32)
     table_ref[...] = total.astype(BF)
+    padded_ref[:NODE_DEV, :] = total.astype(BF)
+    padded_ref[NODE_DEV:, :] = jnp.zeros((EXTRA, LANES), BF)
 
 
 def make_table(parts, node):
     return pl.pallas_call(
         table_kernel,
         in_specs=[VMEM] * 2,
-        out_specs=VMEM,
-        out_shape=shape(node.shape, BF),
+        out_specs=(VMEM,) * 2,
+        out_shape=(shape(node.shape, BF), shape((NODE_DEV + EXTRA, LANES), BF)),
         compiler_params=params(),
         name="make_table",
     )(parts, node)
@@ -516,7 +518,7 @@
     rows = 4 * LANES
     table = jnp.concatenate(
         [
-            far_ref[...].astype(F32),
+            far_ref[:NODE_DEV].astype(F32),
             mid_ref[...].astype(F32),
             own_ref[...].astype(F32),
             jnp.zeros((rows - 3 * nodes, LANES), F32),
@@ -682,11 +684,11 @@
     for bit in (1, 2, 3):
         grad = (grad.astype(F32) + flipped(grad, "band", bit).astype(F32)).astype(BF)
     parts = swap(spread(grad, across(grad), parts))
-    table = make_table(parts, node)
+    table, padded = make_table(parts, node)
     half_grad = gradient_half(parts, w_out)
     grad_dec = add(half_grad, flipped(half_grad, "band", 0), channels)
     grad_dec, mid_rows = lax.optimization_barrier((grad_dec, to_partner(table)))
-    prediction = decode(two_over(table, 1), mid_rows, table, dec_row, grid_in)
+    prediction = decode(two_over(padded, 1), mid_rows, table, dec_row, grid_in)
     return (prediction, grad_dec.T)
 
 

time: 117 us -> 116 us (level)
  waiting for transfers between devices: 31.6 us -> 28.2 us
  starting transfers between devices: 41.7 us -> 43.8 us
    ppermute x3, waiting for transfers between devices: 6.48 us -> 3.41 us  [two_over(): lax.ppermute(block, BOTH, [(i, j) for i, j in pairs if 0 <= j < count])]
    ppermute x6, waiting for transfers between devices: 10.6 us -> 9.12 us  [flipped(): lax.ppermute(block, axis, [(i, i ^ 1 << bit) for i in range(lax.axis_size...]
    ppermute x3, starting transfers between devices: 2.41 us -> 3.79 us  [to_partner(): lax.ppermute(block, BOTH, [(i, i ^ 1) for i in range(total_devices())])]
  transfers between devices with their start and end apart: 16 -> 16, of which waited for: 7 -> 8; matrix products, arithmetic and copies ran while one was open for 0% -> 0% of each run, Pallas kernels for 16% -> 16%
where the time goes in v6:
time: 116 us; the launch traced here: 115 us
  starting transfers between devices  43.8 us (38%)
  waiting for transfers between devices  28.2 us (24%)
  Pallas kernels  27.1 us (23%)
  blocking collectives  14.4 us (12%)
    all_to_all x1, blocking collectives, swap(): lax.all_to_all(block, 'head', split_axis=0, concat_axis=0, tiled=True)  14.4 us
    ppermute x3, starting transfers between devices, two_over(): lax.ppermute(block, BOTH, [(i, j) for i, j in pairs if 0 <= j < count])  13.4 us
    all_to_all x2, waiting for transfers between devices, swap(): lax.all_to_all(block, 'head', split_axis=0, concat_axis=0, tiled=True)  12.6 us
    all_to_all x2, starting transfers between devices, swap(): lax.all_to_all(block, 'head', split_axis=0, concat_axis=0, tiled=True)  9.48 us
    ppermute x6, waiting for transfers between devices, flipped(): lax.ppermute(block, axis, [(i, i ^ 1 << bit) for i in range(lax.axis_size...  9.12 us
    ppermute x6, starting transfers between devices, flipped(): lax.ppermute(block, axis, [(i, i ^ 1 << bit) for i in range(lax.axis_size...  7.72 us
    pallas_call x1, Pallas kernels, near(): pl.pallas_call(functools.partial(near_kernel, reach), in_specs=[VMEM, HBM...  6.25 us
    ppermute x1, starting transfers between devices, across(): lax.ppermute(block, 'band', [(i, other[i // 4] * 4 + i % 4) for i in rang...  5.48 us
  transfers between devices with their start and end apart: 16, of which 8 were waited for; matrix products, arithmetic and copies ran while one was open for 0% of the time, Pallas kernels for 16%

profile of v6, /device:TPU:32, one launch (start us, length us, event | category | flops | bytes accessed | tf_op | source)
XLA Modules:
  0.0 115.2 jit_solution(16697729329510783656)
XLA Ops:
  0.6 4.9 %encode.1 = (bf16[160,1024]{1,0:T(8,128)(2,1)S(1)}, bf16[176,1024]{1,0:T(8,128)(2,1)S(1)}, f32[160,1024]{1,0:T(8,128)S(1)}) custom-call(bf16[110,2048]{1,0:T(8,128)(2,1)} %grid_ref.1, s32[1,2048]{1,0:T(1,128)} %bitcast.11, bf16[110,1024]{1,0:T(8,128)(2,1)} %w_hbm.2, f32[1,1024]{1,0:T(1,128)} %bitcast.12), custom_call_target="tpu_custom_call" | custom-call | tf_op jit(solution)/shard_map/encode/pallas_call | solution.py:98
  5.6 1.6 %collective-permute-start = (bf16[176,1024]{1,0:T(8,128)(2,1)S(1)}, bf16[176,1024]{1,0:T(8,128)(2,1)S(1)}, u32[]{:S(2)}, u32[]{:S(2)}) collective-permute-start(bf16[176,1024]{1,0:T(8,128)(2,1)S(1)} %get-tuple-element.33), channel_id=1, source_target_pairs={{0,1},{1,0},{2,3},{3,2},{4,5},{5,4},{6,7},{7,6},{8,9},{9,8},{10,11... | collective-permute-start | bytes 1081352 | tf_op jit(solution)/shard_map/ppermute | solution.py:625
  7.2 5.8 %collective-permute-start.1 = (bf16[160,1024]{1,0:T(8,128)(2,1)S(1)}, bf16[160,1024]{1,0:T(8,128)(2,1)S(1)}, u32[]{:S(2)}, u32[]{:S(2)}) collective-permute-start(bf16[160,1024]{1,0:T(8,128)(2,1)S(1)} %get-tuple-element.34.after_ref), channel_id=1, source_target_pairs={{1,3},{2,0},{3,5},{4,2},{5,7},{6,4},{7,9},{8,6},{9,11},{10,8},{11,... | collective-permute-start | bytes 983048 | tf_op jit(solution)/shard_map/ppermute | solution.py:631
  13.0 3.2 %prepare.1 = (bf16[1024,3072]{1,0:T(8,128)(2,1)S(1)}, bf16[128,1024]{1,0:T(8,128)(2,1)S(1)}, bf16[128,128]{1,0:T(8,128)(2,1)}, bf16[160,128]{1,0:T(8,128)(2,1)S(...) custom-call(bf16[1024,3072]{1,0:T(8,128)(2,1)} %w_hbm.3, bf16[1024,1024]{1,0:T(8,128)(2,1)} %w_out_ref.1, ...), custom_call_target="tpu_custom_call" | custom-call | flops 500000000 | bytes 6291456 | tf_op jit(solution)/shard_map/prepare/pallas_call | solution.py:158
  16.3 5.1 %collective-permute-start.3 = (bf16[160,128]{1,0:T(8,128)(2,1)S(1)}, bf16[160,128]{1,0:T(8,128)(2,1)S(1)}, u32[]{:S(2)}, u32[]{:S(2)}) collective-permute-start(bf16[160,128]{1,0:T(8,128)(2,1)S(1)} %get-tuple-element.38), channel_id=1, source_target_pairs={{1,3},{2,0},{3,5},{4,2},{5,7},{6,4},{7,9},{8,6},{9,11},{10,8},{11,... | collective-permute-start | bytes 122888 | tf_op jit(solution)/shard_map/ppermute | solution.py:631
  21.4 2.2 %project.1 = (bf16[8,160,384]{2,1,0:T(8,128)(2,1)}, f32[160,1024]{1,0:T(8,128)S(1)}) custom-call(f32[160,1024]{1,0:T(8,128)S(1)} %get-tuple-element.32.own_ref, bf16[176,1024]{1,0:T(8,128)(2,1)S(1)} %collective-permute-done.mid_ref, bf16[160,1024]{1,0:T(8,128)(2,1)S(1)} %collective-permute-done.1.far_ref, f32[1,1024]{1,0:T(1,128)S(1)} %bitcast.8, ...), custom_call_target="tpu_custom_call" | custom-call | tf_op jit(solution)/shard_map/project/pallas_call | solution.py:213
  23.6 5.8 %all-to-all-start = ((bf16[8,160,384]{2,1,0:T(8,128)(2,1)}), bf16[8,160,384]{2,1,0:T(8,128)(2,1)S(1)}, u32[]{:S(2)}, u32[]{:S(2)}) async-start(bf16[8,160,384]{2,1,0:T(8,128)(2,1)} %get-tuple-element.39), calls=%async_computation | async-start | bytes 1966080 | tf_op jit(solution)/shard_map/all_to_all | solution.py:651
  29.4 1.2 %side.1 = (bf16[8,272,128]{2,1,0:T(8,128)(2,1)}, f32[160,128]{1,0:T(8,128)S(1)}) custom-call(f32[160,1024]{1,0:T(8,128)S(1)} %get-tuple-element.40.enc_ref, f32[160,128]{1,0:T(8,128)S(1)} %get-tuple-element.41.own_ref, bf16[160,128]{1,0:T(8,128)(2,1)S(1)} %collective-permute-done.2.mid_ref, bf16[160,128]{1,0:T(8,128)(2,1)S(1)} %collective-permute-done.3.far_ref, ...), custom_call_target="tpu_custom_call" | custom-call | tf_op jit(solution)/shard_map/side/pallas_call | solution.py:249
  30.6 12.6 %all-to-all-done.qkv_ref = bf16[8,160,384]{2,1,0:T(8,128)(2,1)S(1)} async-done(((bf16[8,160,384]{2,1,0:T(8,128)(2,1)}), bf16[8,160,384]{2,1,0:T(8,128)(2,1)S(1)}, u32[]{:S(2)}, u32[]{:S(2)}) %all-to-all-start) | async-done | bytes 983072 | tf_op jit(solution)/shard_map/all_to_all | solution.py:651
  43.4 3.9 %collective-permute-start.4 = (bf16[4,160,256]{2,1,0:T(8,128)(2,1)S(1)}, bf16[4,160,256]{2,1,0:T(8,128)(2,1)S(1)}, u32[]{:S(2)}, u32[]{:S(2)}) collective-permute-start(bf16[4,160,256]{2,1,0:T(8,128)(2,1)S(1)} %get-tuple-element.63), channel_id=1, source_target_pairs={{8,16},{16,8},{24,32},{32,24},{40,48},{48,40},{56,64},{64,56},{72,... | collective-permute-start | bytes 983048 | tf_op jit(solution)/shard_map/ppermute | solution.py:637
  47.7 3.7 %all-to-all-start.1 = ((bf16[8,272,128]{2,1,0:T(8,128)(2,1)}), bf16[8,272,128]{2,1,0:T(8,128)(2,1)S(1)}, u32[]{:S(2)}, u32[]{:S(2)}) async-start(bf16[8,272,128]{2,1,0:T(8,128)(2,1)} %get-tuple-element.53), calls=%async_computation.1 | async-start | bytes 1114112 | tf_op jit(solution)/shard_map/all_to_all | solution.py:651
  51.4 6.2 %near.1 = (f32[5,2,80,256]{3,2,1,0:T(8,128)}, f32[5,1,512]{2,1,0:T(1,128)}, bf16[2,1280,128]{2,1,0:T(8,128)(2,1)}) custom-call(bf16[8,160,384]{2,1,0:T(8,128)(2,1)S(1)} %all-to-all-done.qkv_ref, s32[2,1280]{1,0:T(2,128)} %win_hbm.3), custom_call_target="tpu_custom_call" | custom-call | flops 6000000000 | bytes 4000000 | tf_op jit(solution)/shard_map/near/pallas_call | solution.py:345
  57.7 0.7 copy-done.4
  58.4 5.1 %far.1 = (bf16[8,272,128]{2,1,0:T(8,128)(2,1)}, bf16[128,1280]{1,0:T(8,128)(2,1)S(1)}) custom-call(bf16[2,1280,128]{2,1,0:T(8,128)(2,1)} %get-tuple-element.48.q_hbm, f32[5,2,80,256]{3,2,1,0:T(8,128)} %get-tuple-element.49.acc_hbm, f32[5,1,512]{2,1,0:T(1,128)} %get-tuple-element.50.top_hbm, s32[2,1280]{1,0:T(2,128)} %win_hbm.3, ...), custom_call_target="tpu_custom_call" | custom-call | flops 6000000000 | bytes 2000000 | tf_op jit(solution)/shard_map/far/pallas_call | solution.py:446
  63.5 0.5 grads.1
  64.3 1.0 collective-permute-done.6
  65.4 2.9 %collective-permute-start.7 = (bf16[112,128]{1,0:T(8,128)(2,1)S(1)}, bf16[112,128]{1,0:T(8,128)(2,1)S(1)}, u32[]{:S(2)}, u32[]{:S(2)}) collective-permute-start(bf16[112,128]{1,0:T(8,128)(2,1)S(1)} %add_convert_fusion.3), channel_id=1, source_target_pairs={{0,16},{8,24},{16,0},{24,8},{32,48},{40,56},{48,32},{56,40},{64,80... | collective-permute-start | bytes 86024 | tf_op jit(solution)/shard_map/ppermute | solution.py:641
  68.3 2.5 %collective-permute-done.7 = bf16[112,128]{1,0:T(8,128)(2,1)S(1)} collective-permute-done((bf16[112,128]{1,0:T(8,128)(2,1)S(1)}, bf16[112,128]{1,0:T(8,128)(2,1)S(1)}, u32[]{:S(2)}, u32[]{:S(2)}) %collective-permute-start.7) | collective-permute-done | bytes 28704 | tf_op jit(solution)/shard_map/ppermute | solution.py:641
  71.0 3.8 %collective-permute-done.8 = bf16[112,128]{1,0:T(8,128)(2,1)S(1)} collective-permute-done((bf16[112,128]{1,0:T(8,128)(2,1)S(1)}, bf16[112,128]{1,0:T(8,128)(2,1)S(1)}, u32[]{:S(2)}, u32[]{:S(2)}) %collective-permute-start.8) | collective-permute-done | bytes 28704 | tf_op jit(solution)/shard_map/ppermute | solution.py:641
  74.8 3.8 %collective-permute-start.9 = (bf16[112,128]{1,0:T(8,128)(2,1)S(1)}, bf16[112,128]{1,0:T(8,128)(2,1)S(1)}, u32[]{:S(2)}, u32[]{:S(2)}) collective-permute-start(bf16[112,128]{1,0:T(8,128)(2,1)S(1)} %add_convert_fusion.1), channel_id=1, source_target_pairs={{0,64},{8,72},{16,80},{24,88},{32,96},{40,104},{48,112},{56,120},{... | collective-permute-start | bytes 86024 | tf_op jit(solution)/shard_map/ppermute | solution.py:641
  78.6 1.9 %collective-permute-done.9 = bf16[112,128]{1,0:T(8,128)(2,1)S(1)} collective-permute-done((bf16[112,128]{1,0:T(8,128)(2,1)S(1)}, bf16[112,128]{1,0:T(8,128)(2,1)S(1)}, u32[]{:S(2)}, u32[]{:S(2)}) %collective-permute-start.9) | collective-permute-done | bytes 28704 | tf_op jit(solution)/shard_map/ppermute | solution.py:641
  80.5 5.5 %collective-permute-start.10 = (bf16[112,128]{1,0:T(8,128)(2,1)S(1)}, bf16[112,128]{1,0:T(8,128)(2,1)S(1)}, u32[]{:S(2)}, u32[]{:S(2)}) collective-permute-start(bf16[112,128]{1,0:T(8,128)(2,1)S(1)} %add_convert_fusion.grad_ref), channel_id=1, source_target_pairs={{0,192},{8,200},{16,208},{24,216},{32,224},{40,232},{48,240},{56,2... | collective-permute-start | bytes 86024 | tf_op jit(solution)/shard_map/ppermute | solution.py:647
  86.0 1.9 %collective-permute-done.10.more_ref = bf16[112,128]{1,0:T(8,128)(2,1)S(1)} collective-permute-done((bf16[112,128]{1,0:T(8,128)(2,1)S(1)}, bf16[112,128]{1,0:T(8,128)(2,1)S(1)}, u32[]{:S(2)}, u32[]{:S(2)}) %collective-permute-start.10) | collective-permute-done | bytes 28704 | tf_op jit(solution)/shard_map/ppermute | solution.py:647
  87.8 0.8 spread.1
  88.6 14.4 %all_to_all.15.parts_ref = bf16[8,272,128]{2,1,0:T(8,128)(2,1)S(1)} all-to-all(bf16[8,272,128]{2,1,0:T(8,128)(2,1)} %spread.1), channel_id=1, replica_groups=mesh['band'=32,'head'=8] {'head'}, dimensions={0} | all-to-all | bytes 1114112 | tf_op jit(solution)/shard_map/all_to_all | solution.py:651
  103.0 0.6 gradient_half.1.mine_ref
  103.8 2.5 %collective-permute-start.13 = (bf16[176,128]{1,0:T(8,128)(2,1)S(1)}, bf16[176,128]{1,0:T(8,128)(2,1)S(1)}, u32[]{:S(2)}, u32[]{:S(2)}) collective-permute-start(bf16[176,128]{1,0:T(8,128)(2,1)S(1)} %get-tuple-element.60), channel_id=1, source_target_pairs={{0,2},{2,4},{3,1},{4,6},{5,3},{6,8},{7,5},{8,10},{9,7},{10,12},{11... | collective-permute-start | bytes 135176 | tf_op jit(solution)/shard_map/ppermute | solution.py:631
  106.3 2.1 %collective-permute-start.12 = (bf16[160,128]{1,0:T(8,128)(2,1)S(1)}, bf16[160,128]{1,0:T(8,128)(2,1)S(1)}, u32[]{:S(2)}, u32[]{:S(2)}) collective-permute-start(bf16[160,128]{1,0:T(8,128)(2,1)S(1)} %get-tuple-element.58.own_ref), channel_id=1, source_target_pairs={{0,1},{1,0},{2,3},{3,2},{4,5},{5,4},{6,7},{7,6},{8,9},{9,8},{10,11... | collective-permute-start | bytes 122888 | tf_op jit(solution)/shard_map/ppermute | solution.py:625
  108.4 0.8 add.29
  109.2 1.2 %collective-permute-done.12.mid_ref = bf16[160,128]{1,0:T(8,128)(2,1)S(1)} collective-permute-done((bf16[160,128]{1,0:T(8,128)(2,1)S(1)}, bf16[160,128]{1,0:T(8,128)(2,1)S(1)}, u32[]{:S(2)}, u32[]{:S(2)}) %collective-permute-start.12) | collective-permute-done | bytes 40992 | tf_op jit(solution)/shard_map/ppermute | solution.py:625
  110.4 3.4 %collective-permute-done.13.far_ref = bf16[176,128]{1,0:T(8,128)(2,1)S(1)} collective-permute-done((bf16[176,128]{1,0:T(8,128)(2,1)S(1)}, bf16[176,128]{1,0:T(8,128)(2,1)S(1)}, u32[]{:S(2)}, u32[]{:S(2)}) %collective-permute-start.13) | collective-permute-done | bytes 45088 | tf_op jit(solution)/shard_map/ppermute | solution.py:631
  113.8 1.4 %decode.1 = bf16[110,2048]{1,0:T(8,128)(2,1)} custom-call(bf16[160,128]{1,0:T(8,128)(2,1)S(1)} %collective-permute-done.12.mid_ref, bf16[176,128]{1,0:T(8,128)(2,1)S(1)} %collective-permute-done.13.far_ref, bf16[160,128]{1,0:T(8,128)(2,1)S(1)} %get-tuple-element.58.own_ref, s32[1,2048]{1,0:T(1,128)S(1)} %bitcast.7, bf16[110,2048]{1,0:T(8,128)(2,1)S(1)} %copy-done.1), custom_call_target="tpu_custom_call" | custom-call | tf_op jit(solution)/shard_map/decode/pallas_call | solution.py:542
  (29 shorter events, 1.3 us)
Async XLA Ops:
  0.6 20.8 %copy-start.3 = (f32[1024]{0:T(1024)S(1)}, f32[1024]{0:T(1024)}, u32[]{:S(2)}) copy-start(f32[1024]{0:T(1024)} %param.19) | copy-start | bytes 12292
  5.6 15.8 %collective-permute-start = (bf16[176,1024]{1,0:T(8,128)(2,1)S(1)}, bf16[176,1024]{1,0:T(8,128)(2,1)S(1)}, u32[]{:S(2)}, u32[]{:S(2)}) collective-permute-start(bf16[176,1024]{1,0:T(8,128)(2,1)S(1)} %get-tuple-element.33), channel_id=1, source_target_pairs={{0,1},{1,0},{2,3},{3,2},{4,5},{5,4},{6,7},{7,6},{8,9},{9,8},{10,11... | collective-permute-start | bytes 1081352 | tf_op jit(solution)/shard_map/ppermute | solution.py:625
  7.2 14.2 %collective-permute-start.1 = (bf16[160,1024]{1,0:T(8,128)(2,1)S(1)}, bf16[160,1024]{1,0:T(8,128)(2,1)S(1)}, u32[]{:S(2)}, u32[]{:S(2)}) collective-permute-start(bf16[160,1024]{1,0:T(8,128)(2,1)S(1)} %get-tuple-element.34.after_ref), channel_id=1, source_target_pairs={{1,3},{2,0},{3,5},{4,2},{5,7},{6,4},{7,9},{8,6},{9,11},{10,8},{11,... | collective-permute-start | bytes 983048 | tf_op jit(solution)/shard_map/ppermute | solution.py:631
  16.2 7.4 %collective-permute-start.2 = (bf16[160,128]{1,0:T(8,128)(2,1)S(1)}, bf16[160,128]{1,0:T(8,128)(2,1)S(1)}, u32[]{:S(2)}, u32[]{:S(2)}) collective-permute-start(bf16[160,128]{1,0:T(8,128)(2,1)S(1)} %get-tuple-element.37), channel_id=1, source_target_pairs={{0,1},{1,0},{2,3},{3,2},{4,5},{5,4},{6,7},{7,6},{8,9},{9,8},{10,11... | collective-permute-start | bytes 122888 | tf_op jit(solution)/shard_map/ppermute | solution.py:625
  16.3 7.3 %collective-permute-start.3 = (bf16[160,128]{1,0:T(8,128)(2,1)S(1)}, bf16[160,128]{1,0:T(8,128)(2,1)S(1)}, u32[]{:S(2)}, u32[]{:S(2)}) collective-permute-start(bf16[160,128]{1,0:T(8,128)(2,1)S(1)} %get-tuple-element.38), channel_id=1, source_target_pairs={{1,3},{2,0},{3,5},{4,2},{5,7},{6,4},{7,9},{8,6},{9,11},{10,8},{11,... | collective-permute-start | bytes 122888 | tf_op jit(solution)/shard_map/ppermute | solution.py:631
  23.6 19.6 %all-to-all-start = ((bf16[8,160,384]{2,1,0:T(8,128)(2,1)}), bf16[8,160,384]{2,1,0:T(8,128)(2,1)S(1)}, u32[]{:S(2)}, u32[]{:S(2)}) async-start(bf16[8,160,384]{2,1,0:T(8,128)(2,1)} %get-tuple-element.39), calls=%async_computation | async-start | bytes 1966080 | tf_op jit(solution)/shard_map/all_to_all | solution.py:651
  43.4 14.3 %collective-permute-start.4 = (bf16[4,160,256]{2,1,0:T(8,128)(2,1)S(1)}, bf16[4,160,256]{2,1,0:T(8,128)(2,1)S(1)}, u32[]{:S(2)}, u32[]{:S(2)}) collective-permute-start(bf16[4,160,256]{2,1,0:T(8,128)(2,1)S(1)} %get-tuple-element.63), channel_id=1, source_target_pairs={{8,16},{16,8},{24,32},{32,24},{40,48},{48,40},{56,64},{64,56},{72,... | collective-permute-start | bytes 983048 | tf_op jit(solution)/shard_map/ppermute | solution.py:637
  47.3 10.4 %collective-permute-start.5 = (bf16[4,160,256]{2,1,0:T(8,128)(2,1)S(1)}, bf16[4,160,256]{2,1,0:T(8,128)(2,1)S(1)}, u32[]{:S(2)}, u32[]{:S(2)}) collective-permute-start(bf16[4,160,256]{2,1,0:T(8,128)(2,1)S(1)} %get-tuple-element.62), channel_id=1, source_target_pairs={{0,8},{8,0},{16,24},{24,16},{32,40},{40,32},{48,56},{56,48},{64,72... | collective-permute-start | bytes 983048 | tf_op jit(solution)/shard_map/ppermute | solution.py:641
  47.7 15.9 %all-to-all-start.1 = ((bf16[8,272,128]{2,1,0:T(8,128)(2,1)}), bf16[8,272,128]{2,1,0:T(8,128)(2,1)S(1)}, u32[]{:S(2)}, u32[]{:S(2)}) async-start(bf16[8,272,128]{2,1,0:T(8,128)(2,1)} %get-tuple-element.53), calls=%async_computation.1 | async-start | bytes 1114112 | tf_op jit(solution)/shard_map/all_to_all | solution.py:651
  57.7 0.7 copy-start.4
  58.4 44.6 %copy-start = (bf16[1024,1024]{1,0:T(8,128)(2,1)S(1)}, bf16[1024,1024]{1,0:T(8,128)(2,1)}, u32[]{:S(2)}) copy-start(bf16[1024,1024]{1,0:T(8,128)(2,1)} %w_out_ref.1) | copy-start | bytes 6291460
  63.5 50.3 %copy-start.1 = (bf16[110,2048]{1,0:T(8,128)(2,1)S(1)}, bf16[110,2048]{1,0:T(8,128)(2,1)}, u32[]{:S(2)}) copy-start(bf16[110,2048]{1,0:T(8,128)(2,1)} %grid_ref.1) | copy-start | bytes 1351684
  63.5 50.3 %copy-start.2 = (s32[2048]{0:T(1024)S(1)}, s32[2048]{0:T(1024)}, u32[]{:S(2)}) copy-start(s32[2048]{0:T(1024)} %param.13) | copy-start | bytes 24580
  64.0 1.3 %collective-permute-start.6 = (f32[112,128]{1,0:T(8,128)S(1)}, f32[112,128]{1,0:T(8,128)S(1)}, u32[]{:S(2)}, u32[]{:S(2)}) collective-permute-start(f32[112,128]{1,0:T(8,128)S(1)} %get-tuple-element.55), channel_id=1, source_target_pairs={{0,8},{8,0},{16,24},{24,16},{32,40},{40,32},{48,56},{56,48},{64,72... | collective-permute-start | bytes 172040 | tf_op jit(solution)/shard_map/ppermute | solution.py:641
  65.4 5.5 %collective-permute-start.7 = (bf16[112,128]{1,0:T(8,128)(2,1)S(1)}, bf16[112,128]{1,0:T(8,128)(2,1)S(1)}, u32[]{:S(2)}, u32[]{:S(2)}) collective-permute-start(bf16[112,128]{1,0:T(8,128)(2,1)S(1)} %add_convert_fusion.3), channel_id=1, source_target_pairs={{0,16},{8,24},{16,0},{24,8},{32,48},{40,56},{48,32},{56,40},{64,80... | collective-permute-start | bytes 86024 | tf_op jit(solution)/shard_map/ppermute | solution.py:641
  70.8 4.0 %collective-permute-start.8 = (bf16[112,128]{1,0:T(8,128)(2,1)S(1)}, bf16[112,128]{1,0:T(8,128)(2,1)S(1)}, u32[]{:S(2)}, u32[]{:S(2)}) collective-permute-start(bf16[112,128]{1,0:T(8,128)(2,1)S(1)} %add_convert_fusion.2), channel_id=1, source_target_pairs={{0,32},{8,40},{16,48},{24,56},{32,0},{40,8},{48,16},{56,24},{64,96... | collective-permute-start | bytes 86024 | tf_op jit(solution)/shard_map/ppermute | solution.py:641
  74.8 5.7 %collective-permute-start.9 = (bf16[112,128]{1,0:T(8,128)(2,1)S(1)}, bf16[112,128]{1,0:T(8,128)(2,1)S(1)}, u32[]{:S(2)}, u32[]{:S(2)}) collective-permute-start(bf16[112,128]{1,0:T(8,128)(2,1)S(1)} %add_convert_fusion.1), channel_id=1, source_target_pairs={{0,64},{8,72},{16,80},{24,88},{32,96},{40,104},{48,112},{56,120},{... | collective-permute-start | bytes 86024 | tf_op jit(solution)/shard_map/ppermute | solution.py:641
  80.5 7.3 %collective-permute-start.10 = (bf16[112,128]{1,0:T(8,128)(2,1)S(1)}, bf16[112,128]{1,0:T(8,128)(2,1)S(1)}, u32[]{:S(2)}, u32[]{:S(2)}) collective-permute-start(bf16[112,128]{1,0:T(8,128)(2,1)S(1)} %add_convert_fusion.grad_ref), channel_id=1, source_target_pairs={{0,192},{8,200},{16,208},{24,216},{32,224},{40,232},{48,240},{56,2... | collective-permute-start | bytes 86024 | tf_op jit(solution)/shard_map/ppermute | solution.py:647
  103.6 4.8 %collective-permute-start.11 = (f32[112,1024]{1,0:T(8,128)S(1)}, f32[112,1024]{1,0:T(8,128)S(1)}, u32[]{:S(2)}, u32[]{:S(2)}) collective-permute-start(f32[112,1024]{1,0:T(8,128)S(1)} %gradient_half.1.mine_ref), channel_id=1, source_target_pairs={{0,8},{8,0},{16,24},{24,16},{32,40},{40,32},{48,56},{56,48},{64,72... | collective-permute-start | bytes 1376264 | tf_op jit(solution)/shard_map/ppermute | solution.py:641
  103.8 10.0 %collective-permute-start.13 = (bf16[176,128]{1,0:T(8,128)(2,1)S(1)}, bf16[176,128]{1,0:T(8,128)(2,1)S(1)}, u32[]{:S(2)}, u32[]{:S(2)}) collective-permute-start(bf16[176,128]{1,0:T(8,128)(2,1)S(1)} %get-tuple-element.60), channel_id=1, source_target_pairs={{0,2},{2,4},{3,1},{4,6},{5,3},{6,8},{7,5},{8,10},{9,7},{10,12},{11... | collective-permute-start | bytes 135176 | tf_op jit(solution)/shard_map/ppermute | solution.py:631
  106.3 4.1 %collective-permute-start.12 = (bf16[160,128]{1,0:T(8,128)(2,1)S(1)}, bf16[160,128]{1,0:T(8,128)(2,1)S(1)}, u32[]{:S(2)}, u32[]{:S(2)}) collective-permute-start(bf16[160,128]{1,0:T(8,128)(2,1)S(1)} %get-tuple-element.58.own_ref), channel_id=1, source_target_pairs={{0,1},{1,0},{2,3},{3,2},{4,5},{5,4},{6,7},{7,6},{8,9},{9,8},{10,11... | collective-permute-start | bytes 122888 | tf_op jit(solution)/shard_map/ppermute | solution.py:625

commit v7 on v6

--- a/solution.py
+++ b/solution.py
@@ -666,7 +666,7 @@
     mid_sum = to_partner(mid_sum)
     far_sum = two_over(far_sum, -1)
     packed, enc = project(own, mid_in, far_in, norm_gain[None], weights)
-    packed, mid_sum, far_sum = lax.optimization_barrier((packed, mid_sum, far_sum))
+    packed, mid_sum = lax.optimization_barrier((packed, mid_sum))
     qkv = swap(packed)
     send, node = side(enc, own_sum, mid_sum, far_sum, dec_pad)
     qkv, send, node = lax.optimization_barrier((qkv, send, node))

time: 116 us -> 115 us (level)
  waiting for transfers between devices: 28.2 us -> 26.7 us
    all_to_all x2, waiting for transfers between devices: 12.6 us -> 1.15 us  [swap(): lax.all_to_all(block, 'head', split_axis=0, concat_axis=0, tiled=True)]
    ppermute x3, waiting for transfers between devices: 3.41 us -> 10.2 us  [two_over(): lax.ppermute(block, BOTH, [(i, j) for i, j in pairs if 0 <= j < count])]
    ppermute x3, starting transfers between devices: 13.4 us -> 15.5 us  [two_over(): lax.ppermute(block, BOTH, [(i, j) for i, j in pairs if 0 <= j < count])]
    ppermute x1, starting transfers between devices: 5.48 us -> 3.35 us  [across(): lax.ppermute(block, 'band', [(i, other[i // 4] * 4 + i % 4) for i in rang...]
    ppermute x6, starting transfers between devices: 7.72 us -> 9.84 us  [flipped(): lax.ppermute(block, axis, [(i, i ^ 1 << bit) for i in range(lax.axis_size...]
    ppermute x6, waiting for transfers between devices: 9.12 us -> 11 us  [flipped(): lax.ppermute(block, axis, [(i, i ^ 1 << bit) for i in range(lax.axis_size...]
    all_to_all x2, starting transfers between devices: 9.48 us -> 8.2 us  [swap(): lax.all_to_all(block, 'head', split_axis=0, concat_axis=0, tiled=True)]
    ppermute x1, waiting for transfers between devices: 1.85 us -> 3.02 us  [across(): lax.ppermute(block, 'band', [(i, other[i // 4] * 4 + i % 4) for i in rang...]
  transfers between devices with their start and end apart: 16 -> 16, of which waited for: 8 -> 10; matrix products, arithmetic and copies ran while one was open for 0% -> 0% of each run, Pallas kernels for 16% -> 17%
where the time goes in v7:
time: 115 us; the launch traced here: 114 us
  starting transfers between devices  44.3 us (39%)
  Pallas kernels  27.1 us (24%)
  waiting for transfers between devices  26.7 us (23%)
  blocking collectives  14.6 us (13%)
    ppermute x3, starting transfers between devices, two_over(): lax.ppermute(block, BOTH, [(i, j) for i, j in pairs if 0 <= j < count])  15.5 us
    all_to_all x1, blocking collectives, swap(): lax.all_to_all(block, 'head', split_axis=0, concat_axis=0, tiled=True)  14.6 us
    ppermute x6, waiting for transfers between devices, flipped(): lax.ppermute(block, axis, [(i, i ^ 1 << bit) for i in range(lax.axis_size...  11 us
    ppermute x3, waiting for transfers between devices, two_over(): lax.ppermute(block, BOTH, [(i, j) for i, j in pairs if 0 <= j < count])  10.2 us
    ppermute x6, starting transfers between devices, flipped(): lax.ppermute(block, axis, [(i, i ^ 1 << bit) for i in range(lax.axis_size...  9.84 us
    all_to_all x2, starting transfers between devices, swap(): lax.all_to_all(block, 'head', split_axis=0, concat_axis=0, tiled=True)  8.2 us
    pallas_call x1, Pallas kernels, near(): pl.pallas_call(functools.partial(near_kernel, reach), in_specs=[VMEM, HBM...  6.25 us
    pallas_call x1, Pallas kernels, far(): pl.pallas_call(functools.partial(far_kernel, reach), in_specs=[HBM] * 6 +...  5.11 us
  transfers between devices with their start and end apart: 16, of which 10 were waited for; matrix products, arithmetic and copies ran while one was open for 0% of the time, Pallas kernels for 17%

profile of v7, /device:TPU:32, one launch (start us, length us, event | category | flops | bytes accessed | tf_op | source)
XLA Modules:
  0.0 114.4 jit_solution(14501934736184684948)
XLA Ops:
  0.6 4.9 %encode.1 = (bf16[160,1024]{1,0:T(8,128)(2,1)S(1)}, bf16[176,1024]{1,0:T(8,128)(2,1)S(1)}, f32[160,1024]{1,0:T(8,128)S(1)}) custom-call(bf16[110,2048]{1,0:T(8,128)(2,1)} %grid_ref.1, s32[1,2048]{1,0:T(1,128)} %bitcast.11, bf16[110,1024]{1,0:T(8,128)(2,1)} %w_hbm.2, f32[1,1024]{1,0:T(1,128)} %bitcast.12), custom_call_target="tpu_custom_call" | custom-call | tf_op jit(solution)/shard_map/encode/pallas_call | solution.py:98
  5.6 1.6 %collective-permute-start = (bf16[176,1024]{1,0:T(8,128)(2,1)S(1)}, bf16[176,1024]{1,0:T(8,128)(2,1)S(1)}, u32[]{:S(2)}, u32[]{:S(2)}) collective-permute-start(bf16[176,1024]{1,0:T(8,128)(2,1)S(1)} %get-tuple-element.32), channel_id=1, source_target_pairs={{0,1},{1,0},{2,3},{3,2},{4,5},{5,4},{6,7},{7,6},{8,9},{9,8},{10,11... | collective-permute-start | bytes 1081352 | tf_op jit(solution)/shard_map/ppermute | solution.py:625
  7.2 5.8 %collective-permute-start.1 = (bf16[160,1024]{1,0:T(8,128)(2,1)S(1)}, bf16[160,1024]{1,0:T(8,128)(2,1)S(1)}, u32[]{:S(2)}, u32[]{:S(2)}) collective-permute-start(bf16[160,1024]{1,0:T(8,128)(2,1)S(1)} %get-tuple-element.33.after_ref), channel_id=1, source_target_pairs={{1,3},{2,0},{3,5},{4,2},{5,7},{6,4},{7,9},{8,6},{9,11},{10,8},{11,... | collective-permute-start | bytes 983048 | tf_op jit(solution)/shard_map/ppermute | solution.py:631
  13.0 3.2 %prepare.1 = (bf16[1024,3072]{1,0:T(8,128)(2,1)S(1)}, bf16[128,1024]{1,0:T(8,128)(2,1)S(1)}, bf16[128,128]{1,0:T(8,128)(2,1)}, bf16[160,128]{1,0:T(8,128)(2,1)S(...) custom-call(bf16[1024,3072]{1,0:T(8,128)(2,1)} %w_hbm.3, bf16[1024,1024]{1,0:T(8,128)(2,1)} %w_out_ref.1, ...), custom_call_target="tpu_custom_call" | custom-call | flops 500000000 | bytes 6291456 | tf_op jit(solution)/shard_map/prepare/pallas_call | solution.py:158
  16.3 1.9 %collective-permute-done.1.far_ref = bf16[160,1024]{1,0:T(8,128)(2,1)S(1)} collective-permute-done((bf16[160,1024]{1,0:T(8,128)(2,1)S(1)}, bf16[160,1024]{1,0:T(8,128)(2,1)S(1)}, u32[]{:S(2)}, u32[]{:S(2)}) %collective-permute-start.1) | collective-permute-done | bytes 327712 | tf_op jit(solution)/shard_map/ppermute | solution.py:631
  18.2 2.2 %project.1 = (bf16[8,160,384]{2,1,0:T(8,128)(2,1)}, f32[160,1024]{1,0:T(8,128)S(1)}) custom-call(f32[160,1024]{1,0:T(8,128)S(1)} %get-tuple-element.31.own_ref, bf16[176,1024]{1,0:T(8,128)(2,1)S(1)} %collective-permute-done.mid_ref, bf16[160,1024]{1,0:T(8,128)(2,1)S(1)} %collective-permute-done.1.far_ref, f32[1,1024]{1,0:T(1,128)S(1)} %bitcast.8, ...), custom_call_target="tpu_custom_call" | custom-call | tf_op jit(solution)/shard_map/project/pallas_call | solution.py:213
  20.4 4.5 %all-to-all-start = ((bf16[8,160,384]{2,1,0:T(8,128)(2,1)}), bf16[8,160,384]{2,1,0:T(8,128)(2,1)S(1)}, u32[]{:S(2)}, u32[]{:S(2)}) async-start(bf16[8,160,384]{2,1,0:T(8,128)(2,1)} %get-tuple-element.37), calls=%async_computation | async-start | bytes 1966080 | tf_op jit(solution)/shard_map/all_to_all | solution.py:651
  24.9 7.3 %collective-permute-start.3 = (bf16[160,128]{1,0:T(8,128)(2,1)S(1)}, bf16[160,128]{1,0:T(8,128)(2,1)S(1)}, u32[]{:S(2)}, u32[]{:S(2)}) collective-permute-start(bf16[160,128]{1,0:T(8,128)(2,1)S(1)} %get-tuple-element.41), channel_id=1, source_target_pairs={{1,3},{2,0},{3,5},{4,2},{5,7},{6,4},{7,9},{8,6},{9,11},{10,8},{11,... | collective-permute-start | bytes 122888 | tf_op jit(solution)/shard_map/ppermute | solution.py:631
  32.2 4.9 %collective-permute-done.3.far_ref = bf16[160,128]{1,0:T(8,128)(2,1)S(1)} collective-permute-done((bf16[160,128]{1,0:T(8,128)(2,1)S(1)}, bf16[160,128]{1,0:T(8,128)(2,1)S(1)}, u32[]{:S(2)}, u32[]{:S(2)}) %collective-permute-start.3) | collective-permute-done | bytes 40992 | tf_op jit(solution)/shard_map/ppermute | solution.py:631
  37.1 1.2 %side.1 = (bf16[8,272,128]{2,1,0:T(8,128)(2,1)}, f32[160,128]{1,0:T(8,128)S(1)}) custom-call(f32[160,1024]{1,0:T(8,128)S(1)} %get-tuple-element.38.enc_ref, f32[160,128]{1,0:T(8,128)S(1)} %get-tuple-element.39.own_ref, bf16[160,128]{1,0:T(8,128)(2,1)S(1)} %collective-permute-done.2.mid_ref, bf16[160,128]{1,0:T(8,128)(2,1)S(1)} %collective-permute-done.3.far_ref, ...), custom_call_target="tpu_custom_call" | custom-call | tf_op jit(solution)/shard_map/side/pallas_call | solution.py:249
  38.3 1.1 %all-to-all-done.qkv_ref = bf16[8,160,384]{2,1,0:T(8,128)(2,1)S(1)} async-done(((bf16[8,160,384]{2,1,0:T(8,128)(2,1)}), bf16[8,160,384]{2,1,0:T(8,128)(2,1)S(1)}, u32[]{:S(2)}, u32[]{:S(2)}) %all-to-all-start) | async-done | bytes 983072 | tf_op jit(solution)/shard_map/all_to_all | solution.py:651
  39.6 3.7 %collective-permute-start.4 = (bf16[4,160,256]{2,1,0:T(8,128)(2,1)S(1)}, bf16[4,160,256]{2,1,0:T(8,128)(2,1)S(1)}, u32[]{:S(2)}, u32[]{:S(2)}) collective-permute-start(bf16[4,160,256]{2,1,0:T(8,128)(2,1)S(1)} %get-tuple-element.61), channel_id=1, source_target_pairs={{8,16},{16,8},{24,32},{32,24},{40,48},{48,40},{56,64},{64,56},{72,... | collective-permute-start | bytes 983048 | tf_op jit(solution)/shard_map/ppermute | solution.py:637
  43.3 3.5 %collective-permute-start.5 = (bf16[4,160,256]{2,1,0:T(8,128)(2,1)S(1)}, bf16[4,160,256]{2,1,0:T(8,128)(2,1)S(1)}, u32[]{:S(2)}, u32[]{:S(2)}) collective-permute-start(bf16[4,160,256]{2,1,0:T(8,128)(2,1)S(1)} %get-tuple-element.60), channel_id=1, source_target_pairs={{0,8},{8,0},{16,24},{24,16},{32,40},{40,32},{48,56},{56,48},{64,72... | collective-permute-start | bytes 983048 | tf_op jit(solution)/shard_map/ppermute | solution.py:641
  46.8 3.7 %all-to-all-start.1 = ((bf16[8,272,128]{2,1,0:T(8,128)(2,1)}), bf16[8,272,128]{2,1,0:T(8,128)(2,1)S(1)}, u32[]{:S(2)}, u32[]{:S(2)}) async-start(bf16[8,272,128]{2,1,0:T(8,128)(2,1)} %get-tuple-element.51), calls=%async_computation.1 | async-start | bytes 1114112 | tf_op jit(solution)/shard_map/all_to_all | solution.py:651
  50.6 6.2 %near.1 = (f32[5,2,80,256]{3,2,1,0:T(8,128)}, f32[5,1,512]{2,1,0:T(1,128)}, bf16[2,1280,128]{2,1,0:T(8,128)(2,1)}) custom-call(bf16[8,160,384]{2,1,0:T(8,128)(2,1)S(1)} %all-to-all-done.qkv_ref, s32[2,1280]{1,0:T(2,128)} %win_hbm.3), custom_call_target="tpu_custom_call" | custom-call | flops 6000000000 | bytes 4000000 | tf_op jit(solution)/shard_map/near/pallas_call | solution.py:345
  57.6 5.1 %far.1 = (bf16[8,272,128]{2,1,0:T(8,128)(2,1)}, bf16[128,1280]{1,0:T(8,128)(2,1)S(1)}) custom-call(bf16[2,1280,128]{2,1,0:T(8,128)(2,1)} %get-tuple-element.46.q_hbm, f32[5,2,80,256]{3,2,1,0:T(8,128)} %get-tuple-element.47.acc_hbm, f32[5,1,512]{2,1,0:T(1,128)} %get-tuple-element.48.top_hbm, s32[2,1280]{1,0:T(2,128)} %win_hbm.3, ...), custom_call_target="tpu_custom_call" | custom-call | flops 6000000000 | bytes 2000000 | tf_op jit(solution)/shard_map/far/pallas_call | solution.py:446
  63.3 1.2 %collective-permute-done.6 = f32[112,128]{1,0:T(8,128)S(1)} collective-permute-done((f32[112,128]{1,0:T(8,128)S(1)}, f32[112,128]{1,0:T(8,128)S(1)}, u32[]{:S(2)}, u32[]{:S(2)}) %collective-permute-start.6) | collective-permute-done | bytes 57376 | tf_op jit(solution)/shard_map/ppermute | solution.py:641
  64.5 1.4 %collective-permute-start.7 = (bf16[112,128]{1,0:T(8,128)(2,1)S(1)}, bf16[112,128]{1,0:T(8,128)(2,1)S(1)}, u32[]{:S(2)}, u32[]{:S(2)}) collective-permute-start(bf16[112,128]{1,0:T(8,128)(2,1)S(1)} %add_convert_fusion.3), channel_id=1, source_target_pairs={{0,16},{8,24},{16,0},{24,8},{32,48},{40,56},{48,32},{56,40},{64,80... | collective-permute-start | bytes 86024 | tf_op jit(solution)/shard_map/ppermute | solution.py:641
  65.9 4.1 %collective-permute-done.7 = bf16[112,128]{1,0:T(8,128)(2,1)S(1)} collective-permute-done((bf16[112,128]{1,0:T(8,128)(2,1)S(1)}, bf16[112,128]{1,0:T(8,128)(2,1)S(1)}, u32[]{:S(2)}, u32[]{:S(2)}) %collective-permute-start.7) | collective-permute-done | bytes 28704 | tf_op jit(solution)/shard_map/ppermute | solution.py:641
  70.1 3.9 %collective-permute-done.8 = bf16[112,128]{1,0:T(8,128)(2,1)S(1)} collective-permute-done((bf16[112,128]{1,0:T(8,128)(2,1)S(1)}, bf16[112,128]{1,0:T(8,128)(2,1)S(1)}, u32[]{:S(2)}, u32[]{:S(2)}) %collective-permute-start.8) | collective-permute-done | bytes 28704 | tf_op jit(solution)/shard_map/ppermute | solution.py:641
  74.0 4.6 %collective-permute-start.9 = (bf16[112,128]{1,0:T(8,128)(2,1)S(1)}, bf16[112,128]{1,0:T(8,128)(2,1)S(1)}, u32[]{:S(2)}, u32[]{:S(2)}) collective-permute-start(bf16[112,128]{1,0:T(8,128)(2,1)S(1)} %add_convert_fusion.1), channel_id=1, source_target_pairs={{0,64},{8,72},{16,80},{24,88},{32,96},{40,104},{48,112},{56,120},{... | collective-permute-start | bytes 86024 | tf_op jit(solution)/shard_map/ppermute | solution.py:641
  78.6 1.9 %collective-permute-done.9 = bf16[112,128]{1,0:T(8,128)(2,1)S(1)} collective-permute-done((bf16[112,128]{1,0:T(8,128)(2,1)S(1)}, bf16[112,128]{1,0:T(8,128)(2,1)S(1)}, u32[]{:S(2)}, u32[]{:S(2)}) %collective-permute-start.9) | collective-permute-done | bytes 28704 | tf_op jit(solution)/shard_map/ppermute | solution.py:641
  80.5 3.4 %collective-permute-start.10 = (bf16[112,128]{1,0:T(8,128)(2,1)S(1)}, bf16[112,128]{1,0:T(8,128)(2,1)S(1)}, u32[]{:S(2)}, u32[]{:S(2)}) collective-permute-start(bf16[112,128]{1,0:T(8,128)(2,1)S(1)} %add_convert_fusion.grad_ref), channel_id=1, source_target_pairs={{0,192},{8,200},{16,208},{24,216},{32,224},{40,232},{48,240},{56,2... | collective-permute-start | bytes 86024 | tf_op jit(solution)/shard_map/ppermute | solution.py:647
  83.8 3.0 %collective-permute-done.10.more_ref = bf16[112,128]{1,0:T(8,128)(2,1)S(1)} collective-permute-done((bf16[112,128]{1,0:T(8,128)(2,1)S(1)}, bf16[112,128]{1,0:T(8,128)(2,1)S(1)}, u32[]{:S(2)}, u32[]{:S(2)}) %collective-permute-start.10) | collective-permute-done | bytes 28704 | tf_op jit(solution)/shard_map/ppermute | solution.py:647
  86.9 0.8 spread.1
  87.7 14.6 %all_to_all.15.parts_ref = bf16[8,272,128]{2,1,0:T(8,128)(2,1)S(1)} all-to-all(bf16[8,272,128]{2,1,0:T(8,128)(2,1)} %spread.1), channel_id=1, replica_groups=mesh['band'=32,'head'=8] {'head'}, dimensions={0} | all-to-all | bytes 1114112 | tf_op jit(solution)/shard_map/all_to_all | solution.py:651
  103.0 2.5 %collective-permute-start.13 = (bf16[176,128]{1,0:T(8,128)(2,1)S(1)}, bf16[176,128]{1,0:T(8,128)(2,1)S(1)}, u32[]{:S(2)}, u32[]{:S(2)}) collective-permute-start(bf16[176,128]{1,0:T(8,128)(2,1)S(1)} %get-tuple-element.58), channel_id=1, source_target_pairs={{0,2},{2,4},{3,1},{4,6},{5,3},{6,8},{7,5},{8,10},{9,7},{10,12},{11... | collective-permute-start | bytes 135176 | tf_op jit(solution)/shard_map/ppermute | solution.py:631
  105.5 2.0 %collective-permute-start.12 = (bf16[160,128]{1,0:T(8,128)(2,1)S(1)}, bf16[160,128]{1,0:T(8,128)(2,1)S(1)}, u32[]{:S(2)}, u32[]{:S(2)}) collective-permute-start(bf16[160,128]{1,0:T(8,128)(2,1)S(1)} %get-tuple-element.56.own_ref), channel_id=1, source_target_pairs={{0,1},{1,0},{2,3},{3,2},{4,5},{5,4},{6,7},{7,6},{8,9},{9,8},{10,11... | collective-permute-start | bytes 122888 | tf_op jit(solution)/shard_map/ppermute | solution.py:625
  107.5 0.8 add.29
  108.4 1.2 %collective-permute-done.12.mid_ref = bf16[160,128]{1,0:T(8,128)(2,1)S(1)} collective-permute-done((bf16[160,128]{1,0:T(8,128)(2,1)S(1)}, bf16[160,128]{1,0:T(8,128)(2,1)S(1)}, u32[]{:S(2)}, u32[]{:S(2)}) %collective-permute-start.12) | collective-permute-done | bytes 40992 | tf_op jit(solution)/shard_map/ppermute | solution.py:625
  109.6 3.4 %collective-permute-done.13.far_ref = bf16[176,128]{1,0:T(8,128)(2,1)S(1)} collective-permute-done((bf16[176,128]{1,0:T(8,128)(2,1)S(1)}, bf16[176,128]{1,0:T(8,128)(2,1)S(1)}, u32[]{:S(2)}, u32[]{:S(2)}) %collective-permute-start.13) | collective-permute-done | bytes 45088 | tf_op jit(solution)/shard_map/ppermute | solution.py:631
  113.0 1.4 %decode.1 = bf16[110,2048]{1,0:T(8,128)(2,1)} custom-call(bf16[160,128]{1,0:T(8,128)(2,1)S(1)} %collective-permute-done.12.mid_ref, bf16[176,128]{1,0:T(8,128)(2,1)S(1)} %collective-permute-done.13.far_ref, bf16[160,128]{1,0:T(8,128)(2,1)S(1)} %get-tuple-element.56.own_ref, s32[1,2048]{1,0:T(1,128)S(1)} %bitcast.7, bf16[110,2048]{1,0:T(8,128)(2,1)S(1)} %copy-done.1), custom_call_target="tpu_custom_call" | custom-call | tf_op jit(solution)/shard_map/decode/pallas_call | solution.py:542
  (29 shorter events, 2.4 us)
Async XLA Ops:
  0.6 17.6 %copy-start.3 = (f32[1024]{0:T(1024)S(1)}, f32[1024]{0:T(1024)}, u32[]{:S(2)}) copy-start(f32[1024]{0:T(1024)} %param.19) | copy-start | bytes 12292
  5.6 12.6 %collective-permute-start = (bf16[176,1024]{1,0:T(8,128)(2,1)S(1)}, bf16[176,1024]{1,0:T(8,128)(2,1)S(1)}, u32[]{:S(2)}, u32[]{:S(2)}) collective-permute-start(bf16[176,1024]{1,0:T(8,128)(2,1)S(1)} %get-tuple-element.32), channel_id=1, source_target_pairs={{0,1},{1,0},{2,3},{3,2},{4,5},{5,4},{6,7},{7,6},{8,9},{9,8},{10,11... | collective-permute-start | bytes 1081352 | tf_op jit(solution)/shard_map/ppermute | solution.py:625
  7.2 11.1 %collective-permute-start.1 = (bf16[160,1024]{1,0:T(8,128)(2,1)S(1)}, bf16[160,1024]{1,0:T(8,128)(2,1)S(1)}, u32[]{:S(2)}, u32[]{:S(2)}) collective-permute-start(bf16[160,1024]{1,0:T(8,128)(2,1)S(1)} %get-tuple-element.33.after_ref), channel_id=1, source_target_pairs={{1,3},{2,0},{3,5},{4,2},{5,7},{6,4},{7,9},{8,6},{9,11},{10,8},{11,... | collective-permute-start | bytes 983048 | tf_op jit(solution)/shard_map/ppermute | solution.py:631
  16.2 4.2 %collective-permute-start.2 = (bf16[160,128]{1,0:T(8,128)(2,1)S(1)}, bf16[160,128]{1,0:T(8,128)(2,1)S(1)}, u32[]{:S(2)}, u32[]{:S(2)}) collective-permute-start(bf16[160,128]{1,0:T(8,128)(2,1)S(1)} %get-tuple-element.36), channel_id=1, source_target_pairs={{0,1},{1,0},{2,3},{3,2},{4,5},{5,4},{6,7},{7,6},{8,9},{9,8},{10,11... | collective-permute-start | bytes 122888 | tf_op jit(solution)/shard_map/ppermute | solution.py:625
  20.4 19.0 %all-to-all-start = ((bf16[8,160,384]{2,1,0:T(8,128)(2,1)}), bf16[8,160,384]{2,1,0:T(8,128)(2,1)S(1)}, u32[]{:S(2)}, u32[]{:S(2)}) async-start(bf16[8,160,384]{2,1,0:T(8,128)(2,1)} %get-tuple-element.37), calls=%async_computation | async-start | bytes 1966080 | tf_op jit(solution)/shard_map/all_to_all | solution.py:651
  24.9 12.1 %collective-permute-start.3 = (bf16[160,128]{1,0:T(8,128)(2,1)S(1)}, bf16[160,128]{1,0:T(8,128)(2,1)S(1)}, u32[]{:S(2)}, u32[]{:S(2)}) collective-permute-start(bf16[160,128]{1,0:T(8,128)(2,1)S(1)} %get-tuple-element.41), channel_id=1, source_target_pairs={{1,3},{2,0},{3,5},{4,2},{5,7},{6,4},{7,9},{8,6},{9,11},{10,8},{11,... | collective-permute-start | bytes 122888 | tf_op jit(solution)/shard_map/ppermute | solution.py:631
  39.6 17.3 %collective-permute-start.4 = (bf16[4,160,256]{2,1,0:T(8,128)(2,1)S(1)}, bf16[4,160,256]{2,1,0:T(8,128)(2,1)S(1)}, u32[]{:S(2)}, u32[]{:S(2)}) collective-permute-start(bf16[4,160,256]{2,1,0:T(8,128)(2,1)S(1)} %get-tuple-element.61), channel_id=1, source_target_pairs={{8,16},{16,8},{24,32},{32,24},{40,48},{48,40},{56,64},{64,56},{72,... | collective-permute-start | bytes 983048 | tf_op jit(solution)/shard_map/ppermute | solution.py:637
  43.3 13.5 %collective-permute-start.5 = (bf16[4,160,256]{2,1,0:T(8,128)(2,1)S(1)}, bf16[4,160,256]{2,1,0:T(8,128)(2,1)S(1)}, u32[]{:S(2)}, u32[]{:S(2)}) collective-permute-start(bf16[4,160,256]{2,1,0:T(8,128)(2,1)S(1)} %get-tuple-element.60), channel_id=1, source_target_pairs={{0,8},{8,0},{16,24},{24,16},{32,40},{40,32},{48,56},{56,48},{64,72... | collective-permute-start | bytes 983048 | tf_op jit(solution)/shard_map/ppermute | solution.py:641
  46.8 15.9 %all-to-all-start.1 = ((bf16[8,272,128]{2,1,0:T(8,128)(2,1)}), bf16[8,272,128]{2,1,0:T(8,128)(2,1)S(1)}, u32[]{:S(2)}, u32[]{:S(2)}) async-start(bf16[8,272,128]{2,1,0:T(8,128)(2,1)} %get-tuple-element.51), calls=%async_computation.1 | async-start | bytes 1114112 | tf_op jit(solution)/shard_map/all_to_all | solution.py:651
  56.8 0.7 copy-start.4
  57.6 44.7 %copy-start = (bf16[1024,1024]{1,0:T(8,128)(2,1)S(1)}, bf16[1024,1024]{1,0:T(8,128)(2,1)}, u32[]{:S(2)}) copy-start(bf16[1024,1024]{1,0:T(8,128)(2,1)} %w_out_ref.1) | copy-start | bytes 6291460
  62.7 50.3 %copy-start.1 = (bf16[110,2048]{1,0:T(8,128)(2,1)S(1)}, bf16[110,2048]{1,0:T(8,128)(2,1)}, u32[]{:S(2)}) copy-start(bf16[110,2048]{1,0:T(8,128)(2,1)} %grid_ref.1) | copy-start | bytes 1351684
  62.7 50.3 %copy-start.2 = (s32[2048]{0:T(1024)S(1)}, s32[2048]{0:T(1024)}, u32[]{:S(2)}) copy-start(s32[2048]{0:T(1024)} %param.13) | copy-start | bytes 24580
  63.2 1.3 %collective-permute-start.6 = (f32[112,128]{1,0:T(8,128)S(1)}, f32[112,128]{1,0:T(8,128)S(1)}, u32[]{:S(2)}, u32[]{:S(2)}) collective-permute-start(f32[112,128]{1,0:T(8,128)S(1)} %get-tuple-element.53), channel_id=1, source_target_pairs={{0,8},{8,0},{16,24},{24,16},{32,40},{40,32},{48,56},{56,48},{64,72... | collective-permute-start | bytes 172040 | tf_op jit(solution)/shard_map/ppermute | solution.py:641
  64.5 5.5 %collective-permute-start.7 = (bf16[112,128]{1,0:T(8,128)(2,1)S(1)}, bf16[112,128]{1,0:T(8,128)(2,1)S(1)}, u32[]{:S(2)}, u32[]{:S(2)}) collective-permute-start(bf16[112,128]{1,0:T(8,128)(2,1)S(1)} %add_convert_fusion.3), channel_id=1, source_target_pairs={{0,16},{8,24},{16,0},{24,8},{32,48},{40,56},{48,32},{56,40},{64,80... | collective-permute-start | bytes 86024 | tf_op jit(solution)/shard_map/ppermute | solution.py:641
  70.0 4.0 %collective-permute-start.8 = (bf16[112,128]{1,0:T(8,128)(2,1)S(1)}, bf16[112,128]{1,0:T(8,128)(2,1)S(1)}, u32[]{:S(2)}, u32[]{:S(2)}) collective-permute-start(bf16[112,128]{1,0:T(8,128)(2,1)S(1)} %add_convert_fusion.2), channel_id=1, source_target_pairs={{0,32},{8,40},{16,48},{24,56},{32,0},{40,8},{48,16},{56,24},{64,96... | collective-permute-start | bytes 86024 | tf_op jit(solution)/shard_map/ppermute | solution.py:641
  74.0 6.5 %collective-permute-start.9 = (bf16[112,128]{1,0:T(8,128)(2,1)S(1)}, bf16[112,128]{1,0:T(8,128)(2,1)S(1)}, u32[]{:S(2)}, u32[]{:S(2)}) collective-permute-start(bf16[112,128]{1,0:T(8,128)(2,1)S(1)} %add_convert_fusion.1), channel_id=1, source_target_pairs={{0,64},{8,72},{16,80},{24,88},{32,96},{40,104},{48,112},{56,120},{... | collective-permute-start | bytes 86024 | tf_op jit(solution)/shard_map/ppermute | solution.py:641
  80.5 6.4 %collective-permute-start.10 = (bf16[112,128]{1,0:T(8,128)(2,1)S(1)}, bf16[112,128]{1,0:T(8,128)(2,1)S(1)}, u32[]{:S(2)}, u32[]{:S(2)}) collective-permute-start(bf16[112,128]{1,0:T(8,128)(2,1)S(1)} %add_convert_fusion.grad_ref), channel_id=1, source_target_pairs={{0,192},{8,200},{16,208},{24,216},{32,224},{40,232},{48,240},{56,2... | collective-permute-start | bytes 86024 | tf_op jit(solution)/shard_map/ppermute | solution.py:647
  102.9 4.7 %collective-permute-start.11 = (f32[112,1024]{1,0:T(8,128)S(1)}, f32[112,1024]{1,0:T(8,128)S(1)}, u32[]{:S(2)}, u32[]{:S(2)}) collective-permute-start(f32[112,1024]{1,0:T(8,128)S(1)} %gradient_half.1.mine_ref), channel_id=1, source_target_pairs={{0,8},{8,0},{16,24},{24,16},{32,40},{40,32},{48,56},{56,48},{64,72... | collective-permute-start | bytes 1376264 | tf_op jit(solution)/shard_map/ppermute | solution.py:641
  103.0 10.0 %collective-permute-start.13 = (bf16[176,128]{1,0:T(8,128)(2,1)S(1)}, bf16[176,128]{1,0:T(8,128)(2,1)S(1)}, u32[]{:S(2)}, u32[]{:S(2)}) collective-permute-start(bf16[176,128]{1,0:T(8,128)(2,1)S(1)} %get-tuple-element.58), channel_id=1, source_target_pairs={{0,2},{2,4},{3,1},{4,6},{5,3},{6,8},{7,5},{8,10},{9,7},{10,12},{11... | collective-permute-start | bytes 135176 | tf_op jit(solution)/shard_map/ppermute | solution.py:631
  105.5 4.1 %collective-permute-start.12 = (bf16[160,128]{1,0:T(8,128)(2,1)S(1)}, bf16[160,128]{1,0:T(8,128)(2,1)S(1)}, u32[]{:S(2)}, u32[]{:S(2)}) collective-permute-start(bf16[160,128]{1,0:T(8,128)(2,1)S(1)} %get-tuple-element.56.own_ref), channel_id=1, source_target_pairs={{0,1},{1,0},{2,3},{3,2},{4,5},{5,4},{6,7},{7,6},{8,9},{9,8},{10,11... | collective-permute-start | bytes 122888 | tf_op jit(solution)/shard_map/ppermute | solution.py:625

commit v8 on v7

--- a/solution.py
+++ b/solution.py
@@ -492,26 +492,6 @@
     )(out, extra)
 
 
-def table_kernel(parts_ref, node_ref, table_ref, padded_ref):
-    total = node_ref[...]
-    for group in range(parts_ref.shape[0]):
-        total += parts_ref[group, :NODE_DEV, :].astype(F32)
-    table_ref[...] = total.astype(BF)
-    padded_ref[:NODE_DEV, :] = total.astype(BF)
-    padded_ref[NODE_DEV:, :] = jnp.zeros((EXTRA, LANES), BF)
-
-
-def make_table(parts, node):
-    return pl.pallas_call(
-        table_kernel,
-        in_specs=[VMEM] * 2,
-        out_specs=(VMEM,) * 2,
-        out_shape=(shape(node.shape, BF), shape((NODE_DEV + EXTRA, LANES), BF)),
-        compiler_params=params(),
-        name="make_table",
-    )(parts, node)
-
-
 def decode_kernel(mid_ref, far_ref, own_ref, dec_ref, grid_ref, pred_ref):
     channels, points = grid_ref.shape
     nodes = NODE_DEV
@@ -572,9 +552,15 @@
     )(grad, more, *pinned(parts))
 
 
-def half_kernel(parts_ref, w_out_ref, half_ref):
+def finish_kernel(parts_ref, node_ref, w_out_ref, table_ref, padded_ref, half_ref):
+    groups = parts_ref.shape[0]
+    total = node_ref[...]
+    for group in range(groups):
+        total += parts_ref[group, :NODE_DEV, :].astype(F32)
+    table_ref[...] = total.astype(BF)
+    padded_ref[:NODE_DEV, :] = total.astype(BF)
+    padded_ref[NODE_DEV:, :] = jnp.zeros((EXTRA, LANES), BF)
     first = lax.rem(lax.axis_index("band"), 2) == 0
-    groups = parts_ref.shape[0]
 
     @pl.when(first)
     def _():
@@ -590,15 +576,19 @@
             half_ref[:, group * LANES : (group + 1) * LANES] = parts_ref[group, NODE_DEV:, :].astype(F32)
 
 
-def gradient_half(parts, w_out):
-    return pl.pallas_call(
-        half_kernel,
-        in_specs=[VMEM] * 2,
-        out_specs=VMEM,
-        out_shape=shape((ROWS, w_out.shape[1]), F32),
-        compiler_params=params(),
-        name="gradient_half",
-    )(parts, w_out)
+def finish(parts, node, w_out):
+    return pl.pallas_call(
+        finish_kernel,
+        in_specs=[VMEM] * 3,
+        out_specs=(VMEM,) * 3,
+        out_shape=(
+            shape(node.shape, BF),
+            shape((NODE_DEV + EXTRA, LANES), BF),
+            shape((ROWS, w_out.shape[1]), F32),
+        ),
+        compiler_params=params(),
+        name="finish",
+    )(parts, node, w_out)
 
 
 def add_kernel(mine_ref, other_ref, out_ref):
@@ -684,8 +674,7 @@
     for bit in (1, 2, 3):
         grad = (grad.astype(F32) + flipped(grad, "band", bit).astype(F32)).astype(BF)
     parts = swap(spread(grad, across(grad), parts))
-    table, padded = make_table(parts, node)
-    half_grad = gradient_half(parts, w_out)
+    table, padded, half_grad = finish(parts, node, w_out)
     grad_dec = add(half_grad, flipped(half_grad, "band", 0), channels)
     grad_dec, mid_rows = lax.optimization_barrier((grad_dec, to_partner(table)))
     prediction = decode(two_over(padded, 1), mid_rows, table, dec_row, grid_in)

time: 115 us -> 115 us (level)
  transfers between devices with their start and end apart: 16 -> 16, of which waited for: 10 -> 10; matrix products, arithmetic and copies ran while one was open for 0% -> 0% of each run, Pallas kernels for 17% -> 16%
where the time goes in v8:
time: 115 us; the launch traced here: 114 us
  starting transfers between devices  44.3 us (39%)
  Pallas kernels  27.1 us (24%)
  waiting for transfers between devices  26.7 us (23%)
  blocking collectives  14.6 us (13%)
    ppermute x3, starting transfers between devices, two_over(): lax.ppermute(block, BOTH, [(i, j) for i, j in pairs if 0 <= j < count])  15.5 us
    all_to_all x1, blocking collectives, swap(): lax.all_to_all(block, 'head', split_axis=0, concat_axis=0, tiled=True)  14.6 us
    ppermute x6, waiting for transfers between devices, flipped(): lax.ppermute(block, axis, [(i, i ^ 1 << bit) for i in range(lax.axis_size...  11 us
    ppermute x3, waiting for transfers between devices, two_over(): lax.ppermute(block, BOTH, [(i, j) for i, j in pairs if 0 <= j < count])  10.2 us
    ppermute x6, starting transfers between devices, flipped(): lax.ppermute(block, axis, [(i, i ^ 1 << bit) for i in range(lax.axis_size...  9.84 us
    all_to_all x2, starting transfers between devices, swap(): lax.all_to_all(block, 'head', split_axis=0, concat_axis=0, tiled=True)  8.2 us
    pallas_call x1, Pallas kernels, near(): pl.pallas_call(functools.partial(near_kernel, reach), in_specs=[VMEM, HBM...  6.25 us
    pallas_call x1, Pallas kernels, far(): pl.pallas_call(functools.partial(far_kernel, reach), in_specs=[HBM] * 6 +...  5.11 us
  transfers between devices with their start and end apart: 16, of which 10 were waited for; matrix products, arithmetic and copies ran while one was open for 0% of the time, Pallas kernels for 16%

profile of v8, /device:TPU:32, one launch (start us, length us, event | category | flops | bytes accessed | tf_op | source)
XLA Modules:
  0.0 114.4 jit_solution(344443389128134072)
XLA Ops:
  0.6 4.9 %encode.1 = (bf16[160,1024]{1,0:T(8,128)(2,1)S(1)}, bf16[176,1024]{1,0:T(8,128)(2,1)S(1)}, f32[160,1024]{1,0:T(8,128)S(1)}) custom-call(bf16[110,2048]{1,0:T(8,128)(2,1)} %grid_ref.1, s32[1,2048]{1,0:T(1,128)} %bitcast.11, bf16[110,1024]{1,0:T(8,128)(2,1)} %w_hbm.2, f32[1,1024]{1,0:T(1,128)} %bitcast.12), custom_call_target="tpu_custom_call" | custom-call | tf_op jit(solution)/shard_map/encode/pallas_call | solution.py:98
  5.6 1.6 %collective-permute-start = (bf16[176,1024]{1,0:T(8,128)(2,1)S(1)}, bf16[176,1024]{1,0:T(8,128)(2,1)S(1)}, u32[]{:S(2)}, u32[]{:S(2)}) collective-permute-start(bf16[176,1024]{1,0:T(8,128)(2,1)S(1)} %get-tuple-element.33), channel_id=1, source_target_pairs={{0,1},{1,0},{2,3},{3,2},{4,5},{5,4},{6,7},{7,6},{8,9},{9,8},{10,11... | collective-permute-start | bytes 1081352 | tf_op jit(solution)/shard_map/ppermute | solution.py:615
  7.2 5.8 %collective-permute-start.1 = (bf16[160,1024]{1,0:T(8,128)(2,1)S(1)}, bf16[160,1024]{1,0:T(8,128)(2,1)S(1)}, u32[]{:S(2)}, u32[]{:S(2)}) collective-permute-start(bf16[160,1024]{1,0:T(8,128)(2,1)S(1)} %get-tuple-element.34.after_ref), channel_id=1, source_target_pairs={{1,3},{2,0},{3,5},{4,2},{5,7},{6,4},{7,9},{8,6},{9,11},{10,8},{11,... | collective-permute-start | bytes 983048 | tf_op jit(solution)/shard_map/ppermute | solution.py:621
  13.0 3.2 %prepare.1 = (bf16[1024,3072]{1,0:T(8,128)(2,1)S(1)}, bf16[128,1024]{1,0:T(8,128)(2,1)S(1)}, bf16[128,128]{1,0:T(8,128)(2,1)}, bf16[160,128]{1,0:T(8,128)(2,1)S(...) custom-call(bf16[1024,3072]{1,0:T(8,128)(2,1)} %w_hbm.3, bf16[1024,1024]{1,0:T(8,128)(2,1)} %w_out_ref.1, ...), custom_call_target="tpu_custom_call" | custom-call | flops 500000000 | bytes 6291456 | tf_op jit(solution)/shard_map/prepare/pallas_call | solution.py:158
  16.3 1.9 %collective-permute-done.1.far_ref = bf16[160,1024]{1,0:T(8,128)(2,1)S(1)} collective-permute-done((bf16[160,1024]{1,0:T(8,128)(2,1)S(1)}, bf16[160,1024]{1,0:T(8,128)(2,1)S(1)}, u32[]{:S(2)}, u32[]{:S(2)}) %collective-permute-start.1) | collective-permute-done | bytes 327712 | tf_op jit(solution)/shard_map/ppermute | solution.py:621
  18.2 2.2 %project.1 = (bf16[8,160,384]{2,1,0:T(8,128)(2,1)}, f32[160,1024]{1,0:T(8,128)S(1)}) custom-call(f32[160,1024]{1,0:T(8,128)S(1)} %get-tuple-element.32.own_ref, bf16[176,1024]{1,0:T(8,128)(2,1)S(1)} %collective-permute-done.mid_ref, bf16[160,1024]{1,0:T(8,128)(2,1)S(1)} %collective-permute-done.1.far_ref, f32[1,1024]{1,0:T(1,128)S(1)} %bitcast.8, ...), custom_call_target="tpu_custom_call" | custom-call | tf_op jit(solution)/shard_map/project/pallas_call | solution.py:213
  20.4 4.5 %all-to-all-start = ((bf16[8,160,384]{2,1,0:T(8,128)(2,1)}), bf16[8,160,384]{2,1,0:T(8,128)(2,1)S(1)}, u32[]{:S(2)}, u32[]{:S(2)}) async-start(bf16[8,160,384]{2,1,0:T(8,128)(2,1)} %get-tuple-element.38), calls=%async_computation | async-start | bytes 1966080 | tf_op jit(solution)/shard_map/all_to_all | solution.py:641
  24.9 7.3 %collective-permute-start.3 = (bf16[160,128]{1,0:T(8,128)(2,1)S(1)}, bf16[160,128]{1,0:T(8,128)(2,1)S(1)}, u32[]{:S(2)}, u32[]{:S(2)}) collective-permute-start(bf16[160,128]{1,0:T(8,128)(2,1)S(1)} %get-tuple-element.42), channel_id=1, source_target_pairs={{1,3},{2,0},{3,5},{4,2},{5,7},{6,4},{7,9},{8,6},{9,11},{10,8},{11,... | collective-permute-start | bytes 122888 | tf_op jit(solution)/shard_map/ppermute | solution.py:621
  32.2 4.9 %collective-permute-done.3.far_ref = bf16[160,128]{1,0:T(8,128)(2,1)S(1)} collective-permute-done((bf16[160,128]{1,0:T(8,128)(2,1)S(1)}, bf16[160,128]{1,0:T(8,128)(2,1)S(1)}, u32[]{:S(2)}, u32[]{:S(2)}) %collective-permute-start.3) | collective-permute-done | bytes 40992 | tf_op jit(solution)/shard_map/ppermute | solution.py:621
  37.1 1.2 %side.1 = (bf16[8,272,128]{2,1,0:T(8,128)(2,1)}, f32[160,128]{1,0:T(8,128)S(1)}) custom-call(f32[160,1024]{1,0:T(8,128)S(1)} %get-tuple-element.39.enc_ref, f32[160,128]{1,0:T(8,128)S(1)} %get-tuple-element.40.own_ref, bf16[160,128]{1,0:T(8,128)(2,1)S(1)} %collective-permute-done.2.mid_ref, bf16[160,128]{1,0:T(8,128)(2,1)S(1)} %collective-permute-done.3.far_ref, ...), custom_call_target="tpu_custom_call" | custom-call | tf_op jit(solution)/shard_map/side/pallas_call | solution.py:249
  38.3 1.1 %all-to-all-done.qkv_ref = bf16[8,160,384]{2,1,0:T(8,128)(2,1)S(1)} async-done(((bf16[8,160,384]{2,1,0:T(8,128)(2,1)}), bf16[8,160,384]{2,1,0:T(8,128)(2,1)S(1)}, u32[]{:S(2)}, u32[]{:S(2)}) %all-to-all-start) | async-done | bytes 983072 | tf_op jit(solution)/shard_map/all_to_all | solution.py:641
  39.6 3.7 %collective-permute-start.4 = (bf16[4,160,256]{2,1,0:T(8,128)(2,1)S(1)}, bf16[4,160,256]{2,1,0:T(8,128)(2,1)S(1)}, u32[]{:S(2)}, u32[]{:S(2)}) collective-permute-start(bf16[4,160,256]{2,1,0:T(8,128)(2,1)S(1)} %get-tuple-element.63), channel_id=1, source_target_pairs={{8,16},{16,8},{24,32},{32,24},{40,48},{48,40},{56,64},{64,56},{72,... | collective-permute-start | bytes 983048 | tf_op jit(solution)/shard_map/ppermute | solution.py:627
  43.3 3.5 %collective-permute-start.5 = (bf16[4,160,256]{2,1,0:T(8,128)(2,1)S(1)}, bf16[4,160,256]{2,1,0:T(8,128)(2,1)S(1)}, u32[]{:S(2)}, u32[]{:S(2)}) collective-permute-start(bf16[4,160,256]{2,1,0:T(8,128)(2,1)S(1)} %get-tuple-element.62), channel_id=1, source_target_pairs={{0,8},{8,0},{16,24},{24,16},{32,40},{40,32},{48,56},{56,48},{64,72... | collective-permute-start | bytes 983048 | tf_op jit(solution)/shard_map/ppermute | solution.py:631
  46.8 3.7 %all-to-all-start.1 = ((bf16[8,272,128]{2,1,0:T(8,128)(2,1)}), bf16[8,272,128]{2,1,0:T(8,128)(2,1)S(1)}, u32[]{:S(2)}, u32[]{:S(2)}) async-start(bf16[8,272,128]{2,1,0:T(8,128)(2,1)} %get-tuple-element.52), calls=%async_computation.1 | async-start | bytes 1114112 | tf_op jit(solution)/shard_map/all_to_all | solution.py:641
  50.6 6.2 %near.1 = (f32[5,2,80,256]{3,2,1,0:T(8,128)}, f32[5,1,512]{2,1,0:T(1,128)}, bf16[2,1280,128]{2,1,0:T(8,128)(2,1)}) custom-call(bf16[8,160,384]{2,1,0:T(8,128)(2,1)S(1)} %all-to-all-done.qkv_ref, s32[2,1280]{1,0:T(2,128)} %win_hbm.3), custom_call_target="tpu_custom_call" | custom-call | flops 6000000000 | bytes 4000000 | tf_op jit(solution)/shard_map/near/pallas_call | solution.py:345
  57.6 5.1 %far.1 = (bf16[8,272,128]{2,1,0:T(8,128)(2,1)}, bf16[128,1280]{1,0:T(8,128)(2,1)S(1)}) custom-call(bf16[2,1280,128]{2,1,0:T(8,128)(2,1)} %get-tuple-element.47.q_hbm, f32[5,2,80,256]{3,2,1,0:T(8,128)} %get-tuple-element.48.acc_hbm, f32[5,1,512]{2,1,0:T(1,128)} %get-tuple-element.49.top_hbm, s32[2,1280]{1,0:T(2,128)} %win_hbm.3, ...), custom_call_target="tpu_custom_call" | custom-call | flops 6000000000 | bytes 2000000 | tf_op jit(solution)/shard_map/far/pallas_call | solution.py:446
  63.3 1.2 %collective-permute-done.6 = f32[112,128]{1,0:T(8,128)S(1)} collective-permute-done((f32[112,128]{1,0:T(8,128)S(1)}, f32[112,128]{1,0:T(8,128)S(1)}, u32[]{:S(2)}, u32[]{:S(2)}) %collective-permute-start.6) | collective-permute-done | bytes 57376 | tf_op jit(solution)/shard_map/ppermute | solution.py:631
  64.5 1.4 %collective-permute-start.7 = (bf16[112,128]{1,0:T(8,128)(2,1)S(1)}, bf16[112,128]{1,0:T(8,128)(2,1)S(1)}, u32[]{:S(2)}, u32[]{:S(2)}) collective-permute-start(bf16[112,128]{1,0:T(8,128)(2,1)S(1)} %add_convert_fusion.3), channel_id=1, source_target_pairs={{0,16},{8,24},{16,0},{24,8},{32,48},{40,56},{48,32},{56,40},{64,80... | collective-permute-start | bytes 86024 | tf_op jit(solution)/shard_map/ppermute | solution.py:631
  65.9 4.1 %collective-permute-done.7 = bf16[112,128]{1,0:T(8,128)(2,1)S(1)} collective-permute-done((bf16[112,128]{1,0:T(8,128)(2,1)S(1)}, bf16[112,128]{1,0:T(8,128)(2,1)S(1)}, u32[]{:S(2)}, u32[]{:S(2)}) %collective-permute-start.7) | collective-permute-done | bytes 28704 | tf_op jit(solution)/shard_map/ppermute | solution.py:631
  70.1 3.9 %collective-permute-done.8 = bf16[112,128]{1,0:T(8,128)(2,1)S(1)} collective-permute-done((bf16[112,128]{1,0:T(8,128)(2,1)S(1)}, bf16[112,128]{1,0:T(8,128)(2,1)S(1)}, u32[]{:S(2)}, u32[]{:S(2)}) %collective-permute-start.8) | collective-permute-done | bytes 28704 | tf_op jit(solution)/shard_map/ppermute | solution.py:631
  74.0 4.6 %collective-permute-start.9 = (bf16[112,128]{1,0:T(8,128)(2,1)S(1)}, bf16[112,128]{1,0:T(8,128)(2,1)S(1)}, u32[]{:S(2)}, u32[]{:S(2)}) collective-permute-start(bf16[112,128]{1,0:T(8,128)(2,1)S(1)} %add_convert_fusion.1), channel_id=1, source_target_pairs={{0,64},{8,72},{16,80},{24,88},{32,96},{40,104},{48,112},{56,120},{... | collective-permute-start | bytes 86024 | tf_op jit(solution)/shard_map/ppermute | solution.py:631
  78.6 1.9 %collective-permute-done.9 = bf16[112,128]{1,0:T(8,128)(2,1)S(1)} collective-permute-done((bf16[112,128]{1,0:T(8,128)(2,1)S(1)}, bf16[112,128]{1,0:T(8,128)(2,1)S(1)}, u32[]{:S(2)}, u32[]{:S(2)}) %collective-permute-start.9) | collective-permute-done | bytes 28704 | tf_op jit(solution)/shard_map/ppermute | solution.py:631
  80.5 3.4 %collective-permute-start.10 = (bf16[112,128]{1,0:T(8,128)(2,1)S(1)}, bf16[112,128]{1,0:T(8,128)(2,1)S(1)}, u32[]{:S(2)}, u32[]{:S(2)}) collective-permute-start(bf16[112,128]{1,0:T(8,128)(2,1)S(1)} %add_convert_fusion.grad_ref), channel_id=1, source_target_pairs={{0,192},{8,200},{16,208},{24,216},{32,224},{40,232},{48,240},{56,2... | collective-permute-start | bytes 86024 | tf_op jit(solution)/shard_map/ppermute | solution.py:637
  83.8 3.0 %collective-permute-done.10.more_ref = bf16[112,128]{1,0:T(8,128)(2,1)S(1)} collective-permute-done((bf16[112,128]{1,0:T(8,128)(2,1)S(1)}, bf16[112,128]{1,0:T(8,128)(2,1)S(1)}, u32[]{:S(2)}, u32[]{:S(2)}) %collective-permute-start.10) | collective-permute-done | bytes 28704 | tf_op jit(solution)/shard_map/ppermute | solution.py:637
  86.9 0.8 spread.1
  87.7 14.6 %all_to_all.15.parts_ref = bf16[8,272,128]{2,1,0:T(8,128)(2,1)S(1)} all-to-all(bf16[8,272,128]{2,1,0:T(8,128)(2,1)} %spread.1), channel_id=1, replica_groups=mesh['band'=32,'head'=8] {'head'}, dimensions={0} | all-to-all | bytes 1114112 | tf_op jit(solution)/shard_map/all_to_all | solution.py:641
  103.0 2.5 %collective-permute-start.13 = (bf16[176,128]{1,0:T(8,128)(2,1)S(1)}, bf16[176,128]{1,0:T(8,128)(2,1)S(1)}, u32[]{:S(2)}, u32[]{:S(2)}) collective-permute-start(bf16[176,128]{1,0:T(8,128)(2,1)S(1)} %get-tuple-element.60), channel_id=1, source_target_pairs={{0,2},{2,4},{3,1},{4,6},{5,3},{6,8},{7,5},{8,10},{9,7},{10,12},{11... | collective-permute-start | bytes 135176 | tf_op jit(solution)/shard_map/ppermute | solution.py:621
  105.5 2.0 %collective-permute-start.12 = (bf16[160,128]{1,0:T(8,128)(2,1)S(1)}, bf16[160,128]{1,0:T(8,128)(2,1)S(1)}, u32[]{:S(2)}, u32[]{:S(2)}) collective-permute-start(bf16[160,128]{1,0:T(8,128)(2,1)S(1)} %get-tuple-element.58.own_ref), channel_id=1, source_target_pairs={{0,1},{1,0},{2,3},{3,2},{4,5},{5,4},{6,7},{7,6},{8,9},{9,8},{10,11... | collective-permute-start | bytes 122888 | tf_op jit(solution)/shard_map/ppermute | solution.py:615
  107.5 0.8 add.29
  108.3 1.3 %collective-permute-done.12.mid_ref = bf16[160,128]{1,0:T(8,128)(2,1)S(1)} collective-permute-done((bf16[160,128]{1,0:T(8,128)(2,1)S(1)}, bf16[160,128]{1,0:T(8,128)(2,1)S(1)}, u32[]{:S(2)}, u32[]{:S(2)}) %collective-permute-start.12) | collective-permute-done | bytes 40992 | tf_op jit(solution)/shard_map/ppermute | solution.py:615
  109.6 3.4 %collective-permute-done.13.far_ref = bf16[176,128]{1,0:T(8,128)(2,1)S(1)} collective-permute-done((bf16[176,128]{1,0:T(8,128)(2,1)S(1)}, bf16[176,128]{1,0:T(8,128)(2,1)S(1)}, u32[]{:S(2)}, u32[]{:S(2)}) %collective-permute-start.13) | collective-permute-done | bytes 45088 | tf_op jit(solution)/shard_map/ppermute | solution.py:621
  113.0 1.4 %decode.1 = bf16[110,2048]{1,0:T(8,128)(2,1)} custom-call(bf16[160,128]{1,0:T(8,128)(2,1)S(1)} %collective-permute-done.12.mid_ref, bf16[176,128]{1,0:T(8,128)(2,1)S(1)} %collective-permute-done.13.far_ref, bf16[160,128]{1,0:T(8,128)(2,1)S(1)} %get-tuple-element.58.own_ref, s32[1,2048]{1,0:T(1,128)S(1)} %bitcast.7, bf16[110,2048]{1,0:T(8,128)(2,1)S(1)} %copy-done.1), custom_call_target="tpu_custom_call" | custom-call | tf_op jit(solution)/shard_map/decode/pallas_call | solution.py:522
  (28 shorter events, 2.4 us)
Async XLA Ops:
  0.6 17.6 %copy-start.3 = (f32[1024]{0:T(1024)S(1)}, f32[1024]{0:T(1024)}, u32[]{:S(2)}) copy-start(f32[1024]{0:T(1024)} %param.19) | copy-start | bytes 12292
  5.6 12.6 %collective-permute-start = (bf16[176,1024]{1,0:T(8,128)(2,1)S(1)}, bf16[176,1024]{1,0:T(8,128)(2,1)S(1)}, u32[]{:S(2)}, u32[]{:S(2)}) collective-permute-start(bf16[176,1024]{1,0:T(8,128)(2,1)S(1)} %get-tuple-element.33), channel_id=1, source_target_pairs={{0,1},{1,0},{2,3},{3,2},{4,5},{5,4},{6,7},{7,6},{8,9},{9,8},{10,11... | collective-permute-start | bytes 1081352 | tf_op jit(solution)/shard_map/ppermute | solution.py:615
  7.2 11.1 %collective-permute-start.1 = (bf16[160,1024]{1,0:T(8,128)(2,1)S(1)}, bf16[160,1024]{1,0:T(8,128)(2,1)S(1)}, u32[]{:S(2)}, u32[]{:S(2)}) collective-permute-start(bf16[160,1024]{1,0:T(8,128)(2,1)S(1)} %get-tuple-element.34.after_ref), channel_id=1, source_target_pairs={{1,3},{2,0},{3,5},{4,2},{5,7},{6,4},{7,9},{8,6},{9,11},{10,8},{11,... | collective-permute-start | bytes 983048 | tf_op jit(solution)/shard_map/ppermute | solution.py:621
  16.2 4.2 %collective-permute-start.2 = (bf16[160,128]{1,0:T(8,128)(2,1)S(1)}, bf16[160,128]{1,0:T(8,128)(2,1)S(1)}, u32[]{:S(2)}, u32[]{:S(2)}) collective-permute-start(bf16[160,128]{1,0:T(8,128)(2,1)S(1)} %get-tuple-element.37), channel_id=1, source_target_pairs={{0,1},{1,0},{2,3},{3,2},{4,5},{5,4},{6,7},{7,6},{8,9},{9,8},{10,11... | collective-permute-start | bytes 122888 | tf_op jit(solution)/shard_map/ppermute | solution.py:615
  20.4 19.0 %all-to-all-start = ((bf16[8,160,384]{2,1,0:T(8,128)(2,1)}), bf16[8,160,384]{2,1,0:T(8,128)(2,1)S(1)}, u32[]{:S(2)}, u32[]{:S(2)}) async-start(bf16[8,160,384]{2,1,0:T(8,128)(2,1)} %get-tuple-element.38), calls=%async_computation | async-start | bytes 1966080 | tf_op jit(solution)/shard_map/all_to_all | solution.py:641
  24.9 12.1 %collective-permute-start.3 = (bf16[160,128]{1,0:T(8,128)(2,1)S(1)}, bf16[160,128]{1,0:T(8,128)(2,1)S(1)}, u32[]{:S(2)}, u32[]{:S(2)}) collective-permute-start(bf16[160,128]{1,0:T(8,128)(2,1)S(1)} %get-tuple-element.42), channel_id=1, source_target_pairs={{1,3},{2,0},{3,5},{4,2},{5,7},{6,4},{7,9},{8,6},{9,11},{10,8},{11,... | collective-permute-start | bytes 122888 | tf_op jit(solution)/shard_map/ppermute | solution.py:621
  39.6 17.3 %collective-permute-start.4 = (bf16[4,160,256]{2,1,0:T(8,128)(2,1)S(1)}, bf16[4,160,256]{2,1,0:T(8,128)(2,1)S(1)}, u32[]{:S(2)}, u32[]{:S(2)}) collective-permute-start(bf16[4,160,256]{2,1,0:T(8,128)(2,1)S(1)} %get-tuple-element.63), channel_id=1, source_target_pairs={{8,16},{16,8},{24,32},{32,24},{40,48},{48,40},{56,64},{64,56},{72,... | collective-permute-start | bytes 983048 | tf_op jit(solution)/shard_map/ppermute | solution.py:627
  43.3 13.5 %collective-permute-start.5 = (bf16[4,160,256]{2,1,0:T(8,128)(2,1)S(1)}, bf16[4,160,256]{2,1,0:T(8,128)(2,1)S(1)}, u32[]{:S(2)}, u32[]{:S(2)}) collective-permute-start(bf16[4,160,256]{2,1,0:T(8,128)(2,1)S(1)} %get-tuple-element.62), channel_id=1, source_target_pairs={{0,8},{8,0},{16,24},{24,16},{32,40},{40,32},{48,56},{56,48},{64,72... | collective-permute-start | bytes 983048 | tf_op jit(solution)/shard_map/ppermute | solution.py:631
  46.8 15.9 %all-to-all-start.1 = ((bf16[8,272,128]{2,1,0:T(8,128)(2,1)}), bf16[8,272,128]{2,1,0:T(8,128)(2,1)S(1)}, u32[]{:S(2)}, u32[]{:S(2)}) async-start(bf16[8,272,128]{2,1,0:T(8,128)(2,1)} %get-tuple-element.52), calls=%async_computation.1 | async-start | bytes 1114112 | tf_op jit(solution)/shard_map/all_to_all | solution.py:641
  56.8 0.7 copy-start.4
  57.6 44.7 %copy-start = (bf16[1024,1024]{1,0:T(8,128)(2,1)S(1)}, bf16[1024,1024]{1,0:T(8,128)(2,1)}, u32[]{:S(2)}) copy-start(bf16[1024,1024]{1,0:T(8,128)(2,1)} %w_out_ref.1) | copy-start | bytes 6291460
  62.7 50.3 %copy-start.1 = (bf16[110,2048]{1,0:T(8,128)(2,1)S(1)}, bf16[110,2048]{1,0:T(8,128)(2,1)}, u32[]{:S(2)}) copy-start(bf16[110,2048]{1,0:T(8,128)(2,1)} %grid_ref.1) | copy-start | bytes 1351684
  62.7 50.3 %copy-start.2 = (s32[2048]{0:T(1024)S(1)}, s32[2048]{0:T(1024)}, u32[]{:S(2)}) copy-start(s32[2048]{0:T(1024)} %param.13) | copy-start | bytes 24580
  63.2 1.3 %collective-permute-start.6 = (f32[112,128]{1,0:T(8,128)S(1)}, f32[112,128]{1,0:T(8,128)S(1)}, u32[]{:S(2)}, u32[]{:S(2)}) collective-permute-start(f32[112,128]{1,0:T(8,128)S(1)} %get-tuple-element.54), channel_id=1, source_target_pairs={{0,8},{8,0},{16,24},{24,16},{32,40},{40,32},{48,56},{56,48},{64,72... | collective-permute-start | bytes 172040 | tf_op jit(solution)/shard_map/ppermute | solution.py:631
  64.5 5.5 %collective-permute-start.7 = (bf16[112,128]{1,0:T(8,128)(2,1)S(1)}, bf16[112,128]{1,0:T(8,128)(2,1)S(1)}, u32[]{:S(2)}, u32[]{:S(2)}) collective-permute-start(bf16[112,128]{1,0:T(8,128)(2,1)S(1)} %add_convert_fusion.3), channel_id=1, source_target_pairs={{0,16},{8,24},{16,0},{24,8},{32,48},{40,56},{48,32},{56,40},{64,80... | collective-permute-start | bytes 86024 | tf_op jit(solution)/shard_map/ppermute | solution.py:631
  70.0 4.0 %collective-permute-start.8 = (bf16[112,128]{1,0:T(8,128)(2,1)S(1)}, bf16[112,128]{1,0:T(8,128)(2,1)S(1)}, u32[]{:S(2)}, u32[]{:S(2)}) collective-permute-start(bf16[112,128]{1,0:T(8,128)(2,1)S(1)} %add_convert_fusion.2), channel_id=1, source_target_pairs={{0,32},{8,40},{16,48},{24,56},{32,0},{40,8},{48,16},{56,24},{64,96... | collective-permute-start | bytes 86024 | tf_op jit(solution)/shard_map/ppermute | solution.py:631
  74.0 6.5 %collective-permute-start.9 = (bf16[112,128]{1,0:T(8,128)(2,1)S(1)}, bf16[112,128]{1,0:T(8,128)(2,1)S(1)}, u32[]{:S(2)}, u32[]{:S(2)}) collective-permute-start(bf16[112,128]{1,0:T(8,128)(2,1)S(1)} %add_convert_fusion.1), channel_id=1, source_target_pairs={{0,64},{8,72},{16,80},{24,88},{32,96},{40,104},{48,112},{56,120},{... | collective-permute-start | bytes 86024 | tf_op jit(solution)/shard_map/ppermute | solution.py:631
  80.5 6.4 %collective-permute-start.10 = (bf16[112,128]{1,0:T(8,128)(2,1)S(1)}, bf16[112,128]{1,0:T(8,128)(2,1)S(1)}, u32[]{:S(2)}, u32[]{:S(2)}) collective-permute-start(bf16[112,128]{1,0:T(8,128)(2,1)S(1)} %add_convert_fusion.grad_ref), channel_id=1, source_target_pairs={{0,192},{8,200},{16,208},{24,216},{32,224},{40,232},{48,240},{56,2... | collective-permute-start | bytes 86024 | tf_op jit(solution)/shard_map/ppermute | solution.py:637
  102.9 4.6 %collective-permute-start.11 = (f32[112,1024]{1,0:T(8,128)S(1)}, f32[112,1024]{1,0:T(8,128)S(1)}, u32[]{:S(2)}, u32[]{:S(2)}) collective-permute-start(f32[112,1024]{1,0:T(8,128)S(1)} %get-tuple-element.57.mine_ref), channel_id=1, source_target_pairs={{0,8},{8,0},{16,24},{24,16},{32,40},{40,32},{48,56},{56,48},{64,72... | collective-permute-start | bytes 1376264 | tf_op jit(solution)/shard_map/ppermute | solution.py:631
  103.0 10.0 %collective-permute-start.13 = (bf16[176,128]{1,0:T(8,128)(2,1)S(1)}, bf16[176,128]{1,0:T(8,128)(2,1)S(1)}, u32[]{:S(2)}, u32[]{:S(2)}) collective-permute-start(bf16[176,128]{1,0:T(8,128)(2,1)S(1)} %get-tuple-element.60), channel_id=1, source_target_pairs={{0,2},{2,4},{3,1},{4,6},{5,3},{6,8},{7,5},{8,10},{9,7},{10,12},{11... | collective-permute-start | bytes 135176 | tf_op jit(solution)/shard_map/ppermute | solution.py:621
  105.5 4.1 %collective-permute-start.12 = (bf16[160,128]{1,0:T(8,128)(2,1)S(1)}, bf16[160,128]{1,0:T(8,128)(2,1)S(1)}, u32[]{:S(2)}, u32[]{:S(2)}) collective-permute-start(bf16[160,128]{1,0:T(8,128)(2,1)S(1)} %get-tuple-element.58.own_ref), channel_id=1, source_target_pairs={{0,1},{1,0},{2,3},{3,2},{4,5},{5,4},{6,7},{7,6},{8,9},{9,8},{10,11... | collective-permute-start | bytes 122888 | tf_op jit(solution)/shard_map/ppermute | solution.py:615
